TPU v7x, 256 devices: a whole 4x4x8 slice. The times are simulated.
256 devices in a mesh: row: 32 (over z, y), col: 4 (over x_hi, core), depth: 2 (over x_lo).
Axes of the slice: x: 4 (x_hi: 2, x_lo: 2; x = x_hi * 2 + x_lo), y: 4, z: 8, core: 2. Of those that a mesh axis runs over, the one named last changes fastest.
Arguments:
- src_emb: bfloat16 [2, 512, 32768], P('depth', 'col', 'row'), may hold values from -6 to 6
- tgt_emb: bfloat16 [2, 512, 8192], P('depth', 'row', 'col'), may hold values from -6 to 6
- tile_mask: int32 [64, 16], P('row', 'col'), may hold values from 0 to 1, as said below
- src_mass: float32 [32768], P(('row', 'depth')), may hold values from 0.5 to 2
- tgt_mass: float32 [8192], P('col'), may hold values from 0.5 to 2
Outputs:
- log_src: float32 [32768], P(('row', 'depth'))
- log_tgt: float32 [8192], P('col')
Inputs may be any that keep to these rules, and one draw needn't show every extreme that they name: `tile_mask`: every tile row and every tile column of the mask holds at least one 1.
All inputs are finite; a program needn't handle non-finite values.
Results may differ from a plain program's by a relative error of at most 0.0003.
Values may be sent and summed in bfloat16 or wider, within the bound.
No kernel may reach another device: no remote copies, remote signals or barrier semaphores. Data moves between devices by JAX's collectives and lax.ppermute only.
A program may use at most 64 MiB of HBM per device.

v0:
```python
import math

import jax
import jax.numpy as jnp
from jax import lax
from jax.sharding import PartitionSpec as P

VECTOR_DIMENSION = 1024
TILE = 512
ITERS = 3


smoothing_strength = 0.64


def affinity_between_blocks(first_operand_block, right_part):
    return lax.dot_general(
        first_operand_block,
        right_part,
        (((0, 1), (0, 1)), ((), ())),
        preferred_element_type=jnp.float32,
    )


def shards(src_emb, tgt_emb, tile_mask, src_mass, tgt_mass):
    tile_size = TILE
    sharpness_factor = 1.0 / (smoothing_strength * math.sqrt(VECTOR_DIMENSION))
    row_count = src_mass.shape[0]
    depth_index = lax.axis_index("depth")
    demand_slice = lax.all_gather(tgt_emb, "row", axis=1, tiled=True)
    supply_slice = lax.all_gather(src_emb, "col", axis=1, tiled=True)
    scores = lax.psum_scatter(
        affinity_between_blocks(supply_slice, demand_slice) * sharpness_factor,
        "depth",
        scatter_dimension=0,
        tiled=True,
    )
    my_mask = lax.dynamic_slice_in_dim(
        tile_mask, depth_index * (row_count // tile_size), row_count // tile_size, 0
    )
    row_tiles = row_count // tile_size
    column_tile_count = scores.shape[1] // tile_size
    shaped = jnp.exp(scores).reshape(row_tiles, tile_size, column_tile_count, tile_size)
    kernel = jnp.where(my_mask[:, None, :, None] > 0, shaped, jnp.float32(0.0)).reshape(
        row_count, scores.shape[1]
    )
    tgt_scale = jnp.ones((kernel.shape[1],), jnp.float32)
    src_scale = jnp.ones((row_count,), jnp.float32)
    for sweep_index in range(ITERS):
        row_part = jnp.dot(kernel, tgt_scale, precision=lax.Precision.HIGHEST)
        src_scale = src_mass / lax.psum(row_part, "col")
        col_part = jnp.dot(src_scale, kernel, precision=lax.Precision.HIGHEST)
        tgt_scale = tgt_mass / lax.psum(col_part, ("row", "depth"))
    return (jnp.log(src_scale), jnp.log(tgt_scale))


def solution(mesh):
    placed = (
        P("depth", "col", "row"),
        P("depth", "row", "col"),
        P("row", "col"),
        P(("row", "depth")),
        P("col"),
    )
    return jax.shard_map(
        shards,
        mesh=mesh,
        in_specs=placed,
        out_specs=(P(("row", "depth")), P("col")),
        check_vma=False,
    )
```

profile of v0, /device:TPU:6, one launch (start us, length us, event | category | flops | bytes accessed | tf_op | source)
XLA Modules:
  0.0 758.3 jit_solution(4654843690161913635)
XLA Ops:
  7.2 0.0 all-gather.3.cloned.1.call-start
  7.2 0.7 all-gather.3.cloned.1.call-update
  7.9 0.0 all-gather.5.cloned.1.call-start
  7.9 0.7 all-gather.5.cloned.1.call-update
  8.6 0.0 reduce-scatter.2.cloned.1.call-start
  8.7 25.8 %all-gather.3.cloned.1.call-done = bf16[1,512,1024]{2,1,0:T(8,128)(2,1)} async-done(((bf16[1,128,1024]{2,1,0:T(8,128)(2,1)}), bf16[1,512,1024]{2,1,0:T(8,128)(2,1)}) %all-gather.3.cloned.1.call-update) | async-done | bytes 1048592 | tf_op jit(solution)/shard_map/all_gather | solution.py:31
  34.5 81.6 %all-gather.5.cloned.1.call-done = bf16[1,512,2048]{2,1,0:T(8,128)(2,1)} async-done(((bf16[1,16,2048]{2,1,0:T(8,128)(2,1)}), bf16[1,512,2048]{2,1,0:T(8,128)(2,1)}) %all-gather.5.cloned.1.call-update) | async-done | bytes 2097168 | tf_op jit(solution)/shard_map/all_gather | solution.py:30
  116.1 7.5 convolution_multiply_fusion
  123.6 0.0 copy-start.2
  123.6 0.0 reduce-scatter.2.cloned.1.call-update
  123.6 0.0 copy-start.1
  123.7 0.6 copy-done.2
  124.3 0.1 broadcast_bitcast_fusion
  124.4 100.3 %reduce-scatter.2.cloned.1.call-done = f32[512,2048]{1,0:T(8,128)} async-done(((f32[1024,2048]{1,0:T(8,128)}), f32[512,2048]{1,0:T(8,128)}) %reduce-scatter.2.cloned.1.call-update) | async-done | bytes 4194320 | tf_op jit(solution)/shard_map/reduce_scatter | solution.py:32
  224.7 0.0 copy-start
  224.7 6.3 fusion.6
  231.0 7.2 psum.42
  238.2 0.0 copy-done.1
  238.2 4.7 fusion.5
  242.9 157.0 %psum.43 = f32[2048]{0:T(1024)S(1)} all-reduce(f32[2048]{0:T(1024)S(1)} %bitcast.36), channel_id=1, replica_groups=mesh['row'=32,'col'=4,'depth'=2] {'row','depth'}, use_global_device_ids=true, to_apply=%region_2.3 | all-reduce | flops 2048 | bytes 16384 | tf_op jit(solution)/shard_map/psum | solution.py:53
  399.9 0.0 copy-done
  399.9 6.3 fusion.4
  406.2 7.2 psum.44
  413.4 4.7 fusion.3
  418.1 160.0 %psum.45 = f32[2048]{0:T(1024)S(1)} all-reduce(f32[2048]{0:T(1024)S(1)} %bitcast.37), channel_id=1, replica_groups=mesh['row'=32,'col'=4,'depth'=2] {'row','depth'}, use_global_device_ids=true, to_apply=%region_4.5 | all-reduce | flops 2048 | bytes 16384 | tf_op jit(solution)/shard_map/psum | solution.py:53
  578.1 6.3 fusion.2
  584.4 7.2 psum.46
  591.6 0.6 fusion.16
  592.2 4.7 fusion.1
  596.8 154.3 %psum.47 = f32[2048]{0:T(1024)S(1)} all-reduce(f32[2048]{0:T(1024)S(1)} %bitcast.35), channel_id=1, replica_groups=mesh['row'=32,'col'=4,'depth'=2] {'row','depth'}, use_global_device_ids=true, to_apply=%region_6.7 | all-reduce | flops 2048 | bytes 16384 | tf_op jit(solution)/shard_map/psum | solution.py:53
  751.2 0.6 divide_log_fusion
  (6 shorter events, 0.0 us)
Async XLA Ops:
  7.2 27.4 %all-gather.3.cloned.1.call-start = ((), (), s32[]{:S(2)}) async-start(), calls=%async_computation.1 | async-start | bytes 1310720 | tf_op jit(solution)/shard_map/all_gather | solution.py:31
  7.9 108.2 %all-gather.5.cloned.1.call-start = ((), (), s32[]{:S(2)}) async-start(), calls=%async_computation.2 | async-start | bytes 2162688 | tf_op jit(solution)/shard_map/all_gather | solution.py:30
  8.6 216.0 %reduce-scatter.2.cloned.1.call-start = ((), (), s32[]{:S(2)}) async-start(), calls=%async_computation.3 | async-start | bytes 12582912 | tf_op jit(solution)/shard_map/reduce_scatter | solution.py:32
  123.6 0.7 copy-start.2
  123.6 114.5 %copy-start.1 = (f32[512]{0:T(512)S(1)}, f32[512]{0:T(512)}, u32[]{:S(2)}) copy-start(f32[512]{0:T(512)} %param.8) | copy-start | bytes 6148
  224.7 175.2 %copy-start = (f32[2048]{0:T(1024)S(1)}, f32[2048]{0:T(1024)}, u32[]{:S(2)}) copy-start(f32[2048]{0:T(1024)} %param.9) | copy-start | bytes 24580
Sparse Core Ops, SparseCore 0:
  9.8 24.6 all-gather.2
  37.1 78.9 all-gather.4
  123.8 100.8 reduce-scatter.1
where the time goes:
time: 760 us; the launch traced here: 758 us
  blocking collectives  493 us (65%)
  waiting for transfers between devices  209 us (28%)
  matrix products  40.5 us (5%)
  between operations  13.8 us (2%)
    psum x3, blocking collectives, shards(): tgt_scale = tgt_mass / lax.psum(col_part, ('row', 'depth'))  471 us
    reduce_scatter x1, waiting for transfers between devices, shards(): lax.psum_scatter(affinity_between_blocks(supply_slice, demand_slice) * sh...  100 us
    all_gather x1, waiting for transfers between devices, shards(): demand_slice = lax.all_gather(tgt_emb, 'row', axis=1, tiled=True)  81.6 us
    all_gather x1, waiting for transfers between devices, shards(): supply_slice = lax.all_gather(src_emb, 'col', axis=1, tiled=True)  25.8 us
    psum x3, blocking collectives, shards(): src_scale = src_mass / lax.psum(row_part, 'col')  21.5 us
    dot_general x3, matrix products, shards(): row_part = jnp.dot(kernel, tgt_scale, precision=lax.Precision.HIGHEST)  19 us
  transfers between devices with their start and end apart: 3, of which 3 were waited for; matrix products, arithmetic and copies ran while one was open for 0% of the time, Pallas kernels for 0%

commit v1 on v0

v1 whole, which is shorter than its diff:
```python
import math

import jax
import jax.numpy as jnp
from jax import lax
from jax.experimental import pallas as pl
from jax.experimental.pallas import tpu as pltpu
from jax.sharding import Mesh
from jax.sharding import PartitionSpec as P

VECTOR_DIMENSION = 1024
TILE = 512
ITERS = 3
SHARPNESS = 1.0 / (0.64 * math.sqrt(VECTOR_DIMENSION))

X = ("xh", "xl")
PLANE = ("z", "y")
N_Z, N_Y, N_X = 8, 4, 4
ROWS = 1024
COLS = 1024
LANES = 128
CHUNKS = ROWS // LANES
GROUP = 16
F32 = jnp.float32
VMEM = pl.BlockSpec(memory_space=pltpu.VMEM)
SMEM = pl.BlockSpec(memory_space=pltpu.SMEM)


def shift(value, axis, size, by):
    return lax.ppermute(value, axis, [(i, (i + by) % size) for i in range(size)])


def lane_sums(folded):
    parts = [
        jnp.sum(folded[i * LANES : (i + 1) * LANES, :].T, axis=0, keepdims=True)
        for i in range(folded.shape[0] // LANES)
    ]
    return jnp.concatenate(parts, axis=0)


def build_body(where_ref, mask_ref, src_a_ref, src_b_ref, *refs):
    block_refs, (kernel_ref, sums_ref, tgt_ref, folded_ref) = refs[:-4], refs[-4:]
    z, y, c, xl = where_ref[0], where_ref[1], where_ref[2], where_ref[3]
    steps = (0, -1, 1, -2, 2, -3, 3, 4, 4)
    turns = (0, -1, 1, 2)
    for index, (block, step) in enumerate(zip(block_refs, steps, strict=True)):
        places = range(4) if index < 7 else (range(2) if index == 7 else range(2, 4))
        for row, place in enumerate(places):
            at = lax.rem(z + step + N_Z, N_Z) * N_Y + lax.rem(y + turns[place] + N_Y, N_Y)
            high, core, rest = lax.div(at, 16), lax.rem(lax.div(at, 8), 2), lax.rem(at, 8)
            side = jnp.where(core == c, 0, 1)
            for group in range(2):
                low = xl if group == 0 else 1 - xl
                to = side * 512 + (high * 2 + low) * 128 + rest * GROUP
                start = (row * 2 + group) * GROUP
                tgt_ref[pl.ds(pl.multiple_of(to, GROUP), GROUP), :] = block[start : start + GROUP, :]
    contract = (((0,), (0,)), ((), ()))
    for i in range(ROWS // TILE):
        rows = slice(i * TILE, (i + 1) * TILE)
        folded_ref[rows, :] = jnp.zeros((TILE, LANES), F32)
        for j in range(COLS // TILE):
            cols = slice(j * TILE, (j + 1) * TILE)
            live = mask_ref[i, j] > 0

            @pl.when(live)
            def _():
                scores = lax.dot_general(
                    src_a_ref[:, rows], tgt_ref[:512, cols], contract, preferred_element_type=F32
                ) + lax.dot_general(
                    src_b_ref[:, rows], tgt_ref[512:, cols], contract, preferred_element_type=F32
                )
                part = jnp.exp(scores * SHARPNESS)
                kernel_ref[rows, cols] = part
                total = part[:, :LANES]
                for k in range(1, TILE // LANES):
                    total = total + part[:, k * LANES : (k + 1) * LANES]
                folded_ref[rows, :] += total

            @pl.when(jnp.logical_not(live))
            def _():
                kernel_ref[rows, cols] = jnp.zeros((TILE, TILE), F32)

    sums_ref[...] = lane_sums(folded_ref[...])


def columns_body(kernel_ref, mass_ref, *refs):
    part_refs, (scale_ref, out_ref) = refs[:-2], refs[-2:]
    total = part_refs[0][...]
    for part in part_refs[1:]:
        total = total + part[...]
    scale = mass_ref[...] / total
    scale_ref[...] = scale
    acc = [None] * (COLS // LANES)
    for i in range(CHUNKS):
        wide = jnp.broadcast_to(scale[i : i + 1, :], (LANES, LANES)).T
        for j in range(COLS // LANES):
            prod = kernel_ref[i * LANES : (i + 1) * LANES, j * LANES : (j + 1) * LANES] * wide
            prod = jnp.sum(prod.reshape(LANES // 8, 8, LANES), axis=0)
            acc[j] = prod if acc[j] is None else acc[j] + prod
    sums = jnp.concatenate([jnp.sum(a, axis=0, keepdims=True) for a in acc], axis=0)
    out_ref[...] = jnp.broadcast_to(sums[None], out_ref.shape)


def rows_body(kernel_ref, mass_ref, parts_ref, sums_ref, folded_ref):
    scale = mass_ref[...] / jnp.sum(parts_ref[...], axis=0)
    for i in range(CHUNKS):
        rows = slice(i * LANES, (i + 1) * LANES)
        total = kernel_ref[rows, :LANES] * scale[0:1, :]
        for j in range(1, COLS // LANES):
            total = total + kernel_ref[rows, j * LANES : (j + 1) * LANES] * scale[j : j + 1, :]
        folded_ref[rows, :] = total
    sums_ref[...] = lane_sums(folded_ref[...])


SMALL = jax.ShapeDtypeStruct((CHUNKS, LANES), F32)
WIDE = jax.ShapeDtypeStruct((N_Z * N_Y, CHUNKS, LANES), F32)
KERNEL = jax.ShapeDtypeStruct((ROWS, COLS), F32)
PARAMS = pltpu.CompilerParams(vmem_limit_bytes=40 * 1024 * 1024)


def row_total(sums):
    chip = sums + shift(sums, "c", 2, 1)
    return (
        chip,
        shift(chip, X, N_X, 2),
        shift(chip, X, N_X, 1),
        shift(chip, X, N_X, -1),
    )


def shards(src_emb, tgt_emb, tile_mask, src_mass, tgt_mass):
    z, y, c, xl = (lax.axis_index(a) for a in ("z", "y", "c", "xl"))
    src_a = lax.all_gather(src_emb[0], X, axis=0, tiled=True)
    src_b = shift(src_a, "c", 2, 1)
    tgt = tgt_emb[0]
    kept = lax.dynamic_slice_in_dim(tgt, xl * COLS, COLS, 1)
    sent = lax.dynamic_slice_in_dim(tgt, (1 - xl) * COLS, COLS, 1)
    pair = jnp.concatenate([kept, shift(sent, "xl", 2, 1)], axis=0)
    plane = jnp.concatenate(
        [pair, shift(pair, "y", N_Y, 1), shift(pair, "y", N_Y, -1), shift(pair, "y", N_Y, 2)], axis=0
    )
    blocks = [plane]
    up = down = plane
    for _ in range(3):
        up, down = shift(up, "z", N_Z, 1), shift(down, "z", N_Z, -1)
        blocks += [up, down]
    half = plane.shape[0] // 2
    blocks += [shift(up[:half], "z", N_Z, 1), shift(down[half:], "z", N_Z, -1)]

    other = shift(src_mass, "xl", 2, 1)
    src_rows = jnp.where(
        xl == 0, jnp.concatenate([src_mass, other]), jnp.concatenate([other, src_mass])
    ).reshape(CHUNKS, LANES)
    tgt_cols = lax.dynamic_slice_in_dim(tgt_mass, xl * COLS, COLS, 0).reshape(CHUNKS, LANES)
    mask = lax.dynamic_slice_in_dim(tile_mask, xl * (COLS // TILE), COLS // TILE, 1)
    where = jnp.stack([z, y, c, xl]).astype(jnp.int32)

    kernel, sums = pl.pallas_call(
        build_body,
        out_shape=(KERNEL, SMALL),
        in_specs=[SMEM, SMEM] + [VMEM] * (2 + len(blocks)),
        out_specs=(VMEM, VMEM),
        scratch_shapes=[
            pltpu.VMEM((VECTOR_DIMENSION, COLS), jnp.bfloat16),
            pltpu.VMEM((ROWS, LANES), F32),
        ],
        compiler_params=PARAMS,
    )(where, mask, src_a, src_b, *blocks)

    for sweep in range(ITERS):
        src_scale, sent = pl.pallas_call(
            columns_body,
            out_shape=(SMALL, WIDE),
            in_specs=[VMEM] * 6,
            out_specs=(VMEM, VMEM),
            compiler_params=PARAMS,
        )(kernel, src_rows, *row_total(sums))
        parts = lax.all_to_all(sent, PLANE, 0, 0, tiled=True)
        if sweep < ITERS - 1:
            sums = pl.pallas_call(
                rows_body,
                out_shape=SMALL,
                in_specs=[VMEM] * 3,
                out_specs=VMEM,
                scratch_shapes=[pltpu.VMEM((ROWS, LANES), F32)],
                compiler_params=PARAMS,
            )(kernel, tgt_cols, parts)

    log_src = jnp.log(lax.dynamic_slice_in_dim(src_scale, xl * (CHUNKS // 2), CHUNKS // 2, 0)).reshape(-1)
    mine = jnp.log(tgt_cols / jnp.sum(parts, axis=0)).reshape(-1)
    other = shift(mine, "xl", 2, 1)
    log_tgt = jnp.where(xl == 0, jnp.concatenate([mine, other]), jnp.concatenate([other, mine]))
    return log_src, log_tgt


def solution(mesh):
    fine = Mesh(mesh.devices.reshape(N_Z, N_Y, 2, 2, 2), ("z", "y", "xh", "c", "xl"))
    placed = (
        P("xl", ("xh", "c"), ("z", "y")),
        P("xl", ("z", "y"), ("xh", "c")),
        P(("z", "y"), ("xh", "c")),
        P(("z", "y", "xl")),
        P(("xh", "c")),
    )
    return jax.shard_map(
        shards,
        mesh=fine,
        in_specs=placed,
        out_specs=(P(("z", "y", "xl")), P(("xh", "c"))),
        check_vma=False,
    )
```

time: 760 us -> 173 us (0.23)
  blocking collectives: 493 us -> 13.7 us
  waiting for transfers between devices: 209 us -> 84.6 us
  starting transfers between devices: 0.11 us -> 43.5 us
  matrix products: 40.5 us -> 0 us
  local copies, waits for them, and re-layouts: 0.73 us -> 9.83 us
    psum x6 -> x0, blocking collectives: 493 us -> none  [the longest x3 471 us: shards(): tgt_scale = tgt_mass / lax.psum(col_part, ('row', 'depth'))]
    reduce_scatter x1 -> x0, waiting for transfers between devices: 100 us -> none  [shards(): lax.psum_scatter(affinity_between_blocks(supply_slice, demand_slice) * sh...]
    all_gather x2 -> x1, waiting for transfers between devices: 107 us -> 19.7 us  [shards(): src_a = lax.all_gather(src_emb[0], X, axis=0, tiled=True)]
    ppermute x0 -> x27, waiting for transfers between devices: none -> 43.2 us  [shift(): lax.ppermute(value, axis, [(i, (i + by) % size) for i in range(size)])]
    dot_general x7 -> x0, matrix products: 40.5 us -> none  [the longest x3 19 us: shards(): row_part = jnp.dot(kernel, tgt_scale, precision=lax.Precision.HIGHEST)]
    ppermute x0 -> x27, starting transfers between devices: none -> 28.8 us  [shift(): lax.ppermute(value, axis, [(i, (i + by) % size) for i in range(size)])]
    all_to_all x0 -> x2, waiting for transfers between devices: none -> 21 us  [shards(): parts = lax.all_to_all(sent, PLANE, 0, 0, tiled=True)]
    all_to_all x0 -> x2, starting transfers between devices: none -> 14.6 us  [shards(): parts = lax.all_to_all(sent, PLANE, 0, 0, tiled=True)]
  transfers between devices with their start and end apart: 3 -> 30, of which waited for: 3 -> 21; matrix products, arithmetic and copies ran while one was open for 0% -> 1% of each run, Pallas kernels for 0% -> 0%
where the time goes in v1:
time: 173 us; the launch traced here: 172 us
  waiting for transfers between devices  84.6 us (49%)
  starting transfers between devices  43.5 us (25%)
  between operations  14.2 us (8%)
  blocking collectives  13.7 us (8%)
  local copies, waits for them, and re-layouts  9.83 us (6%)
  Pallas kernels  5.09 us (3%)
    ppermute x27, waiting for transfers between devices, shift(): lax.ppermute(value, axis, [(i, (i + by) % size) for i in range(size)])  43.2 us
    ppermute x27, starting transfers between devices, shift(): lax.ppermute(value, axis, [(i, (i + by) % size) for i in range(size)])  28.8 us
    all_to_all x2, waiting for transfers between devices, shards(): parts = lax.all_to_all(sent, PLANE, 0, 0, tiled=True)  21 us
    all_gather x1, waiting for transfers between devices, shards(): src_a = lax.all_gather(src_emb[0], X, axis=0, tiled=True)  19.7 us
    all_to_all x2, starting transfers between devices, shards(): parts = lax.all_to_all(sent, PLANE, 0, 0, tiled=True)  14.6 us
    all_to_all x1, blocking collectives, shards(): parts = lax.all_to_all(sent, PLANE, 0, 0, tiled=True)  13.7 us
    unnamed x18, local copies, waits for them, and re-layouts  8.36 us
  transfers between devices with their start and end apart: 30, of which 21 were waited for; matrix products, arithmetic and copies ran while one was open for 1% of the time, Pallas kernels for 0%

profile of v1, /device:TPU:6, one launch (start us, length us, event | category | flops | bytes accessed | tf_op | source)
XLA Modules:
  0.0 171.7 jit_solution(11018416244056348307)
XLA Ops:
  10.3 2.3 %collective-permute-done.1 = bf16[16,1024]{1,0:T(8,128)(2,1)S(1)} collective-permute-done((bf16[16,1024]{1,0:T(8,128)(2,1)S(1)}, bf16[16,1024]{1,0:T(8,128)(2,1)S(1)}, u32[]{:S(2)}, u32[]{:S(2)}) %collective-permute-start.1) | collective-permute-done | bytes 32800 | tf_op jit(solution)/shard_map/ppermute | solution.py:30
  12.6 1.6 collective-permute-start.2
  14.2 1.7 collective-permute-start.3
  15.9 2.0 %collective-permute-start.4 = (bf16[32,1024]{1,0:T(8,128)(2,1)S(1)}, bf16[32,1024]{1,0:T(8,128)(2,1)S(1)}, u32[]{:S(2)}, u32[]{:S(2)}) collective-permute-start(bf16[32,1024]{1,0:T(8,128)(2,1)S(1)} %pad_maximum_fusion), channel_id=1, source_target_pairs={{0,16},{8,24},{16,0},{24,8},{1,17},{9,25},{17,1},{25,9},{2,18},{10... | collective-permute-start | bytes 196616 | tf_op jit(solution)/shard_map/ppermute | solution.py:30
  18.6 19.7 %all-gather.3.cloned.1.call-done = bf16[1,512,1024]{2,1,0:T(8,128)(2,1)} async-done(((bf16[1,128,1024]{2,1,0:T(8,128)(2,1)}), bf16[1,512,1024]{2,1,0:T(8,128)(2,1)}) %all-gather.3.cloned.1.call-update) | async-done | bytes 1048592 | tf_op jit(solution)/shard_map/all_gather | solution.py:133
  38.4 1.6 collective-permute-start.5
  40.0 1.8 %collective-permute-start.6 = (bf16[128,1024]{1,0:T(8,128)(2,1)S(1)}, bf16[128,1024]{1,0:T(8,128)(2,1)S(1)}, u32[]{:S(2)}, u32[]{:S(2)}) collective-permute-start(bf16[128,1024]{1,0:T(8,128)(2,1)S(1)} %constant_dynamic-update-slice_fusion.refs_0_), channel_id=1, source_target_pairs={{0,224},{32,0},{64,32},{96,64},{128,96},{160,128},{192,160},{224,1... | collective-permute-start | bytes 786440 | tf_op jit(solution)/shard_map/ppermute | solution.py:30
  41.9 6.9 %collective-permute-done.5.refs_1_ = bf16[128,1024]{1,0:T(8,128)(2,1)S(1)} collective-permute-done((bf16[128,1024]{1,0:T(8,128)(2,1)S(1)}, bf16[128,1024]{1,0:T(8,128)(2,1)S(1)}, u32[]{:S(2)}, u32[]{:S(2)}) %collective-permute-start.5) | collective-permute-done | bytes 262176 | tf_op jit(solution)/shard_map/ppermute | solution.py:30
  48.7 3.2 %collective-permute-start.8 = (bf16[128,1024]{1,0:T(8,128)(2,1)S(1)}, bf16[128,1024]{1,0:T(8,128)(2,1)S(1)}, u32[]{:S(2)}, u32[]{:S(2)}) collective-permute-start(bf16[128,1024]{1,0:T(8,128)(2,1)S(1)} %collective-permute-done.6.refs_2_), channel_id=1, source_target_pairs={{0,224},{32,0},{64,32},{96,64},{128,96},{160,128},{192,160},{224,1... | collective-permute-start | bytes 786440 | tf_op jit(solution)/shard_map/ppermute | solution.py:30
  52.0 6.1 %collective-permute-done.7.refs_3_ = bf16[128,1024]{1,0:T(8,128)(2,1)S(1)} collective-permute-done((bf16[128,1024]{1,0:T(8,128)(2,1)S(1)}, bf16[128,1024]{1,0:T(8,128)(2,1)S(1)}, u32[]{:S(2)}, u32[]{:S(2)}) %collective-permute-start.7) | collective-permute-done | bytes 262176 | tf_op jit(solution)/shard_map/ppermute | solution.py:30
  58.1 3.2 %collective-permute-start.10 = (bf16[128,1024]{1,0:T(8,128)(2,1)S(1)}, bf16[128,1024]{1,0:T(8,128)(2,1)S(1)}, u32[]{:S(2)}, u32[]{:S(2)}) collective-permute-start(bf16[128,1024]{1,0:T(8,128)(2,1)S(1)} %collective-permute-done.8.refs_4_), channel_id=1, source_target_pairs={{0,224},{32,0},{64,32},{96,64},{128,96},{160,128},{192,160},{224,1... | collective-permute-start | bytes 786440 | tf_op jit(solution)/shard_map/ppermute | solution.py:30
  61.3 5.2 %collective-permute-done.9.refs_5_ = bf16[128,1024]{1,0:T(8,128)(2,1)S(1)} collective-permute-done((bf16[128,1024]{1,0:T(8,128)(2,1)S(1)}, bf16[128,1024]{1,0:T(8,128)(2,1)S(1)}, u32[]{:S(2)}, u32[]{:S(2)}) %collective-permute-start.9) | collective-permute-done | bytes 262176 | tf_op jit(solution)/shard_map/ppermute | solution.py:30
  66.7 3.3 %collective-permute-start.12 = (bf16[64,1024]{1,0:T(8,128)(2,1)S(1)}, bf16[64,1024]{1,0:T(8,128)(2,1)S(1)}, u32[]{:S(2)}, u32[]{:S(2)}) collective-permute-start(bf16[64,1024]{1,0:T(8,128)(2,1)S(1)} %slice.9), channel_id=1, source_target_pairs={{0,224},{32,0},{64,32},{96,64},{128,96},{160,128},{192,160},{224,1... | collective-permute-start | bytes 393224 | tf_op jit(solution)/shard_map/ppermute | solution.py:30
  70.2 2.7 %collective-permute-done.11.refs_7_ = bf16[64,1024]{1,0:T(8,128)(2,1)S(1)} collective-permute-done((bf16[64,1024]{1,0:T(8,128)(2,1)S(1)}, bf16[64,1024]{1,0:T(8,128)(2,1)S(1)}, u32[]{:S(2)}, u32[]{:S(2)}) %collective-permute-start.11) | collective-permute-done | bytes 131104 | tf_op jit(solution)/shard_map/ppermute | solution.py:30
  74.1 1.7 shard_map.68
  75.8 2.0 %copy-done.1 = f32[1024,1024]{1,0:T(8,128)} copy-done((f32[1024,1024]{1,0:T(8,128)}, f32[1024,1024]{1,0:T(8,128)S(1)}, u32[]{:S(2)}) %copy-start.1) | copy-done | bytes 4194328
  78.9 1.8 %collective-permute-start.15 = (f32[8,128]{1,0:T(8,128)S(1)}, f32[8,128]{1,0:T(8,128)S(1)}, u32[]{:S(2)}, u32[]{:S(2)}) collective-permute-start(f32[8,128]{1,0:T(8,128)S(1)} %add.25.refs_0_), channel_id=1, source_target_pairs={{0,4},{1,5},{4,0},{5,1},{2,6},{3,7},{6,2},{7,3},{8,12},{9,13},{12,... | collective-permute-start | bytes 12296 | tf_op jit(solution)/shard_map/ppermute | solution.py:30
  80.7 1.8 %collective-permute-start.16 = (f32[8,128]{1,0:T(8,128)S(1)}, f32[8,128]{1,0:T(8,128)S(1)}, u32[]{:S(2)}, u32[]{:S(2)}) collective-permute-start(f32[8,128]{1,0:T(8,128)S(1)} %add.25.refs_0_), channel_id=1, source_target_pairs={{0,1},{1,4},{4,5},{5,0},{2,3},{3,6},{6,7},{7,2},{8,9},{9,12},{12,1... | collective-permute-start | bytes 12296 | tf_op jit(solution)/shard_map/ppermute | solution.py:30
  84.3 3.0 %collective-permute-done.17.refs_3_ = f32[8,128]{1,0:T(8,128)S(1)} collective-permute-done((f32[8,128]{1,0:T(8,128)S(1)}, f32[8,128]{1,0:T(8,128)S(1)}, u32[]{:S(2)}, u32[]{:S(2)}) %collective-permute-start.17) | collective-permute-done | bytes 4128 | tf_op jit(solution)/shard_map/ppermute | solution.py:30
  87.3 2.2 %copy-done.2 = f32[1024,1024]{1,0:T(8,128)S(1)} copy-done((f32[1024,1024]{1,0:T(8,128)S(1)}, f32[1024,1024]{1,0:T(8,128)}, u32[]{:S(2)}) %copy-start.2) | copy-done | bytes 4194328
  90.5 10.8 %all-to-all-start = ((f32[32,8,128]{2,1,0:T(8,128)}), f32[32,8,128]{2,1,0:T(8,128)S(1)}, u32[]{:S(2)}, u32[]{:S(2)}) async-start(f32[32,8,128]{2,1,0:T(8,128)} %get-tuple-element.10), calls=%async_computation | async-start | bytes 262144 | tf_op jit(solution)/shard_map/all_to_all | solution.py:178
  101.3 10.5 %all-to-all-done.parts_ref = f32[32,8,128]{2,1,0:T(8,128)S(1)} async-done(((f32[32,8,128]{2,1,0:T(8,128)}), f32[32,8,128]{2,1,0:T(8,128)S(1)}, u32[]{:S(2)}, u32[]{:S(2)}) %all-to-all-start) | async-done | bytes 131104 | tf_op jit(solution)/shard_map/all_to_all | solution.py:178
  111.9 2.2 %copy-done.3 = f32[1024,1024]{1,0:T(8,128)S(1)} copy-done((f32[1024,1024]{1,0:T(8,128)S(1)}, f32[1024,1024]{1,0:T(8,128)}, u32[]{:S(2)}) %copy-start.3) | copy-done | bytes 4194328
  116.1 2.1 %collective-permute-start.20 = (f32[8,128]{1,0:T(8,128)S(1)}, f32[8,128]{1,0:T(8,128)S(1)}, u32[]{:S(2)}, u32[]{:S(2)}) collective-permute-start(f32[8,128]{1,0:T(8,128)S(1)} %add.26.refs_0_), channel_id=1, source_target_pairs={{0,1},{1,4},{4,5},{5,0},{2,3},{3,6},{6,7},{7,2},{8,9},{9,12},{12,1... | collective-permute-start | bytes 12296 | tf_op jit(solution)/shard_map/ppermute | solution.py:30
  118.2 2.6 %collective-permute-done.19.refs_1_ = f32[8,128]{1,0:T(8,128)S(1)} collective-permute-done((f32[8,128]{1,0:T(8,128)S(1)}, f32[8,128]{1,0:T(8,128)S(1)}, u32[]{:S(2)}, u32[]{:S(2)}) %collective-permute-start.19) | collective-permute-done | bytes 4128 | tf_op jit(solution)/shard_map/ppermute | solution.py:30
  120.8 2.2 %collective-permute-done.21.refs_3_ = f32[8,128]{1,0:T(8,128)S(1)} collective-permute-done((f32[8,128]{1,0:T(8,128)S(1)}, f32[8,128]{1,0:T(8,128)S(1)}, u32[]{:S(2)}, u32[]{:S(2)}) %collective-permute-start.21) | collective-permute-done | bytes 4128 | tf_op jit(solution)/shard_map/ppermute | solution.py:30
  123.6 13.7 %all_to_all.15.parts_ref = f32[32,8,128]{2,1,0:T(8,128)S(1)} all-to-all(f32[32,8,128]{2,1,0:T(8,128)S(1)} %get-tuple-element.11), channel_id=1, replica_groups=mesh['z'=8,'y'=4,'xh'=2,'c'=2,'xl'=2] {'z','y'}, dimensions={0} | all-to-all | bytes 262144 | tf_op jit(solution)/shard_map/all_to_all | solution.py:178
  139.0 1.4 collective-permute-start.24
  141.0 3.1 %collective-permute-done.23.refs_1_ = f32[8,128]{1,0:T(8,128)S(1)} collective-permute-done((f32[8,128]{1,0:T(8,128)S(1)}, f32[8,128]{1,0:T(8,128)S(1)}, u32[]{:S(2)}, u32[]{:S(2)}) %collective-permute-start.23) | collective-permute-done | bytes 4128 | tf_op jit(solution)/shard_map/ppermute | solution.py:30
  146.2 3.8 %all-to-all-start.2 = ((f32[32,8,128]{2,1,0:T(8,128)}), f32[32,8,128]{2,1,0:T(8,128)S(1)}, u32[]{:S(2)}, u32[]{:S(2)}) async-start(f32[32,8,128]{2,1,0:T(8,128)} %get-tuple-element.13), calls=%async_computation.2 | async-start | bytes 262144 | tf_op jit(solution)/shard_map/all_to_all | solution.py:178
  150.1 10.5 %all-to-all-done.2 = f32[32,8,128]{2,1,0:T(8,128)S(1)} async-done(((f32[32,8,128]{2,1,0:T(8,128)}), f32[32,8,128]{2,1,0:T(8,128)S(1)}, u32[]{:S(2)}, u32[]{:S(2)}) %all-to-all-start.2) | async-done | bytes 131104 | tf_op jit(solution)/shard_map/all_to_all | solution.py:178
  161.3 3.0 %collective-permute-done.26 = f32[1024]{0:T(1024)S(1)} collective-permute-done((f32[1024]{0:T(1024)S(1)}, f32[1024]{0:T(1024)S(1)}, u32[]{:S(2)}, u32[]{:S(2)}) %collective-permute-start.26) | collective-permute-done | bytes 4128 | tf_op jit(solution)/shard_map/ppermute | solution.py:30
  (70 shorter events, 17.8 us)
Async XLA Ops:
  7.2 62.9 %copy-start = (s32[2,4]{1,0:T(2,128)S(1)}, s32[2,4]{1,0:T(2,128)}, u32[]{:S(2)}) copy-start(s32[2,4]{1,0:T(2,128)} %param.7) | copy-start | bytes 100
  7.2 70.6 %copy-start.6 = (f32[512]{0:T(512)S(1)}, f32[512]{0:T(512)}, u32[]{:S(2)}) copy-start(f32[512]{0:T(512)} %param.8) | copy-start | bytes 6148
  7.2 31.2 %all-gather.3.cloned.1.call-start = ((), (), s32[]{:S(2)}) async-start(), calls=%async_computation.3 | async-start | bytes 1310720 | tf_op jit(solution)/shard_map/all_gather | solution.py:133
  8.7 3.9 %collective-permute-start.1 = (bf16[16,1024]{1,0:T(8,128)(2,1)S(1)}, bf16[16,1024]{1,0:T(8,128)(2,1)S(1)}, u32[]{:S(2)}, u32[]{:S(2)}) collective-permute-start(bf16[16,1024]{1,0:T(8,128)(2,1)S(1)} %dynamic-slice_bitcast_fusion), channel_id=1, source_target_pairs={{0,1},{1,0},{2,3},{3,2},{4,5},{5,4},{6,7},{7,6},{8,9},{9,8},{10,11... | collective-permute-start | bytes 98312 | tf_op jit(solution)/shard_map/ppermute | solution.py:30
  12.6 5.5 %collective-permute-start.2 = (bf16[32,1024]{1,0:T(8,128)(2,1)S(1)}, bf16[32,1024]{1,0:T(8,128)(2,1)S(1)}, u32[]{:S(2)}, u32[]{:S(2)}) collective-permute-start(bf16[32,1024]{1,0:T(8,128)(2,1)S(1)} %pad_maximum_fusion), channel_id=1, source_target_pairs={{0,8},{8,16},{16,24},{24,0},{1,9},{9,17},{17,25},{25,1},{2,10},{10... | collective-permute-start | bytes 196616 | tf_op jit(solution)/shard_map/ppermute | solution.py:30
  14.2 4.4 %collective-permute-start.3 = (bf16[32,1024]{1,0:T(8,128)(2,1)S(1)}, bf16[32,1024]{1,0:T(8,128)(2,1)S(1)}, u32[]{:S(2)}, u32[]{:S(2)}) collective-permute-start(bf16[32,1024]{1,0:T(8,128)(2,1)S(1)} %pad_maximum_fusion), channel_id=1, source_target_pairs={{0,24},{8,0},{16,8},{24,16},{1,25},{9,1},{17,9},{25,17},{2,26},{10... | collective-permute-start | bytes 196616 | tf_op jit(solution)/shard_map/ppermute | solution.py:30
  15.9 22.5 %collective-permute-start.4 = (bf16[32,1024]{1,0:T(8,128)(2,1)S(1)}, bf16[32,1024]{1,0:T(8,128)(2,1)S(1)}, u32[]{:S(2)}, u32[]{:S(2)}) collective-permute-start(bf16[32,1024]{1,0:T(8,128)(2,1)S(1)} %pad_maximum_fusion), channel_id=1, source_target_pairs={{0,16},{8,24},{16,0},{24,8},{1,17},{9,25},{17,1},{25,9},{2,18},{10... | collective-permute-start | bytes 196616 | tf_op jit(solution)/shard_map/ppermute | solution.py:30
  38.4 34.5 %collective-permute-start = (bf16[512,1024]{1,0:T(8,128)(2,1)}, bf16[512,1024]{1,0:T(8,128)(2,1)S(1)}, u32[]{:S(2)}, u32[]{:S(2)}) collective-permute-start(bf16[512,1024]{1,0:T(8,128)(2,1)} %bitcast.20), channel_id=1, source_target_pairs={{0,2},{2,0},{1,3},{3,1},{4,6},{6,4},{5,7},{7,5},{8,10},{10,8},{9,1... | collective-permute-start | bytes 3145736 | tf_op jit(solution)/shard_map/ppermute | solution.py:30
  38.4 10.4 %collective-permute-start.5 = (bf16[128,1024]{1,0:T(8,128)(2,1)S(1)}, bf16[128,1024]{1,0:T(8,128)(2,1)S(1)}, u32[]{:S(2)}, u32[]{:S(2)}) collective-permute-start(bf16[128,1024]{1,0:T(8,128)(2,1)S(1)} %constant_dynamic-update-slice_fusion.refs_0_), channel_id=1, source_target_pairs={{0,32},{32,64},{64,96},{96,128},{128,160},{160,192},{192,224},{224... | collective-permute-start | bytes 786440 | tf_op jit(solution)/shard_map/ppermute | solution.py:30
  40.0 8.7 %collective-permute-start.6 = (bf16[128,1024]{1,0:T(8,128)(2,1)S(1)}, bf16[128,1024]{1,0:T(8,128)(2,1)S(1)}, u32[]{:S(2)}, u32[]{:S(2)}) collective-permute-start(bf16[128,1024]{1,0:T(8,128)(2,1)S(1)} %constant_dynamic-update-slice_fusion.refs_0_), channel_id=1, source_target_pairs={{0,224},{32,0},{64,32},{96,64},{128,96},{160,128},{192,160},{224,1... | collective-permute-start | bytes 786440 | tf_op jit(solution)/shard_map/ppermute | solution.py:30
  48.7 9.4 %collective-permute-start.7 = (bf16[128,1024]{1,0:T(8,128)(2,1)S(1)}, bf16[128,1024]{1,0:T(8,128)(2,1)S(1)}, u32[]{:S(2)}, u32[]{:S(2)}) collective-permute-start(bf16[128,1024]{1,0:T(8,128)(2,1)S(1)} %collective-permute-done.5.refs_1_), channel_id=1, source_target_pairs={{0,32},{32,64},{64,96},{96,128},{128,160},{160,192},{192,224},{224... | collective-permute-start | bytes 786440 | tf_op jit(solution)/shard_map/ppermute | solution.py:30
  48.7 9.4 %collective-permute-start.8 = (bf16[128,1024]{1,0:T(8,128)(2,1)S(1)}, bf16[128,1024]{1,0:T(8,128)(2,1)S(1)}, u32[]{:S(2)}, u32[]{:S(2)}) collective-permute-start(bf16[128,1024]{1,0:T(8,128)(2,1)S(1)} %collective-permute-done.6.refs_2_), channel_id=1, source_target_pairs={{0,224},{32,0},{64,32},{96,64},{128,96},{160,128},{192,160},{224,1... | collective-permute-start | bytes 786440 | tf_op jit(solution)/shard_map/ppermute | solution.py:30
  58.1 8.5 %collective-permute-start.9 = (bf16[128,1024]{1,0:T(8,128)(2,1)S(1)}, bf16[128,1024]{1,0:T(8,128)(2,1)S(1)}, u32[]{:S(2)}, u32[]{:S(2)}) collective-permute-start(bf16[128,1024]{1,0:T(8,128)(2,1)S(1)} %collective-permute-done.7.refs_3_), channel_id=1, source_target_pairs={{0,32},{32,64},{64,96},{96,128},{128,160},{160,192},{192,224},{224... | collective-permute-start | bytes 786440 | tf_op jit(solution)/shard_map/ppermute | solution.py:30
  58.1 8.6 %collective-permute-start.10 = (bf16[128,1024]{1,0:T(8,128)(2,1)S(1)}, bf16[128,1024]{1,0:T(8,128)(2,1)S(1)}, u32[]{:S(2)}, u32[]{:S(2)}) collective-permute-start(bf16[128,1024]{1,0:T(8,128)(2,1)S(1)} %collective-permute-done.8.refs_4_), channel_id=1, source_target_pairs={{0,224},{32,0},{64,32},{96,64},{128,96},{160,128},{192,160},{224,1... | collective-permute-start | bytes 786440 | tf_op jit(solution)/shard_map/ppermute | solution.py:30
  66.6 6.3 %collective-permute-start.11 = (bf16[64,1024]{1,0:T(8,128)(2,1)S(1)}, bf16[64,1024]{1,0:T(8,128)(2,1)S(1)}, u32[]{:S(2)}, u32[]{:S(2)}) collective-permute-start(bf16[64,1024]{1,0:T(8,128)(2,1)S(1)} %slice.8), channel_id=1, source_target_pairs={{0,32},{32,64},{64,96},{96,128},{128,160},{160,192},{192,224},{224... | collective-permute-start | bytes 393224 | tf_op jit(solution)/shard_map/ppermute | solution.py:30
  66.7 6.1 %collective-permute-start.12 = (bf16[64,1024]{1,0:T(8,128)(2,1)S(1)}, bf16[64,1024]{1,0:T(8,128)(2,1)S(1)}, u32[]{:S(2)}, u32[]{:S(2)}) collective-permute-start(bf16[64,1024]{1,0:T(8,128)(2,1)S(1)} %slice.9), channel_id=1, source_target_pairs={{0,224},{32,0},{64,32},{96,64},{128,96},{160,128},{192,160},{224,1... | collective-permute-start | bytes 393224 | tf_op jit(solution)/shard_map/ppermute | solution.py:30
  77.8 1.2 collective-permute-start.14
  77.8 5.0 %collective-permute-start.13 = (f32[512]{0:T(512)S(1)}, f32[512]{0:T(512)S(1)}, u32[]{:S(2)}, u32[]{:S(2)}) collective-permute-start(f32[512]{0:T(512)S(1)} %copy-done.6), channel_id=1, source_target_pairs={{0,1},{1,0},{2,3},{3,2},{4,5},{5,4},{6,7},{7,6},{8,9},{9,8},{10,11... | collective-permute-start | bytes 6152 | tf_op jit(solution)/shard_map/ppermute | solution.py:30
  78.9 5.1 %collective-permute-start.15 = (f32[8,128]{1,0:T(8,128)S(1)}, f32[8,128]{1,0:T(8,128)S(1)}, u32[]{:S(2)}, u32[]{:S(2)}) collective-permute-start(f32[8,128]{1,0:T(8,128)S(1)} %add.25.refs_0_), channel_id=1, source_target_pairs={{0,4},{1,5},{4,0},{5,1},{2,6},{3,7},{6,2},{7,3},{8,12},{9,13},{12,... | collective-permute-start | bytes 12296 | tf_op jit(solution)/shard_map/ppermute | solution.py:30
  80.7 3.6 %collective-permute-start.16 = (f32[8,128]{1,0:T(8,128)S(1)}, f32[8,128]{1,0:T(8,128)S(1)}, u32[]{:S(2)}, u32[]{:S(2)}) collective-permute-start(f32[8,128]{1,0:T(8,128)S(1)} %add.25.refs_0_), channel_id=1, source_target_pairs={{0,1},{1,4},{4,5},{5,0},{2,3},{3,6},{6,7},{7,2},{8,9},{9,12},{12,1... | collective-permute-start | bytes 12296 | tf_op jit(solution)/shard_map/ppermute | solution.py:30
  82.5 4.8 %collective-permute-start.17 = (f32[8,128]{1,0:T(8,128)S(1)}, f32[8,128]{1,0:T(8,128)S(1)}, u32[]{:S(2)}, u32[]{:S(2)}) collective-permute-start(f32[8,128]{1,0:T(8,128)S(1)} %add.25.refs_0_), channel_id=1, source_target_pairs={{0,5},{1,0},{4,1},{5,4},{2,7},{3,2},{6,3},{7,6},{8,13},{9,8},{12,9... | collective-permute-start | bytes 12296 | tf_op jit(solution)/shard_map/ppermute | solution.py:30
  90.5 21.3 %all-to-all-start = ((f32[32,8,128]{2,1,0:T(8,128)}), f32[32,8,128]{2,1,0:T(8,128)S(1)}, u32[]{:S(2)}, u32[]{:S(2)}) async-start(f32[32,8,128]{2,1,0:T(8,128)} %get-tuple-element.10), calls=%async_computation | async-start | bytes 262144 | tf_op jit(solution)/shard_map/all_to_all | solution.py:178
  114.4 1.3 collective-permute-start.18
  115.7 5.1 %collective-permute-start.19 = (f32[8,128]{1,0:T(8,128)S(1)}, f32[8,128]{1,0:T(8,128)S(1)}, u32[]{:S(2)}, u32[]{:S(2)}) collective-permute-start(f32[8,128]{1,0:T(8,128)S(1)} %add.26.refs_0_), channel_id=1, source_target_pairs={{0,4},{1,5},{4,0},{5,1},{2,6},{3,7},{6,2},{7,3},{8,12},{9,13},{12,... | collective-permute-start | bytes 12296 | tf_op jit(solution)/shard_map/ppermute | solution.py:30
  116.1 4.7 %collective-permute-start.20 = (f32[8,128]{1,0:T(8,128)S(1)}, f32[8,128]{1,0:T(8,128)S(1)}, u32[]{:S(2)}, u32[]{:S(2)}) collective-permute-start(f32[8,128]{1,0:T(8,128)S(1)} %add.26.refs_0_), channel_id=1, source_target_pairs={{0,1},{1,4},{4,5},{5,0},{2,3},{3,6},{6,7},{7,2},{8,9},{9,12},{12,1... | collective-permute-start | bytes 12296 | tf_op jit(solution)/shard_map/ppermute | solution.py:30
  118.2 4.8 %collective-permute-start.21 = (f32[8,128]{1,0:T(8,128)S(1)}, f32[8,128]{1,0:T(8,128)S(1)}, u32[]{:S(2)}, u32[]{:S(2)}) collective-permute-start(f32[8,128]{1,0:T(8,128)S(1)} %add.26.refs_0_), channel_id=1, source_target_pairs={{0,5},{1,0},{4,1},{5,4},{2,7},{3,2},{6,3},{7,6},{8,13},{9,8},{12,9... | collective-permute-start | bytes 12296 | tf_op jit(solution)/shard_map/ppermute | solution.py:30
  137.8 1.3 collective-permute-start.22
  139.0 5.1 %collective-permute-start.23 = (f32[8,128]{1,0:T(8,128)S(1)}, f32[8,128]{1,0:T(8,128)S(1)}, u32[]{:S(2)}, u32[]{:S(2)}) collective-permute-start(f32[8,128]{1,0:T(8,128)S(1)} %add.27.refs_0_), channel_id=1, source_target_pairs={{0,4},{1,5},{4,0},{5,1},{2,6},{3,7},{6,2},{7,3},{8,12},{9,13},{12,... | collective-permute-start | bytes 12296 | tf_op jit(solution)/shard_map/ppermute | solution.py:30
  139.0 5.1 %collective-permute-start.24 = (f32[8,128]{1,0:T(8,128)S(1)}, f32[8,128]{1,0:T(8,128)S(1)}, u32[]{:S(2)}, u32[]{:S(2)}) collective-permute-start(f32[8,128]{1,0:T(8,128)S(1)} %add.27.refs_0_), channel_id=1, source_target_pairs={{0,1},{1,4},{4,5},{5,0},{2,3},{3,6},{6,7},{7,2},{8,9},{9,12},{12,1... | collective-permute-start | bytes 12296 | tf_op jit(solution)/shard_map/ppermute | solution.py:30
  140.4 4.8 %collective-permute-start.25 = (f32[8,128]{1,0:T(8,128)S(1)}, f32[8,128]{1,0:T(8,128)S(1)}, u32[]{:S(2)}, u32[]{:S(2)}) collective-permute-start(f32[8,128]{1,0:T(8,128)S(1)} %add.27.refs_0_), channel_id=1, source_target_pairs={{0,5},{1,0},{4,1},{5,4},{2,7},{3,2},{6,3},{7,6},{8,13},{9,8},{12,9... | collective-permute-start | bytes 12296 | tf_op jit(solution)/shard_map/ppermute | solution.py:30
  146.2 14.3 %all-to-all-start.2 = ((f32[32,8,128]{2,1,0:T(8,128)}), f32[32,8,128]{2,1,0:T(8,128)S(1)}, u32[]{:S(2)}, u32[]{:S(2)}) async-start(f32[32,8,128]{2,1,0:T(8,128)} %get-tuple-element.13), calls=%async_computation.2 | async-start | bytes 262144 | tf_op jit(solution)/shard_map/all_to_all | solution.py:178
  160.6 3.7 %collective-permute-start.26 = (f32[1024]{0:T(1024)S(1)}, f32[1024]{0:T(1024)S(1)}, u32[]{:S(2)}, u32[]{:S(2)}) collective-permute-start(f32[1024]{0:T(1024)S(1)} %fusion), channel_id=1, source_target_pairs={{0,1},{1,0},{2,3},{3,2},{4,5},{5,4},{6,7},{7,6},{8,9},{9,8},{10,11... | collective-permute-start | bytes 12296 | tf_op jit(solution)/shard_map/ppermute | solution.py:30
  (5 other events, 34.8 us)
Sparse Core Ops, SparseCore 0:
  9.8 28.4 all-gather.2

commit v2 on v1

v2 whole, which is shorter than its diff:
```python
import math

import jax
import jax.numpy as jnp
from jax import lax
from jax.experimental import pallas as pl
from jax.experimental.pallas import tpu as pltpu
from jax.sharding import Mesh
from jax.sharding import PartitionSpec as P

VECTOR_DIMENSION = 1024
TILE = 512
ITERS = 3
SHARPNESS = 1.0 / (0.64 * math.sqrt(VECTOR_DIMENSION))

X = ("xh", "xl")
PLANE = ("z", "y")
N_Z, N_Y, N_X = 8, 4, 4
ROWS = 1024
COLS = 1024
LANES = 128
CHUNKS = ROWS // LANES
GROUP = 16
F32 = jnp.float32
VMEM = pl.BlockSpec(memory_space=pltpu.VMEM)
HBM = pl.BlockSpec(memory_space=pltpu.HBM)
SMEM = pl.BlockSpec(memory_space=pltpu.SMEM)


def shift(value, axis, size, by):
    return lax.ppermute(value, axis, [(i, (i + by) % size) for i in range(size)])


def wheel(value, by):
    pairs = [
        (i * 2 + c, (i + (by if c == 0 else -by)) % N_Z * 2 + c) for i in range(N_Z) for c in range(2)
    ]
    return lax.ppermute(value, ("z", "c"), pairs)


def wheel_x(value, by):
    place = lambda x, c: x // 2 * 4 + c * 2 + x % 2
    pairs = [
        (place(i, c), place((i + (by if c == 0 else -by)) % N_X, c)) for i in range(N_X) for c in range(2)
    ]
    return lax.ppermute(value, ("xh", "c", "xl"), pairs)


def in_vmem(value):
    return pltpu.with_memory_space_constraint(value, pltpu.VMEM)


def in_hbm(value):
    return pltpu.with_memory_space_constraint(value, pltpu.HBM)


def lane_sums(folded):
    parts = [
        jnp.sum(folded[i * LANES : (i + 1) * LANES, :].T, axis=0, keepdims=True)
        for i in range(folded.shape[0] // LANES)
    ]
    return jnp.concatenate(parts, axis=0)


def natural(low, z, y):
    return pl.multiple_of(low * 512 + z * (N_Y * GROUP) + y * GROUP, GROUP)


def turned(value, size):
    return lax.rem(value + size, size)


CONTRACT = (((0,), (0,)), ((), ()))
TURNS = (0, -1, 1, 2)
STEPS = (0, -1, 1, -2, 2, -3, 3)


def halves_body(tgt_ref, out_ref):
    for y in range(N_Y):
        for low in range(2):
            out_ref[y * 2 + low] = tgt_ref[:, low * COLS : (low + 1) * COLS]


def partial_body(where_ref, mask_hbm, tgt_mass_hbm, src_hbm, *refs):
    src_refs, block_refs = refs[:7], refs[7:14]
    scores_ref, src_last_ref, live_ref, tgt_cols_ref, side_ref = refs[14:19]
    src_ref, tgt_ref, mask_ref, tgt_mass_ref, sems = refs[19:]
    z, c, xh, xl = (where_ref[i] for i in range(4))

    def src_at(core, turn):
        x = turned(xh * 2 + xl + turn * (1 - 2 * core), N_X)
        to = lax.rem(x, 2) * 512 + lax.div(x, 2) * 256 + core * 128
        return src_ref.at[pl.ds(pl.multiple_of(to, LANES), LANES), :]

    fetches = [
        pltpu.make_async_copy(src_hbm, src_at(c, 0), sems.at[0]),
        pltpu.make_async_copy(mask_hbm, mask_ref, sems.at[1]),
        pltpu.make_async_copy(tgt_mass_hbm, tgt_mass_ref, sems.at[2]),
    ]
    for fetch in fetches:
        fetch.start()
    for index, part in enumerate(src_refs):
        core, turn = (c, index + 1) if index < 3 else (1 - c, index - 3)
        src_at(core, TURNS[turn])[...] = part[...]
    for block, step in zip(block_refs, STEPS, strict=True):
        plane = turned(z + step * (1 - 2 * c), N_Z)
        for place in range(4):
            for low in range(2):
                to = natural(low, plane, place)
                start = (place * 2 + low) * GROUP
                tgt_ref[pl.ds(to, GROUP), :] = block[start : start + GROUP, :]
    plane = turned(z + 4, N_Z)
    for low in range(2):
        tgt_ref[pl.ds(natural(low, plane, 0), N_Y * GROUP), :] = jnp.zeros((N_Y * GROUP, COLS), jnp.bfloat16)
    for fetch in fetches:
        fetch.wait()
    for place in range(4):
        for low in range(2):
            start = (place * 2 + low) * GROUP
            src_last_ref[start : start + GROUP, :] = src_ref[pl.ds(natural(low, plane, place), GROUP), :]
    tgt_cols_ref[...] = jnp.where(xl == 0, tgt_mass_ref[:CHUNKS, :], tgt_mass_ref[CHUNKS:, :])
    side_ref[...] = jnp.full(side_ref.shape, xl.astype(F32))
    for i in range(ROWS // TILE):
        rows = slice(i * TILE, (i + 1) * TILE)
        for j in range(COLS // TILE):
            cols = slice(j * TILE, (j + 1) * TILE)
            live = mask_ref[i, xl * (COLS // TILE) + j] > 0
            live_ref[i, j] = jnp.full((8, LANES), live.astype(F32))

            @pl.when(live)
            def _():
                scores_ref[rows, cols] = lax.dot_general(
                    src_ref[:, rows], tgt_ref[:, cols], CONTRACT, preferred_element_type=F32
                )


def build_body(src_last_ref, scores_ref, live_ref, mass_ref, block_ref, kernel_ref, sums_ref, folded_ref):
    for i in range(ROWS // TILE):
        rows = slice(i * TILE, (i + 1) * TILE)
        folded = jnp.zeros((TILE, LANES), F32)
        for j in range(COLS // TILE):
            cols = slice(j * TILE, (j + 1) * TILE)
            scores = scores_ref[rows, cols] + lax.dot_general(
                src_last_ref[:, rows], block_ref[:, cols], CONTRACT, preferred_element_type=F32
            )
            live = live_ref[i, j][:1, :1] > 0.0
            part = jnp.where(live, jnp.exp(scores * SHARPNESS), 0.0)
            kernel_ref[rows, cols] = part
            for k in range(TILE // LANES):
                folded = folded + part[:, k * LANES : (k + 1) * LANES]
        folded_ref[rows, :] = folded
    own = mass_ref[...]
    sums = jnp.concatenate([lane_sums(folded_ref[...]), own, own], axis=0)
    sums_ref[...] = jnp.broadcast_to(sums[None], sums_ref.shape)


def first_columns_body(kernel_ref, parts_ref, mass_ref, out_ref):
    half = CHUNKS // 2
    mass = jnp.concatenate([parts_ref[k, CHUNKS : CHUNKS + half, :] for k in range(2)], axis=0)
    mass_ref[...] = mass
    column_sums(kernel_ref, mass / jnp.sum(parts_ref[:, :CHUNKS, :], axis=0), out_ref)


def columns_body(kernel_ref, parts_ref, mass_ref, out_ref):
    column_sums(kernel_ref, mass_ref[...] / jnp.sum(parts_ref[...], axis=0), out_ref)


def last_columns_body(kernel_ref, parts_ref, mass_ref, side_ref, log_ref, out_ref):
    scale = mass_ref[...] / jnp.sum(parts_ref[...], axis=0)
    log_ref[...] = jnp.log(
        jnp.where(side_ref[...] == 0.0, scale[: CHUNKS // 2], scale[CHUNKS // 2 :])
    )
    column_sums(kernel_ref, scale, out_ref)


def column_sums(kernel_ref, scale, out_ref):
    acc = [None] * (COLS // LANES)
    for i in range(CHUNKS):
        wide = jnp.broadcast_to(scale[i : i + 1, :], (LANES, LANES)).T
        for j in range(COLS // LANES):
            prod = kernel_ref[i * LANES : (i + 1) * LANES, j * LANES : (j + 1) * LANES] * wide
            prod = jnp.sum(prod.reshape(LANES // 8, 8, LANES), axis=0)
            acc[j] = prod if acc[j] is None else acc[j] + prod
    sums = jnp.concatenate([jnp.sum(a, axis=0, keepdims=True) for a in acc], axis=0)
    out_ref[...] = jnp.broadcast_to(sums[None], out_ref.shape)


def rows_body(kernel_ref, mass_ref, parts_ref, sums_ref, folded_ref):
    scale = mass_ref[...] / jnp.sum(parts_ref[...], axis=0)
    for i in range(CHUNKS):
        rows = slice(i * LANES, (i + 1) * LANES)
        total = kernel_ref[rows, :LANES] * scale[0:1, :]
        for j in range(1, COLS // LANES):
            total = total + kernel_ref[rows, j * LANES : (j + 1) * LANES] * scale[j : j + 1, :]
        folded_ref[rows, :] = total
    sums_ref[...] = jnp.broadcast_to(lane_sums(folded_ref[...])[None], sums_ref.shape)


HALF = jax.ShapeDtypeStruct((CHUNKS // 2, LANES), F32)
SMALL = jax.ShapeDtypeStruct((CHUNKS, LANES), F32)
WIDE = pltpu.VMEM((N_Z * N_Y, CHUNKS, LANES), F32)
RING = (2 * N_X, CHUNKS, LANES)
KERNEL = pltpu.VMEM((ROWS, COLS), F32)
BUILD = pltpu.CompilerParams(vmem_limit_bytes=28 * 1024 * 1024)
SWEEP = pltpu.CompilerParams(vmem_limit_bytes=16 * 1024 * 1024)


def shards(src_emb, tgt_emb, tile_mask, src_mass, tgt_mass):
    sent = pl.pallas_call(
        halves_body,
        out_shape=jax.ShapeDtypeStruct((2 * N_Y, GROUP, COLS), jnp.bfloat16),
        in_specs=[VMEM],
        out_specs=VMEM,
        compiler_params=SWEEP,
    )(tgt_emb[0])
    plane = lax.all_to_all(sent, ("y", "xl"), 0, 0, tiled=True).reshape(2 * N_Y * GROUP, COLS)
    src = src_emb[0]
    plane, one, two = lax.optimization_barrier((plane, wheel_x(src, 1), wheel_x(src, -1)))
    three = wheel_x(one, 1)
    swapped = [shift(s, "c", 2, 1) for s in (src, one, two)]
    blocks = [plane]
    near = away = plane
    for step in range(3):
        near, away = wheel(near, 1), wheel(away, -1)
        if step == 0:
            near, away, three, *swapped = lax.optimization_barrier((near, away, three, *swapped))
            swapped.append(shift(three, "c", 2, 1))
        if step == 1:
            near, away, swapped[3] = lax.optimization_barrier((near, away, swapped[3]))
        blocks += [near, away]
    far = wheel(near, 1)

    where = jnp.stack([lax.axis_index(a) for a in ("z", "c", "xh", "xl")]).astype(jnp.int32)
    scores, src_last, live, tgt_cols, side = pl.pallas_call(
        partial_body,
        out_shape=(
            KERNEL,
            pltpu.VMEM((LANES, ROWS), jnp.bfloat16),
            pltpu.VMEM((ROWS // TILE, COLS // TILE, 8, LANES), F32),
            SMALL,
            HALF,
        ),
        in_specs=[SMEM] + [HBM] * 3 + [VMEM] * (7 + len(blocks)),
        out_specs=(VMEM,) * 5,
        scratch_shapes=[
            pltpu.VMEM((VECTOR_DIMENSION, ROWS), jnp.bfloat16),
            pltpu.VMEM((VECTOR_DIMENSION, COLS), jnp.bfloat16),
            pltpu.SMEM(tile_mask.shape, jnp.int32),
            pltpu.VMEM((2 * CHUNKS, LANES), F32),
            pltpu.SemaphoreType.DMA((3,)),
        ],
        compiler_params=BUILD,
        cost_estimate=pl.CostEstimate(
            flops=2 * ROWS * COLS * VECTOR_DIMENSION, bytes_accessed=10_000_000, transcendentals=0
        ),
    )(where, *map(in_hbm, (tile_mask, tgt_mass.reshape(-1, LANES), src)), one, two, three, *swapped, *blocks)
    own = src_mass.reshape(-1, LANES)
    kernel, sums = pl.pallas_call(
        build_body,
        out_shape=(KERNEL, pltpu.VMEM((2 * N_X, 2 * CHUNKS, LANES), F32)),
        in_specs=[VMEM] * 5,
        out_specs=(VMEM, VMEM),
        scratch_shapes=[pltpu.VMEM((ROWS, LANES), F32)],
        compiler_params=BUILD,
    )(in_vmem(src_last), in_vmem(scores), in_vmem(live), own, far)

    kernel = in_vmem(kernel)
    for sweep in range(ITERS):
        parts = lax.all_to_all(sums, ("xh", "c", "xl"), 0, 0, tiled=True)
        if sweep == 0:
            body, operands, extra = first_columns_body, (), (SMALL,)
        elif sweep < ITERS - 1:
            body, operands, extra = columns_body, (mass,), ()
        else:
            body, operands, extra = last_columns_body, (mass, side), (HALF,)
        outs = pl.pallas_call(
            body,
            out_shape=(*extra, WIDE),
            in_specs=[VMEM] * (2 + len(operands)),
            out_specs=(VMEM,) * (1 + len(extra)),
            compiler_params=SWEEP,
        )(kernel, parts, *operands)
        if sweep == 0:
            mass = outs[0]
        parts = lax.all_to_all(outs[-1], PLANE, 0, 0, tiled=True)
        if sweep < ITERS - 1:
            sums = pl.pallas_call(
                rows_body,
                out_shape=pltpu.VMEM(RING, F32),
                in_specs=[VMEM] * 3,
                out_specs=VMEM,
                scratch_shapes=[pltpu.VMEM((ROWS, LANES), F32)],
                compiler_params=SWEEP,
            )(kernel, tgt_cols, parts)

    log_src = outs[0]
    mine = jnp.log(tgt_cols / jnp.sum(parts, axis=0)).reshape(-1)
    theirs = shift(mine, "xl", 2, 1)
    log_tgt = jnp.where(lax.axis_index("xl") == 0, jnp.concatenate([mine, theirs]), jnp.concatenate([theirs, mine]))
    return log_src.reshape(-1), log_tgt


def solution(mesh):
    fine = Mesh(mesh.devices.reshape(N_Z, N_Y, 2, 2, 2), ("z", "y", "xh", "c", "xl"))
    placed = (
        P("xl", ("xh", "c"), ("z", "y")),
        P("xl", ("z", "y"), ("xh", "c")),
        P(("z", "y"), ("xh", "c")),
        P(("z", "y", "xl")),
        P(("xh", "c")),
    )
    return jax.shard_map(
        shards,
        mesh=fine,
        in_specs=placed,
        out_specs=(P(("z", "y", "xl")), P(("xh", "c"))),
        check_vma=False,
    )
```

time: 173 us -> 136 us (0.79)
  blocking collectives: 13.7 us -> 79.8 us
  waiting for transfers between devices: 84.6 us -> 27.1 us
  starting transfers between devices: 43.5 us -> 17.8 us
  between operations: 14.2 us -> 0.73 us
  local copies, waits for them, and re-layouts: 9.83 us -> 0.85 us
  Pallas kernels: 5.09 us -> 7.53 us
    all_to_all x1 -> x7, blocking collectives: 13.7 us -> 79.8 us  [the longest x3 43.6 us: shards(): parts = lax.all_to_all(outs[-1], PLANE, 0, 0, tiled=True)]
    ppermute x27 -> x5, waiting for transfers between devices: 43.2 us -> 2.96 us  [shift(): lax.ppermute(value, axis, [(i, (i + by) % size) for i in range(size)])]
    ppermute x27 -> x5, starting transfers between devices: 28.8 us -> 2.05 us  [shift(): lax.ppermute(value, axis, [(i, (i + by) % size) for i in range(size)])]
    ppermute x0 -> x10, waiting for transfers between devices: none -> 24.2 us  [the longest x7 24.2 us: wheel(): return lax.ppermute(value, ('z', 'c'), pairs)]
    all_to_all x2 -> x0, waiting for transfers between devices: 21 us -> none  [shards(): parts = lax.all_to_all(sent, PLANE, 0, 0, tiled=True)]
    all_gather x1 -> x0, waiting for transfers between devices: 19.7 us -> none  [shards(): src_a = lax.all_gather(src_emb[0], X, axis=0, tiled=True)]
    ppermute x0 -> x10, starting transfers between devices: none -> 15.7 us  [the longest x7 12.3 us: wheel(): return lax.ppermute(value, ('z', 'c'), pairs)]
    all_to_all x2 -> x0, starting transfers between devices: 14.6 us -> none  [shards(): parts = lax.all_to_all(sent, PLANE, 0, 0, tiled=True)]
  transfers between devices with their start and end apart: 30 -> 15, of which waited for: 21 -> 6; matrix products, arithmetic and copies ran while one was open for 1% -> 0% of each run, Pallas kernels for 0% -> 3%
where the time goes in v2:
time: 136 us; the launch traced here: 134 us
  blocking collectives  79.8 us (59%)
  waiting for transfers between devices  27.1 us (20%)
  starting transfers between devices  17.8 us (13%)
  Pallas kernels  7.53 us (6%)
    all_to_all x3, blocking collectives, shards(): parts = lax.all_to_all(outs[-1], PLANE, 0, 0, tiled=True)  43.6 us
    ppermute x7, waiting for transfers between devices, wheel(): return lax.ppermute(value, ('z', 'c'), pairs)  24.2 us
    all_to_all x3, blocking collectives, shards(): parts = lax.all_to_all(sums, ('xh', 'c', 'xl'), 0, 0, tiled=True)  23.6 us
    all_to_all x1, blocking collectives, shards(): lax.all_to_all(sent, ('y', 'xl'), 0, 0, tiled=True)  12.5 us
    ppermute x7, starting transfers between devices, wheel(): return lax.ppermute(value, ('z', 'c'), pairs)  12.3 us
    pallas_call x1, Pallas kernels, shards(): pl.pallas_call(partial_body, out_shape=(KERNEL, pltpu.VMEM((LANES, ROWS),...  3.78 us
    ppermute x3, starting transfers between devices, wheel_x(): return lax.ppermute(value, ('xh', 'c', 'xl'), pairs)  3.4 us
    ppermute x5, waiting for transfers between devices, shift(): lax.ppermute(value, axis, [(i, (i + by) % size) for i in range(size)])  2.96 us
  transfers between devices with their start and end apart: 15, of which 6 were waited for; matrix products, arithmetic and copies ran while one was open for 0% of the time, Pallas kernels for 3%

profile of v2, /device:TPU:6, one launch (start us, length us, event | category | flops | bytes accessed | tf_op | source)
XLA Modules:
  0.0 134.5 jit_solution(7571709306601937846)
XLA Ops:
  0.6 0.9 collective-permute-start.1
  1.5 2.4 %collective-permute-start = (bf16[128,1024]{1,0:T(8,128)(2,1)}, bf16[128,1024]{1,0:T(8,128)(2,1)S(1)}, u32[]{:S(2)}, u32[]{:S(2)}) collective-permute-start(bf16[128,1024]{1,0:T(8,128)(2,1)} %bitcast.18), channel_id=1, source_target_pairs={{0,1},{2,7},{1,4},{3,2},{4,5},{6,3},{5,0},{7,6},{8,9},{10,15},{9,1... | collective-permute-start | bytes 786440 | tf_op jit(solution)/shard_map/ppermute | solution.py:46
  3.9 0.8 copy-done
  4.8 0.0 copy-start.1
  4.8 12.5 %all_to_all.35 = bf16[8,16,1024]{2,1,0:T(8,128)(2,1)S(1)} all-to-all(bf16[8,16,1024]{2,1,0:T(8,128)(2,1)S(1)} %shard_map.68), channel_id=1, replica_groups=mesh['z'=8,'y'=4,'xh'=2,'c'=2,'xl'=2] {'y','xl'}, dimensions={0} | all-to-all | bytes 524288 | tf_op jit(solution)/shard_map/all_to_all | solution.py:216
  17.3 0.1 collective-permute-start.4
  17.4 1.3 collective-permute-start.7
  18.7 5.9 %collective-permute-start.3 = (bf16[128,1024]{1,0:T(8,128)(2,1)S(1)}, bf16[128,1024]{1,0:T(8,128)(2,1)S(1)}, u32[]{:S(2)}, u32[]{:S(2)}) collective-permute-start(bf16[128,1024]{1,0:T(8,128)(2,1)S(1)} %bitcast.12), channel_id=1, source_target_pairs={{0,224},{2,34},{32,0},{34,66},{64,32},{66,98},{96,64},{98,130},{12... | collective-permute-start | bytes 786440 | tf_op jit(solution)/shard_map/ppermute | solution.py:38
  24.6 5.8 %collective-permute-done.3.refs_9_ = bf16[128,1024]{1,0:T(8,128)(2,1)S(1)} collective-permute-done((bf16[128,1024]{1,0:T(8,128)(2,1)S(1)}, bf16[128,1024]{1,0:T(8,128)(2,1)S(1)}, u32[]{:S(2)}, u32[]{:S(2)}) %collective-permute-start.3) | collective-permute-done | bytes 262176 | tf_op jit(solution)/shard_map/ppermute | solution.py:38
  30.4 1.8 %collective-permute-done.2.refs_8_ = bf16[128,1024]{1,0:T(8,128)(2,1)S(1)} collective-permute-done((bf16[128,1024]{1,0:T(8,128)(2,1)S(1)}, bf16[128,1024]{1,0:T(8,128)(2,1)S(1)}, u32[]{:S(2)}, u32[]{:S(2)}) %collective-permute-start.2) | collective-permute-done | bytes 262176 | tf_op jit(solution)/shard_map/ppermute | solution.py:38
  32.2 3.2 %collective-permute-start.9 = (bf16[128,1024]{1,0:T(8,128)(2,1)S(1)}, bf16[128,1024]{1,0:T(8,128)(2,1)S(1)}, u32[]{:S(2)}, u32[]{:S(2)}) collective-permute-start(bf16[128,1024]{1,0:T(8,128)(2,1)S(1)} %collective-permute-done.3.refs_9_), channel_id=1, source_target_pairs={{0,224},{2,34},{32,0},{34,66},{64,32},{66,98},{96,64},{98,130},{12... | collective-permute-start | bytes 786440 | tf_op jit(solution)/shard_map/ppermute | solution.py:38
  35.4 5.9 %collective-permute-done.8.refs_10_ = bf16[128,1024]{1,0:T(8,128)(2,1)S(1)} collective-permute-done((bf16[128,1024]{1,0:T(8,128)(2,1)S(1)}, bf16[128,1024]{1,0:T(8,128)(2,1)S(1)}, u32[]{:S(2)}, u32[]{:S(2)}) %collective-permute-start.8) | collective-permute-done | bytes 262176 | tf_op jit(solution)/shard_map/ppermute | solution.py:38
  41.4 3.2 %collective-permute-start.12 = (bf16[128,1024]{1,0:T(8,128)(2,1)S(1)}, bf16[128,1024]{1,0:T(8,128)(2,1)}, u32[]{:S(2)}, u32[]{:S(2)}) collective-permute-start(bf16[128,1024]{1,0:T(8,128)(2,1)S(1)} %collective-permute-done.9.refs_11_), channel_id=1, source_target_pairs={{0,224},{2,34},{32,0},{34,66},{64,32},{66,98},{96,64},{98,130},{12... | collective-permute-start | bytes 786440 | tf_op jit(solution)/shard_map/ppermute | solution.py:38
  44.6 6.9 %collective-permute-done.11.refs_12_ = bf16[128,1024]{1,0:T(8,128)(2,1)S(1)} collective-permute-done((bf16[128,1024]{1,0:T(8,128)(2,1)S(1)}, bf16[128,1024]{1,0:T(8,128)(2,1)S(1)}, u32[]{:S(2)}, u32[]{:S(2)}) %collective-permute-start.11) | collective-permute-done | bytes 262176 | tf_op jit(solution)/shard_map/ppermute | solution.py:38
  51.6 0.1 pad_add_fusion.where_ref
  51.6 3.8 %shard_map.69 = (f32[1024,1024]{1,0:T(8,128)S(1)}, bf16[128,1024]{1,0:T(8,128)(2,1)S(1)}, f32[2,2,8,128]{3,2,1,0:T(8,128)S(1)}, f32[8,128]{1,0:T(8,128)S(1)}, f32[4,128]{1,0:T(4,128)S(1)}) custom-call(s32[4]{0:T(128)S(1)} %pad_add_fusion.where_ref, s32[2,4]{1,0:T(2,128)} %mask_hbm.1, f32[16,128]{1,0:T(8,128)} %bitcast.21, bf16[128,1024]{1,0:T(8,128)(2,1)} %bitcast.20, ...), custom_call_target="tpu_custom_call" | custom-call | flops 2147483648 | bytes 10000000 | tf_op jit(solution)/shard_map/pallas_call | solution.py:234
  55.4 3.7 %collective-permute-done.13.block_ref = bf16[128,1024]{1,0:T(8,128)(2,1)S(1)} collective-permute-done((bf16[128,1024]{1,0:T(8,128)(2,1)S(1)}, bf16[128,1024]{1,0:T(8,128)(2,1)S(1)}, u32[]{:S(2)}, u32[]{:S(2)}) %collective-permute-start.13) | collective-permute-done | bytes 262176 | tf_op jit(solution)/shard_map/ppermute | solution.py:38
  59.1 1.3 shard_map.70
  60.4 8.0 %all_to_all.36.parts_ref = f32[8,16,128]{2,1,0:T(8,128)S(1)} all-to-all(f32[8,16,128]{2,1,0:T(8,128)S(1)} %get-tuple-element.42), channel_id=1, replica_groups=mesh['z'=8,'y'=4,'xh'=2,'c'=2,'xl'=2] {'xh','c','xl'}, dimensions={0} | all-to-all | bytes 131072 | tf_op jit(solution)/shard_map/all_to_all | solution.py:269
  68.4 0.4 shard_map.71
  68.8 16.1 %all_to_all.37.parts_ref = f32[32,8,128]{2,1,0:T(8,128)S(1)} all-to-all(f32[32,8,128]{2,1,0:T(8,128)S(1)} %get-tuple-element.43), channel_id=1, replica_groups=mesh['z'=8,'y'=4,'xh'=2,'c'=2,'xl'=2] {'z','y'}, dimensions={0} | all-to-all | bytes 262144 | tf_op jit(solution)/shard_map/all_to_all | solution.py:285
  84.8 0.4 shard_map.72
  85.2 7.8 %all_to_all.38.parts_ref = f32[8,8,128]{2,1,0:T(8,128)S(1)} all-to-all(f32[8,8,128]{2,1,0:T(8,128)S(1)} %shard_map.72), channel_id=1, replica_groups=mesh['z'=8,'y'=4,'xh'=2,'c'=2,'xl'=2] {'xh','c','xl'}, dimensions={0} | all-to-all | bytes 65536 | tf_op jit(solution)/shard_map/all_to_all | solution.py:269
  93.0 0.4 shard_map.73
  93.4 13.7 %all_to_all.39.parts_ref = f32[32,8,128]{2,1,0:T(8,128)S(1)} all-to-all(f32[32,8,128]{2,1,0:T(8,128)S(1)} %shard_map.73), channel_id=1, replica_groups=mesh['z'=8,'y'=4,'xh'=2,'c'=2,'xl'=2] {'z','y'}, dimensions={0} | all-to-all | bytes 262144 | tf_op jit(solution)/shard_map/all_to_all | solution.py:285
  107.2 0.4 shard_map.74
  107.5 7.8 %all_to_all.40.parts_ref = f32[8,8,128]{2,1,0:T(8,128)S(1)} all-to-all(f32[8,8,128]{2,1,0:T(8,128)S(1)} %shard_map.74), channel_id=1, replica_groups=mesh['z'=8,'y'=4,'xh'=2,'c'=2,'xl'=2] {'xh','c','xl'}, dimensions={0} | all-to-all | bytes 65536 | tf_op jit(solution)/shard_map/all_to_all | solution.py:269
  115.4 1.0 shard_map.75
  116.3 13.8 %all_to_all.41 = f32[32,8,128]{2,1,0:T(8,128)S(1)} all-to-all(f32[32,8,128]{2,1,0:T(8,128)S(1)} %get-tuple-element.47), channel_id=1, replica_groups=mesh['z'=8,'y'=4,'xh'=2,'c'=2,'xl'=2] {'z','y'}, dimensions={0} | all-to-all | bytes 262144 | tf_op jit(solution)/shard_map/all_to_all | solution.py:285
  130.2 0.7 collective-permute-start.14
  130.9 2.9 %collective-permute-done.14 = f32[1024]{0:T(1024)S(1)} collective-permute-done((f32[1024]{0:T(1024)S(1)}, f32[1024]{0:T(1024)S(1)}, u32[]{:S(2)}, u32[]{:S(2)}) %collective-permute-start.14) | collective-permute-done | bytes 4128 | tf_op jit(solution)/shard_map/ppermute | solution.py:31
  133.9 0.6 maximum_select_fusion
  (21 shorter events, 0.1 us)
Async XLA Ops:
  0.6 16.7 %collective-permute-start.1 = (bf16[128,1024]{1,0:T(8,128)(2,1)}, bf16[128,1024]{1,0:T(8,128)(2,1)S(1)}, u32[]{:S(2)}, u32[]{:S(2)}) collective-permute-start(bf16[128,1024]{1,0:T(8,128)(2,1)} %bitcast.17), channel_id=1, source_target_pairs={{0,5},{2,3},{1,0},{3,6},{4,1},{6,7},{5,4},{7,2},{8,13},{10,11},{9,... | collective-permute-start | bytes 786440 | tf_op jit(solution)/shard_map/ppermute | solution.py:46
  1.5 15.8 %collective-permute-start = (bf16[128,1024]{1,0:T(8,128)(2,1)}, bf16[128,1024]{1,0:T(8,128)(2,1)S(1)}, u32[]{:S(2)}, u32[]{:S(2)}) collective-permute-start(bf16[128,1024]{1,0:T(8,128)(2,1)} %bitcast.18), channel_id=1, source_target_pairs={{0,1},{2,7},{1,4},{3,2},{4,5},{6,3},{5,0},{7,6},{8,9},{10,15},{9,1... | collective-permute-start | bytes 786440 | tf_op jit(solution)/shard_map/ppermute | solution.py:46
  3.9 20.6 %collective-permute-start.5 = (bf16[128,1024]{1,0:T(8,128)(2,1)}, bf16[128,1024]{1,0:T(8,128)(2,1)S(1)}, u32[]{:S(2)}, u32[]{:S(2)}) collective-permute-start(bf16[128,1024]{1,0:T(8,128)(2,1)} %bitcast.19), channel_id=1, source_target_pairs={{0,2},{2,0},{1,3},{3,1},{4,6},{6,4},{5,7},{7,5},{8,10},{10,8},{9,1... | collective-permute-start | bytes 786440 | tf_op jit(solution)/shard_map/ppermute | solution.py:31
  3.9 0.8 copy-start
  4.8 54.3 %copy-start.1 = (f32[512]{0:T(512)S(1)}, f32[512]{0:T(512)}, u32[]{:S(2)}) copy-start(f32[512]{0:T(512)} %param.8) | copy-start | bytes 6148
  17.3 7.3 %collective-permute-start.6 = (bf16[128,1024]{1,0:T(8,128)(2,1)S(1)}, bf16[128,1024]{1,0:T(8,128)(2,1)S(1)}, u32[]{:S(2)}, u32[]{:S(2)}) collective-permute-start(bf16[128,1024]{1,0:T(8,128)(2,1)S(1)} %collective-permute-done.refs_0_), channel_id=1, source_target_pairs={{0,2},{2,0},{1,3},{3,1},{4,6},{6,4},{5,7},{7,5},{8,10},{10,8},{9,1... | collective-permute-start | bytes 786440 | tf_op jit(solution)/shard_map/ppermute | solution.py:31
  17.3 7.3 %collective-permute-start.4 = (bf16[128,1024]{1,0:T(8,128)(2,1)S(1)}, bf16[128,1024]{1,0:T(8,128)(2,1)S(1)}, u32[]{:S(2)}, u32[]{:S(2)}) collective-permute-start(bf16[128,1024]{1,0:T(8,128)(2,1)S(1)} %collective-permute-done.refs_0_), channel_id=1, source_target_pairs={{0,1},{2,7},{1,4},{3,2},{4,5},{6,3},{5,0},{7,6},{8,9},{10,15},{9,1... | collective-permute-start | bytes 786440 | tf_op jit(solution)/shard_map/ppermute | solution.py:46
  17.4 7.2 %collective-permute-start.7 = (bf16[128,1024]{1,0:T(8,128)(2,1)S(1)}, bf16[128,1024]{1,0:T(8,128)(2,1)S(1)}, u32[]{:S(2)}, u32[]{:S(2)}) collective-permute-start(bf16[128,1024]{1,0:T(8,128)(2,1)S(1)} %collective-permute-done.1.refs_1_), channel_id=1, source_target_pairs={{0,2},{2,0},{1,3},{3,1},{4,6},{6,4},{5,7},{7,5},{8,10},{10,8},{9,1... | collective-permute-start | bytes 786440 | tf_op jit(solution)/shard_map/ppermute | solution.py:31
  18.7 11.7 %collective-permute-start.3 = (bf16[128,1024]{1,0:T(8,128)(2,1)S(1)}, bf16[128,1024]{1,0:T(8,128)(2,1)S(1)}, u32[]{:S(2)}, u32[]{:S(2)}) collective-permute-start(bf16[128,1024]{1,0:T(8,128)(2,1)S(1)} %bitcast.12), channel_id=1, source_target_pairs={{0,224},{2,34},{32,0},{34,66},{64,32},{66,98},{96,64},{98,130},{12... | collective-permute-start | bytes 786440 | tf_op jit(solution)/shard_map/ppermute | solution.py:38
  24.6 7.6 %collective-permute-start.2 = (bf16[128,1024]{1,0:T(8,128)(2,1)S(1)}, bf16[128,1024]{1,0:T(8,128)(2,1)S(1)}, u32[]{:S(2)}, u32[]{:S(2)}) collective-permute-start(bf16[128,1024]{1,0:T(8,128)(2,1)S(1)} %bitcast.13), channel_id=1, source_target_pairs={{0,32},{2,226},{32,64},{34,2},{64,96},{66,34},{96,128},{98,66},{12... | collective-permute-start | bytes 786440 | tf_op jit(solution)/shard_map/ppermute | solution.py:38
  32.2 3.2 %collective-permute-start.10 = (bf16[128,1024]{1,0:T(8,128)(2,1)S(1)}, bf16[128,1024]{1,0:T(8,128)(2,1)S(1)}, u32[]{:S(2)}, u32[]{:S(2)}) collective-permute-start(bf16[128,1024]{1,0:T(8,128)(2,1)S(1)} %collective-permute-done.4.refs_2_), channel_id=1, source_target_pairs={{0,2},{2,0},{1,3},{3,1},{4,6},{6,4},{5,7},{7,5},{8,10},{10,8},{9,1... | collective-permute-start | bytes 786440 | tf_op jit(solution)/shard_map/ppermute | solution.py:31
  32.2 9.2 %collective-permute-start.8 = (bf16[128,1024]{1,0:T(8,128)(2,1)S(1)}, bf16[128,1024]{1,0:T(8,128)(2,1)S(1)}, u32[]{:S(2)}, u32[]{:S(2)}) collective-permute-start(bf16[128,1024]{1,0:T(8,128)(2,1)S(1)} %collective-permute-done.2.refs_8_), channel_id=1, source_target_pairs={{0,32},{2,226},{32,64},{34,2},{64,96},{66,34},{96,128},{98,66},{12... | collective-permute-start | bytes 786440 | tf_op jit(solution)/shard_map/ppermute | solution.py:38
  32.2 9.2 %collective-permute-start.9 = (bf16[128,1024]{1,0:T(8,128)(2,1)S(1)}, bf16[128,1024]{1,0:T(8,128)(2,1)S(1)}, u32[]{:S(2)}, u32[]{:S(2)}) collective-permute-start(bf16[128,1024]{1,0:T(8,128)(2,1)S(1)} %collective-permute-done.3.refs_9_), channel_id=1, source_target_pairs={{0,224},{2,34},{32,0},{34,66},{64,32},{66,98},{96,64},{98,130},{12... | collective-permute-start | bytes 786440 | tf_op jit(solution)/shard_map/ppermute | solution.py:38
  41.4 10.2 %collective-permute-start.11 = (bf16[128,1024]{1,0:T(8,128)(2,1)S(1)}, bf16[128,1024]{1,0:T(8,128)(2,1)S(1)}, u32[]{:S(2)}, u32[]{:S(2)}) collective-permute-start(bf16[128,1024]{1,0:T(8,128)(2,1)S(1)} %collective-permute-done.8.refs_10_), channel_id=1, source_target_pairs={{0,32},{2,226},{32,64},{34,2},{64,96},{66,34},{96,128},{98,66},{12... | collective-permute-start | bytes 786440 | tf_op jit(solution)/shard_map/ppermute | solution.py:38
  41.4 10.3 %collective-permute-start.12 = (bf16[128,1024]{1,0:T(8,128)(2,1)S(1)}, bf16[128,1024]{1,0:T(8,128)(2,1)}, u32[]{:S(2)}, u32[]{:S(2)}) collective-permute-start(bf16[128,1024]{1,0:T(8,128)(2,1)S(1)} %collective-permute-done.9.refs_11_), channel_id=1, source_target_pairs={{0,224},{2,34},{32,0},{34,66},{64,32},{66,98},{96,64},{98,130},{12... | collective-permute-start | bytes 786440 | tf_op jit(solution)/shard_map/ppermute | solution.py:38
  51.6 7.6 %collective-permute-start.13 = (bf16[128,1024]{1,0:T(8,128)(2,1)S(1)}, bf16[128,1024]{1,0:T(8,128)(2,1)S(1)}, u32[]{:S(2)}, u32[]{:S(2)}) collective-permute-start(bf16[128,1024]{1,0:T(8,128)(2,1)S(1)} %collective-permute-done.11.refs_12_), channel_id=1, source_target_pairs={{0,32},{2,226},{32,64},{34,2},{64,96},{66,34},{96,128},{98,66},{12... | collective-permute-start | bytes 786440 | tf_op jit(solution)/shard_map/ppermute | solution.py:38
  130.2 3.7 %collective-permute-start.14 = (f32[1024]{0:T(1024)S(1)}, f32[1024]{0:T(1024)S(1)}, u32[]{:S(2)}, u32[]{:S(2)}) collective-permute-start(f32[1024]{0:T(1024)S(1)} %log_bitcast_fusion), channel_id=1, source_target_pairs={{0,1},{1,0},{2,3},{3,2},{4,5},{5,4},{6,7},{7,6},{8,9},{9,8},{10,11... | collective-permute-start | bytes 12296 | tf_op jit(solution)/shard_map/ppermute | solution.py:31

commit v3 on v2

--- a/solution.py
+++ b/solution.py
@@ -31,11 +31,11 @@
     return lax.ppermute(value, axis, [(i, (i + by) % size) for i in range(size)])
 
 
-def wheel(value, by):
+def wheel_y(value, by):
     pairs = [
-        (i * 2 + c, (i + (by if c == 0 else -by)) % N_Z * 2 + c) for i in range(N_Z) for c in range(2)
+        (i * 2 + c, (i + (by if c == 0 else -by)) % N_Y * 2 + c) for i in range(N_Y) for c in range(2)
     ]
-    return lax.ppermute(value, ("z", "c"), pairs)
+    return lax.ppermute(value, ("y", "c"), pairs)
 
 
 def wheel_x(value, by):
@@ -62,30 +62,26 @@
     return jnp.concatenate(parts, axis=0)
 
 
-def natural(low, z, y):
-    return pl.multiple_of(low * 512 + z * (N_Y * GROUP) + y * GROUP, GROUP)
-
-
 def turned(value, size):
     return lax.rem(value + size, size)
 
 
 CONTRACT = (((0,), (0,)), ((), ()))
 TURNS = (0, -1, 1, 2)
-STEPS = (0, -1, 1, -2, 2, -3, 3)
+BAND = 2 * N_Z * GROUP
 
 
 def halves_body(tgt_ref, out_ref):
-    for y in range(N_Y):
+    for z in range(N_Z):
         for low in range(2):
-            out_ref[y * 2 + low] = tgt_ref[:, low * COLS : (low + 1) * COLS]
-
-
-def partial_body(where_ref, mask_hbm, tgt_mass_hbm, src_hbm, *refs):
-    src_refs, block_refs = refs[:7], refs[7:14]
-    scores_ref, src_last_ref, live_ref, tgt_cols_ref, side_ref = refs[14:19]
-    src_ref, tgt_ref, mask_ref, tgt_mass_ref, sems = refs[19:]
-    z, c, xh, xl = (where_ref[i] for i in range(4))
+            out_ref[z * 2 + low] = tgt_ref[:, low * COLS : (low + 1) * COLS]
+
+
+def prepare_body(where_ref, mask_hbm, tgt_mass_hbm, src_hbm, *refs):
+    src_refs, block_ref = refs[:7], refs[7]
+    scores_ref, ordered_ref, live_ref, tgt_cols_ref, side_ref = refs[8:13]
+    src_ref, mask_ref, tgt_mass_ref, sems = refs[13:]
+    y, c, xh, xl = (where_ref[i] for i in range(4))
 
     def src_at(core, turn):
         x = turned(xh * 2 + xl + turn * (1 - 2 * core), N_X)
@@ -102,22 +98,15 @@
     for index, part in enumerate(src_refs):
         core, turn = (c, index + 1) if index < 3 else (1 - c, index - 3)
         src_at(core, TURNS[turn])[...] = part[...]
-    for block, step in zip(block_refs, STEPS, strict=True):
-        plane = turned(z + step * (1 - 2 * c), N_Z)
-        for place in range(4):
-            for low in range(2):
-                to = natural(low, plane, place)
-                start = (place * 2 + low) * GROUP
-                tgt_ref[pl.ds(to, GROUP), :] = block[start : start + GROUP, :]
-    plane = turned(z + 4, N_Z)
-    for low in range(2):
-        tgt_ref[pl.ds(natural(low, plane, 0), N_Y * GROUP), :] = jnp.zeros((N_Y * GROUP, COLS), jnp.bfloat16)
     for fetch in fetches:
         fetch.wait()
-    for place in range(4):
-        for low in range(2):
-            start = (place * 2 + low) * GROUP
-            src_last_ref[start : start + GROUP, :] = src_ref[pl.ds(natural(low, plane, place), GROUP), :]
+    for band, turn in enumerate(TURNS):
+        at_y = turned(y + turn * (1 - 2 * c), N_Y)
+        for z in range(N_Z):
+            for low in range(2):
+                to = band * BAND + (z * 2 + low) * GROUP
+                at = pl.multiple_of(low * 512 + z * (N_Y * GROUP) + at_y * GROUP, GROUP)
+                ordered_ref[to : to + GROUP, :] = src_ref[pl.ds(at, GROUP), :]
     tgt_cols_ref[...] = jnp.where(xl == 0, tgt_mass_ref[:CHUNKS, :], tgt_mass_ref[CHUNKS:, :])
     side_ref[...] = jnp.full(side_ref.shape, xl.astype(F32))
     for i in range(ROWS // TILE):
@@ -126,23 +115,37 @@
             cols = slice(j * TILE, (j + 1) * TILE)
             live = mask_ref[i, xl * (COLS // TILE) + j] > 0
             live_ref[i, j] = jnp.full((8, LANES), live.astype(F32))
-
-            @pl.when(live)
-            def _():
-                scores_ref[rows, cols] = lax.dot_general(
-                    src_ref[:, rows], tgt_ref[:, cols], CONTRACT, preferred_element_type=F32
-                )
-
-
-def build_body(src_last_ref, scores_ref, live_ref, mass_ref, block_ref, kernel_ref, sums_ref, folded_ref):
+            scores_ref[rows, cols] = band_scores(ordered_ref, 0, block_ref, rows, cols)
+
+
+def band_scores(ordered_ref, band, block_ref, rows, cols):
+    return lax.dot_general(
+        ordered_ref[band * BAND : (band + 1) * BAND, rows],
+        block_ref[:, cols],
+        CONTRACT,
+        preferred_element_type=F32,
+    )
+
+
+def partial_body(ordered_ref, scores_ref, near_ref, away_ref, out_ref):
+    for i in range(ROWS // TILE):
+        rows = slice(i * TILE, (i + 1) * TILE)
+        for j in range(COLS // TILE):
+            cols = slice(j * TILE, (j + 1) * TILE)
+            out_ref[rows, cols] = (
+                scores_ref[rows, cols]
+                + band_scores(ordered_ref, 1, near_ref, rows, cols)
+                + band_scores(ordered_ref, 2, away_ref, rows, cols)
+            )
+
+
+def build_body(ordered_ref, scores_ref, live_ref, mass_ref, far_ref, kernel_ref, sums_ref, folded_ref):
     for i in range(ROWS // TILE):
         rows = slice(i * TILE, (i + 1) * TILE)
         folded = jnp.zeros((TILE, LANES), F32)
         for j in range(COLS // TILE):
             cols = slice(j * TILE, (j + 1) * TILE)
-            scores = scores_ref[rows, cols] + lax.dot_general(
-                src_last_ref[:, rows], block_ref[:, cols], CONTRACT, preferred_element_type=F32
-            )
+            scores = scores_ref[rows, cols] + band_scores(ordered_ref, 3, far_ref, rows, cols)
             live = live_ref[i, j][:1, :1] > 0.0
             part = jnp.where(live, jnp.exp(scores * SHARPNESS), 0.0)
             kernel_ref[rows, cols] = part
@@ -205,55 +208,58 @@
 SWEEP = pltpu.CompilerParams(vmem_limit_bytes=16 * 1024 * 1024)
 
 
+def work(bands):
+    return pl.CostEstimate(
+        flops=2 * ROWS * COLS * BAND * bands, bytes_accessed=8_000_000, transcendentals=0
+    )
+
+
 def shards(src_emb, tgt_emb, tile_mask, src_mass, tgt_mass):
+    src = src_emb[0]
+    src_a = [wheel_x(src, 1), wheel_x(src, -1), wheel_x(src, 2)]
     sent = pl.pallas_call(
         halves_body,
-        out_shape=jax.ShapeDtypeStruct((2 * N_Y, GROUP, COLS), jnp.bfloat16),
+        out_shape=jax.ShapeDtypeStruct((2 * N_Z, GROUP, COLS), jnp.bfloat16),
         in_specs=[VMEM],
         out_specs=VMEM,
         compiler_params=SWEEP,
     )(tgt_emb[0])
-    plane = lax.all_to_all(sent, ("y", "xl"), 0, 0, tiled=True).reshape(2 * N_Y * GROUP, COLS)
-    src = src_emb[0]
-    plane, one, two = lax.optimization_barrier((plane, wheel_x(src, 1), wheel_x(src, -1)))
-    three = wheel_x(one, 1)
-    swapped = [shift(s, "c", 2, 1) for s in (src, one, two)]
-    blocks = [plane]
-    near = away = plane
-    for step in range(3):
-        near, away = wheel(near, 1), wheel(away, -1)
-        if step == 0:
-            near, away, three, *swapped = lax.optimization_barrier((near, away, three, *swapped))
-            swapped.append(shift(three, "c", 2, 1))
-        if step == 1:
-            near, away, swapped[3] = lax.optimization_barrier((near, away, swapped[3]))
-        blocks += [near, away]
-    far = wheel(near, 1)
-
-    where = jnp.stack([lax.axis_index(a) for a in ("z", "c", "xh", "xl")]).astype(jnp.int32)
-    scores, src_last, live, tgt_cols, side = pl.pallas_call(
-        partial_body,
+    own_band = lax.all_to_all(sent, ("z", "xl"), 0, 0, tiled=True).reshape(BAND, COLS)
+    swapped = [shift(s, "c", 2, 1) for s in (src, *src_a)]
+    near, away = wheel_y(own_band, 1), wheel_y(own_band, -1)
+    near, *swapped = lax.optimization_barrier((near, *swapped))
+    far = wheel_y(near, 1)
+
+    where = jnp.stack([lax.axis_index(a) for a in ("y", "c", "xh", "xl")]).astype(jnp.int32)
+    scores, ordered, live, tgt_cols, side = pl.pallas_call(
+        prepare_body,
         out_shape=(
             KERNEL,
-            pltpu.VMEM((LANES, ROWS), jnp.bfloat16),
+            pltpu.VMEM((VECTOR_DIMENSION, ROWS), jnp.bfloat16),
             pltpu.VMEM((ROWS // TILE, COLS // TILE, 8, LANES), F32),
             SMALL,
             HALF,
         ),
-        in_specs=[SMEM] + [HBM] * 3 + [VMEM] * (7 + len(blocks)),
+        in_specs=[SMEM] + [HBM] * 3 + [VMEM] * 8,
         out_specs=(VMEM,) * 5,
         scratch_shapes=[
             pltpu.VMEM((VECTOR_DIMENSION, ROWS), jnp.bfloat16),
-            pltpu.VMEM((VECTOR_DIMENSION, COLS), jnp.bfloat16),
             pltpu.SMEM(tile_mask.shape, jnp.int32),
             pltpu.VMEM((2 * CHUNKS, LANES), F32),
             pltpu.SemaphoreType.DMA((3,)),
         ],
         compiler_params=BUILD,
-        cost_estimate=pl.CostEstimate(
-            flops=2 * ROWS * COLS * VECTOR_DIMENSION, bytes_accessed=10_000_000, transcendentals=0
-        ),
-    )(where, *map(in_hbm, (tile_mask, tgt_mass.reshape(-1, LANES), src)), one, two, three, *swapped, *blocks)
+        cost_estimate=work(1),
+    )(where, *map(in_hbm, (tile_mask, tgt_mass.reshape(-1, LANES), src)), *src_a, *swapped, own_band)
+    ordered = in_vmem(ordered)
+    scores = pl.pallas_call(
+        partial_body,
+        out_shape=KERNEL,
+        in_specs=[VMEM] * 4,
+        out_specs=VMEM,
+        compiler_params=BUILD,
+        cost_estimate=work(2),
+    )(ordered, in_vmem(scores), near, away)
     own = src_mass.reshape(-1, LANES)
     kernel, sums = pl.pallas_call(
         build_body,
@@ -262,7 +268,8 @@
         out_specs=(VMEM, VMEM),
         scratch_shapes=[pltpu.VMEM((ROWS, LANES), F32)],
         compiler_params=BUILD,
-    )(in_vmem(src_last), in_vmem(scores), in_vmem(live), own, far)
+        cost_estimate=work(1),
+    )(ordered, in_vmem(scores), in_vmem(live), own, far)
 
     kernel = in_vmem(kernel)
     for sweep in range(ITERS):

time: 136 us -> 128 us (0.941)
  blocking collectives: 79.8 us -> 67.6 us
  local copies, waits for them, and re-layouts: 0.85 us -> 4.13 us
  starting transfers between devices: 17.8 us -> 19.4 us
    ppermute x7 -> x3, waiting for transfers between devices: 24.2 us -> 9.59 us  [wheel_y(): return lax.ppermute(value, ('y', 'c'), pairs)]
    all_to_all x1 -> x0, blocking collectives: 12.5 us -> none  [shards(): lax.all_to_all(sent, ('y', 'xl'), 0, 0, tiled=True)]
    all_to_all x0 -> x1, waiting for transfers between devices: none -> 11.9 us  [shards(): lax.all_to_all(sent, ('z', 'xl'), 0, 0, tiled=True).reshape(BAND, COLS)]
    all_to_all x0 -> x1, starting transfers between devices: none -> 9.94 us  [shards(): lax.all_to_all(sent, ('z', 'xl'), 0, 0, tiled=True).reshape(BAND, COLS)]
    ppermute x7 -> x3, starting transfers between devices: 12.3 us -> 4.66 us  [wheel_y(): return lax.ppermute(value, ('y', 'c'), pairs)]
    unnamed x4 -> x12, local copies, waits for them, and re-layouts: 0.85 us -> 4.13 us
    pallas_call x2 -> x3, Pallas kernels: 3.8 us -> 4.57 us  [the longest x1 2.42 us: shards(): pl.pallas_call(prepare_body, out_shape=(KERNEL, pltpu.VMEM((VECTOR_DIMENS...]
  transfers between devices with their start and end apart: 15 -> 12, of which waited for: 6 -> 6; matrix products, arithmetic and copies ran while one was open for 0% -> 0% of each run, Pallas kernels for 3% -> 3%
where the time goes in v3:
time: 128 us; the launch traced here: 127 us
  blocking collectives  67.6 us (53%)
  waiting for transfers between devices  25.9 us (20%)
  starting transfers between devices  19.4 us (15%)
  Pallas kernels  8.39 us (7%)
  local copies, waits for them, and re-layouts  4.13 us (3%)
    all_to_all x3, blocking collectives, shards(): parts = lax.all_to_all(outs[-1], PLANE, 0, 0, tiled=True)  42.6 us
    all_to_all x3, blocking collectives, shards(): parts = lax.all_to_all(sums, ('xh', 'c', 'xl'), 0, 0, tiled=True)  25 us
    all_to_all x1, waiting for transfers between devices, shards(): lax.all_to_all(sent, ('z', 'xl'), 0, 0, tiled=True).reshape(BAND, COLS)  11.9 us
    all_to_all x1, starting transfers between devices, shards(): lax.all_to_all(sent, ('z', 'xl'), 0, 0, tiled=True).reshape(BAND, COLS)  9.94 us
    ppermute x3, waiting for transfers between devices, wheel_y(): return lax.ppermute(value, ('y', 'c'), pairs)  9.59 us
    ppermute x3, starting transfers between devices, wheel_y(): return lax.ppermute(value, ('y', 'c'), pairs)  4.66 us
    unnamed x12, local copies, waits for them, and re-layouts  4.13 us
    ppermute x3, starting transfers between devices, wheel_x(): return lax.ppermute(value, ('xh', 'c', 'xl'), pairs)  3.43 us
  transfers between devices with their start and end apart: 12, of which 6 were waited for; matrix products, arithmetic and copies ran while one was open for 0% of the time, Pallas kernels for 3%

profile of v3, /device:TPU:6, one launch (start us, length us, event | category | flops | bytes accessed | tf_op | source)
XLA Modules:
  0.0 126.8 jit_solution(3708234443331172554)
XLA Ops:
  0.6 0.8 copy-done.4
  1.5 0.8 shard_map.68
  2.3 9.9 %all-to-all-start = ((bf16[16,16,1024]{2,1,0:T(8,128)(2,1)}), bf16[16,16,1024]{2,1,0:T(8,128)(2,1)S(1)}, u32[]{:S(2)}, u32[]{:S(2)}) async-start(bf16[16,16,1024]{2,1,0:T(8,128)(2,1)} %shard_map.68), calls=%async_computation | async-start | bytes 1048576 | tf_op jit(solution)/shard_map/all_to_all | solution.py:227
  12.4 1.9 %collective-permute-start.1 = (bf16[128,1024]{1,0:T(8,128)(2,1)}, bf16[128,1024]{1,0:T(8,128)(2,1)S(1)}, u32[]{:S(2)}, u32[]{:S(2)}) collective-permute-start(bf16[128,1024]{1,0:T(8,128)(2,1)} %bitcast.18), channel_id=1, source_target_pairs={{0,5},{2,3},{1,0},{3,6},{4,1},{6,7},{5,4},{7,2},{8,13},{10,11},{9,... | collective-permute-start | bytes 786440 | tf_op jit(solution)/shard_map/ppermute | solution.py:46
  14.3 1.4 %collective-permute-start.2 = (bf16[128,1024]{1,0:T(8,128)(2,1)}, bf16[128,1024]{1,0:T(8,128)(2,1)S(1)}, u32[]{:S(2)}, u32[]{:S(2)}) collective-permute-start(bf16[128,1024]{1,0:T(8,128)(2,1)} %bitcast.19), channel_id=1, source_target_pairs={{0,4},{2,6},{1,5},{3,7},{4,0},{6,2},{5,1},{7,3},{8,12},{10,14},{9,... | collective-permute-start | bytes 786440 | tf_op jit(solution)/shard_map/ppermute | solution.py:46
  15.7 11.9 %all-to-all-done = bf16[16,16,1024]{2,1,0:T(8,128)(2,1)S(1)} async-done(((bf16[16,16,1024]{2,1,0:T(8,128)(2,1)}), bf16[16,16,1024]{2,1,0:T(8,128)(2,1)S(1)}, u32[]{:S(2)}, u32[]{:S(2)}) %all-to-all-start) | async-done | bytes 524320 | tf_op jit(solution)/shard_map/all_to_all | solution.py:227
  27.6 1.6 %collective-permute-start.3 = (bf16[256,1024]{1,0:T(8,128)(2,1)S(1)}, bf16[256,1024]{1,0:T(8,128)(2,1)S(1)}, u32[]{:S(2)}, u32[]{:S(2)}) collective-permute-start(bf16[256,1024]{1,0:T(8,128)(2,1)S(1)} %bitcast.12), channel_id=1, source_target_pairs={{0,8},{2,26},{8,16},{10,2},{16,24},{18,10},{24,0},{26,18},{1,9},{3... | collective-permute-start | bytes 1572872 | tf_op jit(solution)/shard_map/ppermute | solution.py:38
  29.1 0.5 collective-permute-start.5
  29.8 1.1 collective-permute-done.2.refs_2_
  31.2 2.7 %collective-permute-start.8 = (bf16[256,1024]{1,0:T(8,128)(2,1)S(1)}, bf16[256,1024]{1,0:T(8,128)(2,1)S(1)}, u32[]{:S(2)}, u32[]{:S(2)}) collective-permute-start(bf16[256,1024]{1,0:T(8,128)(2,1)S(1)} %bitcast.13), channel_id=1, source_target_pairs={{0,24},{2,10},{8,0},{10,18},{16,8},{18,26},{24,16},{26,2},{1,25},{... | collective-permute-start | bytes 1572872 | tf_op jit(solution)/shard_map/ppermute | solution.py:38
  33.9 0.7 copy-done
  34.6 0.7 copy-done.2
  35.3 5.4 %collective-permute-done.3.near_ref = bf16[256,1024]{1,0:T(8,128)(2,1)S(1)} collective-permute-done((bf16[256,1024]{1,0:T(8,128)(2,1)S(1)}, bf16[256,1024]{1,0:T(8,128)(2,1)S(1)}, u32[]{:S(2)}, u32[]{:S(2)}) %collective-permute-start.3) | collective-permute-done | bytes 524320 | tf_op jit(solution)/shard_map/ppermute | solution.py:38
  40.6 0.4 collective-permute-start.9
  41.1 0.9 copy-done.1
  42.1 0.9 copy-done.3
  43.0 2.4 %shard_map.69 = (f32[1024,1024]{1,0:T(8,128)S(1)}, bf16[1024,1024]{1,0:T(8,128)(2,1)S(1)}, f32[2,2,8,128]{3,2,1,0:T(8,128)S(1)}, f32[8,128]{1,0:T(8,128)S(1)}, f32[4,128]{1,0:T(4,128)S(1)}) custom-call(s32[4]{0:T(128)S(1)} %pad_add_fusion.where_ref, s32[2,4]{1,0:T(2,128)} %mask_hbm.1, f32[16,128]{1,0:T(8,128)} %bitcast.22, bf16[128,1024]{1,0:T(8,128)(2,1)} %bitcast.21, ...), custom_call_target="tpu_custom_call" | custom-call | flops 536870912 | bytes 8000000 | tf_op jit(solution)/shard_map/pallas_call | solution.py:234
  45.5 1.3 %shard_map.70.scores_ref = f32[1024,1024]{1,0:T(8,128)S(1)} custom-call(bf16[1024,1024]{1,0:T(8,128)(2,1)S(1)} %get-tuple-element.22.ordered_ref, f32[1024,1024]{1,0:T(8,128)S(1)} %get-tuple-element.23.scores_ref, bf16[256,1024]{1,0:T(8,128)(2,1)S(1)} %collective-permute-done.3.near_ref, bf16[256,1024]{1,0:T(8,128)(2,1)S(1)} %collective-permute-done.8.away_ref), custom_call_target="tpu_custom_call" | custom-call | flops 1073741824 | bytes 8000000 | tf_op jit(solution)/shard_map/pallas_call | solution.py:255
  46.8 4.2 %collective-permute-done.9.far_ref = bf16[256,1024]{1,0:T(8,128)(2,1)S(1)} collective-permute-done((bf16[256,1024]{1,0:T(8,128)(2,1)S(1)}, bf16[256,1024]{1,0:T(8,128)(2,1)S(1)}, u32[]{:S(2)}, u32[]{:S(2)}) %collective-permute-start.9) | collective-permute-done | bytes 524320 | tf_op jit(solution)/shard_map/ppermute | solution.py:38
  51.0 1.4 %shard_map.71 = (f32[1024,1024]{1,0:T(8,128)S(1)}, f32[8,16,128]{2,1,0:T(8,128)S(1)}) custom-call(bf16[1024,1024]{1,0:T(8,128)(2,1)S(1)} %get-tuple-element.22.ordered_ref, f32[1024,1024]{1,0:T(8,128)S(1)} %shard_map.70.scores_ref, f32[2,2,8,128]{3,2,1,0:T(8,128)S(1)} %get-tuple-element.25.live_ref, f32[4,128]{1,0:T(4,128)S(1)} %bitcast.16, ...), custom_call_target="tpu_custom_call" | custom-call | flops 536870912 | bytes 8000000 | tf_op jit(solution)/shard_map/pallas_call | solution.py:264
  52.4 9.3 %all_to_all.35.parts_ref = f32[8,16,128]{2,1,0:T(8,128)S(1)} all-to-all(f32[8,16,128]{2,1,0:T(8,128)S(1)} %get-tuple-element.28), channel_id=1, replica_groups=mesh['z'=8,'y'=4,'xh'=2,'c'=2,'xl'=2] {'xh','c','xl'}, dimensions={0} | all-to-all | bytes 131072 | tf_op jit(solution)/shard_map/all_to_all | solution.py:276
  62.1 15.1 %all_to_all.36.parts_ref = f32[32,8,128]{2,1,0:T(8,128)S(1)} all-to-all(f32[32,8,128]{2,1,0:T(8,128)S(1)} %get-tuple-element.29), channel_id=1, replica_groups=mesh['z'=8,'y'=4,'xh'=2,'c'=2,'xl'=2] {'z','y'}, dimensions={0} | all-to-all | bytes 262144 | tf_op jit(solution)/shard_map/all_to_all | solution.py:292
  77.1 0.4 shard_map.73
  77.5 7.8 %all_to_all.37.parts_ref = f32[8,8,128]{2,1,0:T(8,128)S(1)} all-to-all(f32[8,8,128]{2,1,0:T(8,128)S(1)} %shard_map.73), channel_id=1, replica_groups=mesh['z'=8,'y'=4,'xh'=2,'c'=2,'xl'=2] {'xh','c','xl'}, dimensions={0} | all-to-all | bytes 65536 | tf_op jit(solution)/shard_map/all_to_all | solution.py:276
  85.7 13.7 %all_to_all.38.parts_ref = f32[32,8,128]{2,1,0:T(8,128)S(1)} all-to-all(f32[32,8,128]{2,1,0:T(8,128)S(1)} %shard_map.74), channel_id=1, replica_groups=mesh['z'=8,'y'=4,'xh'=2,'c'=2,'xl'=2] {'z','y'}, dimensions={0} | all-to-all | bytes 262144 | tf_op jit(solution)/shard_map/all_to_all | solution.py:292
  99.5 0.4 shard_map.75
  99.9 7.8 %all_to_all.39.parts_ref = f32[8,8,128]{2,1,0:T(8,128)S(1)} all-to-all(f32[8,8,128]{2,1,0:T(8,128)S(1)} %shard_map.75), channel_id=1, replica_groups=mesh['z'=8,'y'=4,'xh'=2,'c'=2,'xl'=2] {'xh','c','xl'}, dimensions={0} | all-to-all | bytes 65536 | tf_op jit(solution)/shard_map/all_to_all | solution.py:276
  107.7 1.0 shard_map.76
  108.6 13.8 %all_to_all.40 = f32[32,8,128]{2,1,0:T(8,128)S(1)} all-to-all(f32[32,8,128]{2,1,0:T(8,128)S(1)} %get-tuple-element.33), channel_id=1, replica_groups=mesh['z'=8,'y'=4,'xh'=2,'c'=2,'xl'=2] {'z','y'}, dimensions={0} | all-to-all | bytes 262144 | tf_op jit(solution)/shard_map/all_to_all | solution.py:292
  122.5 0.7 collective-permute-start.10
  123.2 2.9 %collective-permute-done.10 = f32[1024]{0:T(1024)S(1)} collective-permute-done((f32[1024]{0:T(1024)S(1)}, f32[1024]{0:T(1024)S(1)}, u32[]{:S(2)}, u32[]{:S(2)}) %collective-permute-start.10) | collective-permute-done | bytes 4128 | tf_op jit(solution)/shard_map/ppermute | solution.py:31
  126.2 0.6 maximum_select_fusion
  (23 shorter events, 1.5 us)
Async XLA Ops:
  0.6 0.8 copy-start.4
  2.3 25.3 %all-to-all-start = ((bf16[16,16,1024]{2,1,0:T(8,128)(2,1)}), bf16[16,16,1024]{2,1,0:T(8,128)(2,1)S(1)}, u32[]{:S(2)}, u32[]{:S(2)}) async-start(bf16[16,16,1024]{2,1,0:T(8,128)(2,1)} %shard_map.68), calls=%async_computation | async-start | bytes 1048576 | tf_op jit(solution)/shard_map/all_to_all | solution.py:227
  12.2 16.9 %collective-permute-start = (bf16[128,1024]{1,0:T(8,128)(2,1)}, bf16[128,1024]{1,0:T(8,128)(2,1)S(1)}, u32[]{:S(2)}, u32[]{:S(2)}) collective-permute-start(bf16[128,1024]{1,0:T(8,128)(2,1)} %bitcast.17), channel_id=1, source_target_pairs={{0,1},{2,7},{1,4},{3,2},{4,5},{6,3},{5,0},{7,6},{8,9},{10,15},{9,1... | collective-permute-start | bytes 786440 | tf_op jit(solution)/shard_map/ppermute | solution.py:46
  12.4 17.3 %collective-permute-start.1 = (bf16[128,1024]{1,0:T(8,128)(2,1)}, bf16[128,1024]{1,0:T(8,128)(2,1)S(1)}, u32[]{:S(2)}, u32[]{:S(2)}) collective-permute-start(bf16[128,1024]{1,0:T(8,128)(2,1)} %bitcast.18), channel_id=1, source_target_pairs={{0,5},{2,3},{1,0},{3,6},{4,1},{6,7},{5,4},{7,2},{8,13},{10,11},{9,... | collective-permute-start | bytes 786440 | tf_op jit(solution)/shard_map/ppermute | solution.py:46
  14.3 16.6 %collective-permute-start.2 = (bf16[128,1024]{1,0:T(8,128)(2,1)}, bf16[128,1024]{1,0:T(8,128)(2,1)S(1)}, u32[]{:S(2)}, u32[]{:S(2)}) collective-permute-start(bf16[128,1024]{1,0:T(8,128)(2,1)} %bitcast.19), channel_id=1, source_target_pairs={{0,4},{2,6},{1,5},{3,7},{4,0},{6,2},{5,1},{7,3},{8,12},{10,14},{9,... | collective-permute-start | bytes 786440 | tf_op jit(solution)/shard_map/ppermute | solution.py:46
  27.6 13.1 %collective-permute-start.3 = (bf16[256,1024]{1,0:T(8,128)(2,1)S(1)}, bf16[256,1024]{1,0:T(8,128)(2,1)S(1)}, u32[]{:S(2)}, u32[]{:S(2)}) collective-permute-start(bf16[256,1024]{1,0:T(8,128)(2,1)S(1)} %bitcast.12), channel_id=1, source_target_pairs={{0,8},{2,26},{8,16},{10,2},{16,24},{18,10},{24,0},{26,18},{1,9},{3... | collective-permute-start | bytes 1572872 | tf_op jit(solution)/shard_map/ppermute | solution.py:38
  29.1 2.0 %collective-permute-start.4 = (bf16[128,1024]{1,0:T(8,128)(2,1)}, bf16[128,1024]{1,0:T(8,128)(2,1)S(1)}, u32[]{:S(2)}, u32[]{:S(2)}) collective-permute-start(bf16[128,1024]{1,0:T(8,128)(2,1)} %bitcast.20), channel_id=1, source_target_pairs={{0,2},{2,0},{1,3},{3,1},{4,6},{6,4},{5,7},{7,5},{8,10},{10,8},{9,1... | collective-permute-start | bytes 786440 | tf_op jit(solution)/shard_map/ppermute | solution.py:31
  29.1 4.7 %collective-permute-start.5 = (bf16[128,1024]{1,0:T(8,128)(2,1)S(1)}, bf16[128,1024]{1,0:T(8,128)(2,1)S(1)}, u32[]{:S(2)}, u32[]{:S(2)}) collective-permute-start(bf16[128,1024]{1,0:T(8,128)(2,1)S(1)} %collective-permute-done.refs_0_), channel_id=1, source_target_pairs={{0,2},{2,0},{1,3},{3,1},{4,6},{6,4},{5,7},{7,5},{8,10},{10,8},{9,1... | collective-permute-start | bytes 786440 | tf_op jit(solution)/shard_map/ppermute | solution.py:31
  29.7 4.2 %collective-permute-start.6 = (bf16[128,1024]{1,0:T(8,128)(2,1)S(1)}, bf16[128,1024]{1,0:T(8,128)(2,1)S(1)}, u32[]{:S(2)}, u32[]{:S(2)}) collective-permute-start(bf16[128,1024]{1,0:T(8,128)(2,1)S(1)} %collective-permute-done.1.refs_1_), channel_id=1, source_target_pairs={{0,2},{2,0},{1,3},{3,1},{4,6},{6,4},{5,7},{7,5},{8,10},{10,8},{9,1... | collective-permute-start | bytes 786440 | tf_op jit(solution)/shard_map/ppermute | solution.py:31
  30.8 3.7 %collective-permute-start.7 = (bf16[128,1024]{1,0:T(8,128)(2,1)S(1)}, bf16[128,1024]{1,0:T(8,128)(2,1)S(1)}, u32[]{:S(2)}, u32[]{:S(2)}) collective-permute-start(bf16[128,1024]{1,0:T(8,128)(2,1)S(1)} %collective-permute-done.2.refs_2_), channel_id=1, source_target_pairs={{0,2},{2,0},{1,3},{3,1},{4,6},{6,4},{5,7},{7,5},{8,10},{10,8},{9,1... | collective-permute-start | bytes 786440 | tf_op jit(solution)/shard_map/ppermute | solution.py:31
  31.2 14.3 %collective-permute-start.8 = (bf16[256,1024]{1,0:T(8,128)(2,1)S(1)}, bf16[256,1024]{1,0:T(8,128)(2,1)S(1)}, u32[]{:S(2)}, u32[]{:S(2)}) collective-permute-start(bf16[256,1024]{1,0:T(8,128)(2,1)S(1)} %bitcast.13), channel_id=1, source_target_pairs={{0,24},{2,10},{8,0},{10,18},{16,8},{18,26},{24,16},{26,2},{1,25},{... | collective-permute-start | bytes 1572872 | tf_op jit(solution)/shard_map/ppermute | solution.py:38
  33.9 0.7 copy-start
  34.6 0.7 copy-start.2
  40.6 10.4 %collective-permute-start.9 = (bf16[256,1024]{1,0:T(8,128)(2,1)S(1)}, bf16[256,1024]{1,0:T(8,128)(2,1)S(1)}, u32[]{:S(2)}, u32[]{:S(2)}) collective-permute-start(bf16[256,1024]{1,0:T(8,128)(2,1)S(1)} %collective-permute-done.3.near_ref), channel_id=1, source_target_pairs={{0,8},{2,26},{8,16},{10,2},{16,24},{18,10},{24,0},{26,18},{1,9},{3... | collective-permute-start | bytes 1572872 | tf_op jit(solution)/shard_map/ppermute | solution.py:38
  41.1 1.0 copy-start.1
  42.1 0.9 copy-start.3
  45.5 5.6 %copy-start.5 = (f32[512]{0:T(512)S(1)}, f32[512]{0:T(512)}, u32[]{:S(2)}) copy-start(f32[512]{0:T(512)} %param.8) | copy-start | bytes 6148
  122.5 3.7 %collective-permute-start.10 = (f32[1024]{0:T(1024)S(1)}, f32[1024]{0:T(1024)S(1)}, u32[]{:S(2)}, u32[]{:S(2)}) collective-permute-start(f32[1024]{0:T(1024)S(1)} %log_bitcast_fusion), channel_id=1, source_target_pairs={{0,1},{1,0},{2,3},{3,2},{4,5},{5,4},{6,7},{7,6},{8,9},{9,8},{10,11... | collective-permute-start | bytes 12296 | tf_op jit(solution)/shard_map/ppermute | solution.py:31

commit v4 on v3

--- a/solution.py
+++ b/solution.py
@@ -44,6 +44,12 @@
         (place(i, c), place((i + (by if c == 0 else -by)) % N_X, c)) for i in range(N_X) for c in range(2)
     ]
     return lax.ppermute(value, ("xh", "c", "xl"), pairs)
+
+
+def ring_parts(sums):
+    chip = sums + shift(sums, "c", 2, 1)
+    one, far = wheel_x(chip, 1), shift(chip, X, N_X, 2)
+    return [chip, one, far, shift(one, "c", 2, 1)]
 
 
 def in_vmem(value):
@@ -127,7 +133,18 @@
     )
 
 
-def partial_body(ordered_ref, scores_ref, near_ref, away_ref, out_ref):
+def split_body(band_ref, first_ref, second_ref):
+    first_ref[...] = band_ref[: BAND // 2, :]
+    second_ref[...] = band_ref[BAND // 2 :, :]
+
+
+def joined(ref, halves):
+    for k, half in enumerate(halves):
+        ref[k * BAND // 2 : (k + 1) * BAND // 2, :] = half[...]
+
+
+def partial_body(ordered_ref, scores_ref, near_0_ref, near_1_ref, away_ref, out_ref, near_ref):
+    joined(near_ref, (near_0_ref, near_1_ref))
     for i in range(ROWS // TILE):
         rows = slice(i * TILE, (i + 1) * TILE)
         for j in range(COLS // TILE):
@@ -139,7 +156,10 @@
             )
 
 
-def build_body(ordered_ref, scores_ref, live_ref, mass_ref, far_ref, kernel_ref, sums_ref, folded_ref):
+def build_body(
+    ordered_ref, scores_ref, live_ref, mass_ref, far_0_ref, far_1_ref, kernel_ref, sums_ref, folded_ref, far_ref
+):
+    joined(far_ref, (far_0_ref, far_1_ref))
     for i in range(ROWS // TILE):
         rows = slice(i * TILE, (i + 1) * TILE)
         folded = jnp.zeros((TILE, LANES), F32)
@@ -164,12 +184,15 @@
     column_sums(kernel_ref, mass / jnp.sum(parts_ref[:, :CHUNKS, :], axis=0), out_ref)
 
 
-def columns_body(kernel_ref, parts_ref, mass_ref, out_ref):
-    column_sums(kernel_ref, mass_ref[...] / jnp.sum(parts_ref[...], axis=0), out_ref)
-
-
-def last_columns_body(kernel_ref, parts_ref, mass_ref, side_ref, log_ref, out_ref):
-    scale = mass_ref[...] / jnp.sum(parts_ref[...], axis=0)
+def columns_body(kernel_ref, mass_ref, *refs):
+    part_refs, out_ref = refs[:4], refs[4]
+    total = sum(part[...] for part in part_refs)
+    column_sums(kernel_ref, mass_ref[...] / total, out_ref)
+
+
+def last_columns_body(kernel_ref, mass_ref, side_ref, *refs):
+    part_refs, (log_ref, out_ref) = refs[:4], refs[4:]
+    scale = mass_ref[...] / sum(part[...] for part in part_refs)
     log_ref[...] = jnp.log(
         jnp.where(side_ref[...] == 0.0, scale[: CHUNKS // 2], scale[CHUNKS // 2 :])
     )
@@ -196,7 +219,7 @@
         for j in range(1, COLS // LANES):
             total = total + kernel_ref[rows, j * LANES : (j + 1) * LANES] * scale[j : j + 1, :]
         folded_ref[rows, :] = total
-    sums_ref[...] = jnp.broadcast_to(lane_sums(folded_ref[...])[None], sums_ref.shape)
+    sums_ref[...] = lane_sums(folded_ref[...])
 
 
 HALF = jax.ShapeDtypeStruct((CHUNKS // 2, LANES), F32)
@@ -204,6 +227,7 @@
 WIDE = pltpu.VMEM((N_Z * N_Y, CHUNKS, LANES), F32)
 RING = (2 * N_X, CHUNKS, LANES)
 KERNEL = pltpu.VMEM((ROWS, COLS), F32)
+HALF_BAND = pltpu.VMEM((N_Z * GROUP, COLS), jnp.bfloat16)
 BUILD = pltpu.CompilerParams(vmem_limit_bytes=28 * 1024 * 1024)
 SWEEP = pltpu.CompilerParams(vmem_limit_bytes=16 * 1024 * 1024)
 
@@ -225,10 +249,19 @@
         compiler_params=SWEEP,
     )(tgt_emb[0])
     own_band = lax.all_to_all(sent, ("z", "xl"), 0, 0, tiled=True).reshape(BAND, COLS)
-    swapped = [shift(s, "c", 2, 1) for s in (src, *src_a)]
-    near, away = wheel_y(own_band, 1), wheel_y(own_band, -1)
-    near, *swapped = lax.optimization_barrier((near, *swapped))
-    far = wheel_y(near, 1)
+    split_band = pl.pallas_call(
+        split_body,
+        out_shape=(HALF_BAND, HALF_BAND),
+        in_specs=[VMEM],
+        out_specs=(VMEM, VMEM),
+        compiler_params=SWEEP,
+    )(own_band)
+    swapped = [shift(s, "c", 2, 1) for s in (src, *src_a[:2])]
+    near = [wheel_y(v, 1) for v in split_band]
+    away = wheel_y(own_band, -1)
+    late, _ = lax.optimization_barrier((src_a[2], near[0]))
+    swapped.append(shift(late, "c", 2, 1))
+    far = [wheel_y(v, 1) for v in near]
 
     where = jnp.stack([lax.axis_index(a) for a in ("y", "c", "xh", "xl")]).astype(jnp.int32)
     scores, ordered, live, tgt_cols, side = pl.pallas_call(
@@ -255,25 +288,29 @@
     scores = pl.pallas_call(
         partial_body,
         out_shape=KERNEL,
-        in_specs=[VMEM] * 4,
+        in_specs=[VMEM] * 5,
         out_specs=VMEM,
+        scratch_shapes=[pltpu.VMEM((BAND, COLS), jnp.bfloat16)],
         compiler_params=BUILD,
         cost_estimate=work(2),
-    )(ordered, in_vmem(scores), near, away)
+    )(ordered, in_vmem(scores), *near, away)
     own = src_mass.reshape(-1, LANES)
     kernel, sums = pl.pallas_call(
         build_body,
         out_shape=(KERNEL, pltpu.VMEM((2 * N_X, 2 * CHUNKS, LANES), F32)),
-        in_specs=[VMEM] * 5,
+        in_specs=[VMEM] * 6,
         out_specs=(VMEM, VMEM),
-        scratch_shapes=[pltpu.VMEM((ROWS, LANES), F32)],
+        scratch_shapes=[pltpu.VMEM((ROWS, LANES), F32), pltpu.VMEM((BAND, COLS), jnp.bfloat16)],
         compiler_params=BUILD,
         cost_estimate=work(1),
-    )(ordered, in_vmem(scores), in_vmem(live), own, far)
+    )(ordered, in_vmem(scores), in_vmem(live), own, *far)
 
     kernel = in_vmem(kernel)
     for sweep in range(ITERS):
-        parts = lax.all_to_all(sums, ("xh", "c", "xl"), 0, 0, tiled=True)
+        if sweep == 0:
+            parts = [lax.all_to_all(sums, ("xh", "c", "xl"), 0, 0, tiled=True)]
+        else:
+            parts = ring_parts(sums)
         if sweep == 0:
             body, operands, extra = first_columns_body, (), (SMALL,)
         elif sweep < ITERS - 1:
@@ -283,17 +320,17 @@
         outs = pl.pallas_call(
             body,
             out_shape=(*extra, WIDE),
-            in_specs=[VMEM] * (2 + len(operands)),
+            in_specs=[VMEM] * (1 + len(operands) + len(parts)),
             out_specs=(VMEM,) * (1 + len(extra)),
             compiler_params=SWEEP,
-        )(kernel, parts, *operands)
+        )(kernel, *operands, *parts)
         if sweep == 0:
             mass = outs[0]
         parts = lax.all_to_all(outs[-1], PLANE, 0, 0, tiled=True)
         if sweep < ITERS - 1:
             sums = pl.pallas_call(
                 rows_body,
-                out_shape=pltpu.VMEM(RING, F32),
+                out_shape=SMALL,
                 in_specs=[VMEM] * 3,
                 out_specs=VMEM,
                 scratch_shapes=[pltpu.VMEM((ROWS, LANES), F32)],

time: 128 us -> 127 us (level)
  blocking collectives: 67.6 us -> 51.9 us
  waiting for transfers between devices: 25.9 us -> 38 us
  starting transfers between devices: 19.4 us -> 25.5 us
  local copies, waits for them, and re-layouts: 4.13 us -> 0.84 us
    all_to_all x3 -> x1, blocking collectives: 25 us -> 9.23 us  [shards(): parts = [lax.all_to_all(sums, ('xh', 'c', 'xl'), 0, 0, tiled=True)]]
    ppermute x5 -> x11, waiting for transfers between devices: 3.32 us -> 11 us  [shift(): lax.ppermute(value, axis, [(i, (i + by) % size) for i in range(size)])]
    unnamed x12 -> x4, local copies, waits for them, and re-layouts: 4.13 us -> 0.84 us
    ppermute x3 -> x5, starting transfers between devices: 3.43 us -> 6.69 us  [wheel_x(): return lax.ppermute(value, ('xh', 'c', 'xl'), pairs)]
    ppermute x3 -> x5, waiting for transfers between devices: 9.59 us -> 12.6 us  [wheel_y(): return lax.ppermute(value, ('y', 'c'), pairs)]
    ppermute x5 -> x11, starting transfers between devices: 1.35 us -> 3.64 us  [shift(): lax.ppermute(value, axis, [(i, (i + by) % size) for i in range(size)])]
    ppermute x3 -> x5, waiting for transfers between devices: 1.08 us -> 2.45 us  [wheel_x(): return lax.ppermute(value, ('xh', 'c', 'xl'), pairs)]
    pallas_call x6 -> x7, Pallas kernels: 3.79 us -> 4.5 us  [the longest x3 1.69 us: shards(): pl.pallas_call(body, out_shape=(*extra, WIDE), in_specs=[VMEM] * (1 + len...]
  transfers between devices with their start and end apart: 12 -> 22, of which waited for: 6 -> 11; matrix products, arithmetic and copies ran while one was open for 0% -> 0% of each run, Pallas kernels for 3% -> 4%
where the time goes in v4:
time: 127 us
  blocking collectives  51.9 us (41%)
  waiting for transfers between devices  38 us (30%)
  starting transfers between devices  25.5 us (20%)
  Pallas kernels  9.08 us (7%)
    all_to_all x3, blocking collectives, shards(): parts = lax.all_to_all(outs[-1], PLANE, 0, 0, tiled=True)  42.7 us
    ppermute x5, waiting for transfers between devices, wheel_y(): return lax.ppermute(value, ('y', 'c'), pairs)  12.6 us
    all_to_all x1, waiting for transfers between devices, shards(): lax.all_to_all(sent, ('z', 'xl'), 0, 0, tiled=True).reshape(BAND, COLS)  11.9 us
    ppermute x11, waiting for transfers between devices, shift(): lax.ppermute(value, axis, [(i, (i + by) % size) for i in range(size)])  11 us
    all_to_all x1, starting transfers between devices, shards(): lax.all_to_all(sent, ('z', 'xl'), 0, 0, tiled=True).reshape(BAND, COLS)  9.94 us
    all_to_all x1, blocking collectives, shards(): parts = [lax.all_to_all(sums, ('xh', 'c', 'xl'), 0, 0, tiled=True)]  9.23 us
    ppermute x5, starting transfers between devices, wheel_x(): return lax.ppermute(value, ('xh', 'c', 'xl'), pairs)  6.69 us
    ppermute x5, starting transfers between devices, wheel_y(): return lax.ppermute(value, ('y', 'c'), pairs)  5.25 us
  transfers between devices with their start and end apart: 22, of which 11 were waited for; matrix products, arithmetic and copies ran while one was open for 0% of the time, Pallas kernels for 4%

profile of v4, /device:TPU:6, one launch (start us, length us, event | category | flops | bytes accessed | tf_op | source)
XLA Modules:
  0.0 126.8 jit_solution(6246553650091921341)
XLA Ops:
  0.6 0.8 copy-done
  1.5 0.8 shard_map.68
  2.3 9.9 %all-to-all-start = ((bf16[16,16,1024]{2,1,0:T(8,128)(2,1)}), bf16[16,16,1024]{2,1,0:T(8,128)(2,1)S(1)}, u32[]{:S(2)}, u32[]{:S(2)}) async-start(bf16[16,16,1024]{2,1,0:T(8,128)(2,1)} %shard_map.68), calls=%async_computation | async-start | bytes 1048576 | tf_op jit(solution)/shard_map/all_to_all | solution.py:251
  12.3 1.4 %collective-permute-start.2 = (bf16[128,1024]{1,0:T(8,128)(2,1)}, bf16[128,1024]{1,0:T(8,128)(2,1)S(1)}, u32[]{:S(2)}, u32[]{:S(2)}) collective-permute-start(bf16[128,1024]{1,0:T(8,128)(2,1)} %bitcast.17), channel_id=1, source_target_pairs={{0,4},{2,6},{1,5},{3,7},{4,0},{6,2},{5,1},{7,3},{8,12},{10,14},{9,... | collective-permute-start | bytes 786440 | tf_op jit(solution)/shard_map/ppermute | solution.py:46
  13.7 1.5 %collective-permute-start = (bf16[128,1024]{1,0:T(8,128)(2,1)}, bf16[128,1024]{1,0:T(8,128)(2,1)S(1)}, u32[]{:S(2)}, u32[]{:S(2)}) collective-permute-start(bf16[128,1024]{1,0:T(8,128)(2,1)} %bitcast.18), channel_id=1, source_target_pairs={{0,1},{2,7},{1,4},{3,2},{4,5},{6,3},{5,0},{7,6},{8,9},{10,15},{9,1... | collective-permute-start | bytes 786440 | tf_op jit(solution)/shard_map/ppermute | solution.py:46
  15.7 11.9 %all-to-all-done = bf16[16,16,1024]{2,1,0:T(8,128)(2,1)S(1)} async-done(((bf16[16,16,1024]{2,1,0:T(8,128)(2,1)}), bf16[16,16,1024]{2,1,0:T(8,128)(2,1)S(1)}, u32[]{:S(2)}, u32[]{:S(2)}) %all-to-all-start) | async-done | bytes 524320 | tf_op jit(solution)/shard_map/all_to_all | solution.py:251
  27.6 0.7 shard_map.69
  28.3 1.6 %collective-permute-start.6 = (bf16[128,1024]{1,0:T(8,128)(2,1)S(1)}, bf16[128,1024]{1,0:T(8,128)(2,1)S(1)}, u32[]{:S(2)}, u32[]{:S(2)}) collective-permute-start(bf16[128,1024]{1,0:T(8,128)(2,1)S(1)} %get-tuple-element.16), channel_id=1, source_target_pairs={{0,8},{2,26},{8,16},{10,2},{16,24},{18,10},{24,0},{26,18},{1,9},{3... | collective-permute-start | bytes 786440 | tf_op jit(solution)/shard_map/ppermute | solution.py:38
  29.9 1.7 %collective-permute-start.9 = (bf16[256,1024]{1,0:T(8,128)(2,1)S(1)}, bf16[256,1024]{1,0:T(8,128)(2,1)S(1)}, u32[]{:S(2)}, u32[]{:S(2)}) collective-permute-start(bf16[256,1024]{1,0:T(8,128)(2,1)S(1)} %bitcast.13), channel_id=1, source_target_pairs={{0,24},{2,10},{8,0},{10,18},{16,8},{18,26},{24,16},{26,2},{1,25},{... | collective-permute-start | bytes 1572872 | tf_op jit(solution)/shard_map/ppermute | solution.py:38
  31.7 1.3 %collective-permute-start.8 = (bf16[128,1024]{1,0:T(8,128)(2,1)}, bf16[128,1024]{1,0:T(8,128)(2,1)S(1)}, u32[]{:S(2)}, u32[]{:S(2)}) collective-permute-start(bf16[128,1024]{1,0:T(8,128)(2,1)} %get-tuple-element.20), channel_id=1, source_target_pairs={{0,8},{2,26},{8,16},{10,2},{16,24},{18,10},{24,0},{26,18},{1,9},{3... | collective-permute-start | bytes 786440 | tf_op jit(solution)/shard_map/ppermute | solution.py:38
  33.0 4.6 %collective-permute-done.6.near_0_ref = bf16[128,1024]{1,0:T(8,128)(2,1)S(1)} collective-permute-done((bf16[128,1024]{1,0:T(8,128)(2,1)S(1)}, bf16[128,1024]{1,0:T(8,128)(2,1)S(1)}, u32[]{:S(2)}, u32[]{:S(2)}) %collective-permute-start.6) | collective-permute-done | bytes 262176 | tf_op jit(solution)/shard_map/ppermute | solution.py:38
  38.5 4.7 %collective-permute-done.8.near_1_ref = bf16[128,1024]{1,0:T(8,128)(2,1)S(1)} collective-permute-done((bf16[128,1024]{1,0:T(8,128)(2,1)}, bf16[128,1024]{1,0:T(8,128)(2,1)S(1)}, u32[]{:S(2)}, u32[]{:S(2)}) %collective-permute-start.8) | collective-permute-done | bytes 262176 | tf_op jit(solution)/shard_map/ppermute | solution.py:38
  43.6 2.4 %shard_map.70 = (f32[1024,1024]{1,0:T(8,128)S(1)}, bf16[1024,1024]{1,0:T(8,128)(2,1)S(1)}, f32[2,2,8,128]{3,2,1,0:T(8,128)S(1)}, f32[8,128]{1,0:T(8,128)S(1)}, f32[4,128]{1,0:T(4,128)S(1)}) custom-call(s32[4]{0:T(128)S(1)} %pad_add_fusion.where_ref, s32[2,4]{1,0:T(2,128)} %mask_hbm.1, f32[16,128]{1,0:T(8,128)} %bitcast.22, bf16[128,1024]{1,0:T(8,128)(2,1)} %bitcast.21, ...), custom_call_target="tpu_custom_call" | custom-call | flops 536870912 | bytes 8000000 | tf_op jit(solution)/shard_map/pallas_call | solution.py:267
  46.1 1.3 %shard_map.71.scores_ref = f32[1024,1024]{1,0:T(8,128)S(1)} custom-call(bf16[1024,1024]{1,0:T(8,128)(2,1)S(1)} %get-tuple-element.18.ordered_ref, f32[1024,1024]{1,0:T(8,128)S(1)} %get-tuple-element.19.scores_ref, bf16[128,1024]{1,0:T(8,128)(2,1)S(1)} %collective-permute-done.6.near_0_ref, bf16[128,1024]{1,0:T(8,128)(2,1)S(1)} %collective-permute-done.8.near_1_ref, ...), custom_call_target="tpu_custom_call" | custom-call | flops 1073741824 | bytes 8000000 | tf_op jit(solution)/shard_map/pallas_call | solution.py:288
  47.4 3.3 %collective-permute-done.11.far_1_ref = bf16[128,1024]{1,0:T(8,128)(2,1)S(1)} collective-permute-done((bf16[128,1024]{1,0:T(8,128)(2,1)S(1)}, bf16[128,1024]{1,0:T(8,128)(2,1)S(1)}, u32[]{:S(2)}, u32[]{:S(2)}) %collective-permute-start.11) | collective-permute-done | bytes 262176 | tf_op jit(solution)/shard_map/ppermute | solution.py:38
  50.8 1.3 %shard_map.72 = (f32[1024,1024]{1,0:T(8,128)S(1)}, f32[8,16,128]{2,1,0:T(8,128)S(1)}) custom-call(bf16[1024,1024]{1,0:T(8,128)(2,1)S(1)} %get-tuple-element.18.ordered_ref, f32[1024,1024]{1,0:T(8,128)S(1)} %shard_map.71.scores_ref, f32[2,2,8,128]{3,2,1,0:T(8,128)S(1)} %get-tuple-element.21.live_ref, f32[4,128]{1,0:T(4,128)S(1)} %bitcast.16, ...), custom_call_target="tpu_custom_call" | custom-call | flops 536870912 | bytes 8000000 | tf_op jit(solution)/shard_map/pallas_call | solution.py:298
  52.1 9.2 %all_to_all.25.parts_ref = f32[8,16,128]{2,1,0:T(8,128)S(1)} all-to-all(f32[8,16,128]{2,1,0:T(8,128)S(1)} %get-tuple-element.23), channel_id=1, replica_groups=mesh['z'=8,'y'=4,'xh'=2,'c'=2,'xl'=2] {'xh','c','xl'}, dimensions={0} | all-to-all | bytes 131072 | tf_op jit(solution)/shard_map/all_to_all | solution.py:311
  61.7 15.1 %all_to_all.26.parts_ref = f32[32,8,128]{2,1,0:T(8,128)S(1)} all-to-all(f32[32,8,128]{2,1,0:T(8,128)S(1)} %get-tuple-element.27), channel_id=1, replica_groups=mesh['z'=8,'y'=4,'xh'=2,'c'=2,'xl'=2] {'z','y'}, dimensions={0} | all-to-all | bytes 262144 | tf_op jit(solution)/shard_map/all_to_all | solution.py:329
  77.2 1.2 collective-permute-done.12
  78.4 2.1 %collective-permute-start.13 = (f32[8,128]{1,0:T(8,128)S(1)}, f32[8,128]{1,0:T(8,128)S(1)}, u32[]{:S(2)}, u32[]{:S(2)}) collective-permute-start(f32[8,128]{1,0:T(8,128)S(1)} %add.6.refs_0_), channel_id=1, source_target_pairs={{0,1},{2,7},{1,4},{3,2},{4,5},{6,3},{5,0},{7,6},{8,9},{10,15},{9,1... | collective-permute-start | bytes 12296 | tf_op jit(solution)/shard_map/ppermute | solution.py:46
  81.0 1.0 collective-permute-done.13.refs_1_
  82.2 3.3 %collective-permute-done.14.refs_2_ = f32[8,128]{1,0:T(8,128)S(1)} collective-permute-done((f32[8,128]{1,0:T(8,128)S(1)}, f32[8,128]{1,0:T(8,128)S(1)}, u32[]{:S(2)}, u32[]{:S(2)}) %collective-permute-start.14) | collective-permute-done | bytes 4128 | tf_op jit(solution)/shard_map/ppermute | solution.py:31
  86.0 13.7 %all_to_all.27.parts_ref = f32[32,8,128]{2,1,0:T(8,128)S(1)} all-to-all(f32[32,8,128]{2,1,0:T(8,128)S(1)} %shard_map.75), channel_id=1, replica_groups=mesh['z'=8,'y'=4,'xh'=2,'c'=2,'xl'=2] {'z','y'}, dimensions={0} | all-to-all | bytes 262144 | tf_op jit(solution)/shard_map/all_to_all | solution.py:329
  100.2 1.2 collective-permute-done.16
  101.3 1.2 collective-permute-start.17
  102.5 1.0 collective-permute-start.18
  103.5 1.4 %collective-permute-done.17.refs_1_ = f32[8,128]{1,0:T(8,128)S(1)} collective-permute-done((f32[8,128]{1,0:T(8,128)S(1)}, f32[8,128]{1,0:T(8,128)S(1)}, u32[]{:S(2)}, u32[]{:S(2)}) %collective-permute-start.17) | collective-permute-done | bytes 4128 | tf_op jit(solution)/shard_map/ppermute | solution.py:46
  105.2 2.5 %collective-permute-done.18.refs_2_ = f32[8,128]{1,0:T(8,128)S(1)} collective-permute-done((f32[8,128]{1,0:T(8,128)S(1)}, f32[8,128]{1,0:T(8,128)S(1)}, u32[]{:S(2)}, u32[]{:S(2)}) %collective-permute-start.18) | collective-permute-done | bytes 4128 | tf_op jit(solution)/shard_map/ppermute | solution.py:31
  107.6 0.9 shard_map.77
  108.6 13.9 %all_to_all.28 = f32[32,8,128]{2,1,0:T(8,128)S(1)} all-to-all(f32[32,8,128]{2,1,0:T(8,128)S(1)} %get-tuple-element.29), channel_id=1, replica_groups=mesh['z'=8,'y'=4,'xh'=2,'c'=2,'xl'=2] {'z','y'}, dimensions={0} | all-to-all | bytes 262144 | tf_op jit(solution)/shard_map/all_to_all | solution.py:329
  122.5 0.8 collective-permute-start.20
  123.3 2.9 %collective-permute-done.20 = f32[1024]{0:T(1024)S(1)} collective-permute-done((f32[1024]{0:T(1024)S(1)}, f32[1024]{0:T(1024)S(1)}, u32[]{:S(2)}, u32[]{:S(2)}) %collective-permute-start.20) | collective-permute-done | bytes 4128 | tf_op jit(solution)/shard_map/ppermute | solution.py:31
  (36 shorter events, 5.4 us)
Async XLA Ops:
  0.6 0.8 copy-start
  2.3 25.3 %all-to-all-start = ((bf16[16,16,1024]{2,1,0:T(8,128)(2,1)}), bf16[16,16,1024]{2,1,0:T(8,128)(2,1)S(1)}, u32[]{:S(2)}, u32[]{:S(2)}) async-start(bf16[16,16,1024]{2,1,0:T(8,128)(2,1)} %shard_map.68), calls=%async_computation | async-start | bytes 1048576 | tf_op jit(solution)/shard_map/all_to_all | solution.py:251
  12.3 17.6 %collective-permute-start.2 = (bf16[128,1024]{1,0:T(8,128)(2,1)}, bf16[128,1024]{1,0:T(8,128)(2,1)S(1)}, u32[]{:S(2)}, u32[]{:S(2)}) collective-permute-start(bf16[128,1024]{1,0:T(8,128)(2,1)} %bitcast.17), channel_id=1, source_target_pairs={{0,4},{2,6},{1,5},{3,7},{4,0},{6,2},{5,1},{7,3},{8,12},{10,14},{9,... | collective-permute-start | bytes 786440 | tf_op jit(solution)/shard_map/ppermute | solution.py:46
  13.7 17.9 %collective-permute-start = (bf16[128,1024]{1,0:T(8,128)(2,1)}, bf16[128,1024]{1,0:T(8,128)(2,1)S(1)}, u32[]{:S(2)}, u32[]{:S(2)}) collective-permute-start(bf16[128,1024]{1,0:T(8,128)(2,1)} %bitcast.18), channel_id=1, source_target_pairs={{0,1},{2,7},{1,4},{3,2},{4,5},{6,3},{5,0},{7,6},{8,9},{10,15},{9,1... | collective-permute-start | bytes 786440 | tf_op jit(solution)/shard_map/ppermute | solution.py:46
  15.1 16.6 %collective-permute-start.1 = (bf16[128,1024]{1,0:T(8,128)(2,1)}, bf16[128,1024]{1,0:T(8,128)(2,1)S(1)}, u32[]{:S(2)}, u32[]{:S(2)}) collective-permute-start(bf16[128,1024]{1,0:T(8,128)(2,1)} %bitcast.19), channel_id=1, source_target_pairs={{0,5},{2,3},{1,0},{3,6},{4,1},{6,7},{5,4},{7,2},{8,13},{10,11},{9,... | collective-permute-start | bytes 786440 | tf_op jit(solution)/shard_map/ppermute | solution.py:46
  28.3 9.3 %collective-permute-start.6 = (bf16[128,1024]{1,0:T(8,128)(2,1)S(1)}, bf16[128,1024]{1,0:T(8,128)(2,1)S(1)}, u32[]{:S(2)}, u32[]{:S(2)}) collective-permute-start(bf16[128,1024]{1,0:T(8,128)(2,1)S(1)} %get-tuple-element.16), channel_id=1, source_target_pairs={{0,8},{2,26},{8,16},{10,2},{16,24},{18,10},{24,0},{26,18},{1,9},{3... | collective-permute-start | bytes 786440 | tf_op jit(solution)/shard_map/ppermute | solution.py:38
  29.9 7.7 %collective-permute-start.3 = (bf16[128,1024]{1,0:T(8,128)(2,1)}, bf16[128,1024]{1,0:T(8,128)(2,1)S(1)}, u32[]{:S(2)}, u32[]{:S(2)}) collective-permute-start(bf16[128,1024]{1,0:T(8,128)(2,1)} %bitcast.20), channel_id=1, source_target_pairs={{0,2},{2,0},{1,3},{3,1},{4,6},{6,4},{5,7},{7,5},{8,10},{10,8},{9,1... | collective-permute-start | bytes 786440 | tf_op jit(solution)/shard_map/ppermute | solution.py:31
  29.9 16.2 %collective-permute-start.9 = (bf16[256,1024]{1,0:T(8,128)(2,1)S(1)}, bf16[256,1024]{1,0:T(8,128)(2,1)S(1)}, u32[]{:S(2)}, u32[]{:S(2)}) collective-permute-start(bf16[256,1024]{1,0:T(8,128)(2,1)S(1)} %bitcast.13), channel_id=1, source_target_pairs={{0,24},{2,10},{8,0},{10,18},{16,8},{18,26},{24,16},{26,2},{1,25},{... | collective-permute-start | bytes 1572872 | tf_op jit(solution)/shard_map/ppermute | solution.py:38
  31.6 6.5 %collective-permute-start.4 = (bf16[128,1024]{1,0:T(8,128)(2,1)S(1)}, bf16[128,1024]{1,0:T(8,128)(2,1)S(1)}, u32[]{:S(2)}, u32[]{:S(2)}) collective-permute-start(bf16[128,1024]{1,0:T(8,128)(2,1)S(1)} %collective-permute-done.refs_0_), channel_id=1, source_target_pairs={{0,2},{2,0},{1,3},{3,1},{4,6},{6,4},{5,7},{7,5},{8,10},{10,8},{9,1... | collective-permute-start | bytes 786440 | tf_op jit(solution)/shard_map/ppermute | solution.py:31
  31.7 11.5 %collective-permute-start.8 = (bf16[128,1024]{1,0:T(8,128)(2,1)}, bf16[128,1024]{1,0:T(8,128)(2,1)S(1)}, u32[]{:S(2)}, u32[]{:S(2)}) collective-permute-start(bf16[128,1024]{1,0:T(8,128)(2,1)} %get-tuple-element.20), channel_id=1, source_target_pairs={{0,8},{2,26},{8,16},{10,2},{16,24},{18,10},{24,0},{26,18},{1,9},{3... | collective-permute-start | bytes 786440 | tf_op jit(solution)/shard_map/ppermute | solution.py:38
  37.6 6.1 %collective-permute-start.5 = (bf16[128,1024]{1,0:T(8,128)(2,1)S(1)}, bf16[128,1024]{1,0:T(8,128)(2,1)S(1)}, u32[]{:S(2)}, u32[]{:S(2)}) collective-permute-start(bf16[128,1024]{1,0:T(8,128)(2,1)S(1)} %collective-permute-done.1.refs_1_), channel_id=1, source_target_pairs={{0,2},{2,0},{1,3},{3,1},{4,6},{6,4},{5,7},{7,5},{8,10},{10,8},{9,1... | collective-permute-start | bytes 786440 | tf_op jit(solution)/shard_map/ppermute | solution.py:31
  37.6 6.1 %collective-permute-start.7 = (bf16[128,1024]{1,0:T(8,128)(2,1)S(1)}, bf16[128,1024]{1,0:T(8,128)(2,1)S(1)}, u32[]{:S(2)}, u32[]{:S(2)}) collective-permute-start(bf16[128,1024]{1,0:T(8,128)(2,1)S(1)} %collective-permute-done.2.refs_2_), channel_id=1, source_target_pairs={{0,2},{2,0},{1,3},{3,1},{4,6},{6,4},{5,7},{7,5},{8,10},{10,8},{9,1... | collective-permute-start | bytes 786440 | tf_op jit(solution)/shard_map/ppermute | solution.py:31
  38.1 9.3 %collective-permute-start.10 = (bf16[128,1024]{1,0:T(8,128)(2,1)S(1)}, bf16[128,1024]{1,0:T(8,128)(2,1)S(1)}, u32[]{:S(2)}, u32[]{:S(2)}) collective-permute-start(bf16[128,1024]{1,0:T(8,128)(2,1)S(1)} %collective-permute-done.6.near_0_ref), channel_id=1, source_target_pairs={{0,8},{2,26},{8,16},{10,2},{16,24},{18,10},{24,0},{26,18},{1,9},{3... | collective-permute-start | bytes 786440 | tf_op jit(solution)/shard_map/ppermute | solution.py:38
  43.2 7.6 %collective-permute-start.11 = (bf16[128,1024]{1,0:T(8,128)(2,1)S(1)}, bf16[128,1024]{1,0:T(8,128)(2,1)S(1)}, u32[]{:S(2)}, u32[]{:S(2)}) collective-permute-start(bf16[128,1024]{1,0:T(8,128)(2,1)S(1)} %collective-permute-done.8.near_1_ref), channel_id=1, source_target_pairs={{0,8},{2,26},{8,16},{10,2},{16,24},{18,10},{24,0},{26,18},{1,9},{3... | collective-permute-start | bytes 786440 | tf_op jit(solution)/shard_map/ppermute | solution.py:38
  46.1 4.7 %copy-start.1 = (f32[512]{0:T(512)S(1)}, f32[512]{0:T(512)}, u32[]{:S(2)}) copy-start(f32[512]{0:T(512)} %param.8) | copy-start | bytes 6148
  77.1 1.3 collective-permute-start.12
  78.4 3.6 %collective-permute-start.13 = (f32[8,128]{1,0:T(8,128)S(1)}, f32[8,128]{1,0:T(8,128)S(1)}, u32[]{:S(2)}, u32[]{:S(2)}) collective-permute-start(f32[8,128]{1,0:T(8,128)S(1)} %add.6.refs_0_), channel_id=1, source_target_pairs={{0,1},{2,7},{1,4},{3,2},{4,5},{6,3},{5,0},{7,6},{8,9},{10,15},{9,1... | collective-permute-start | bytes 12296 | tf_op jit(solution)/shard_map/ppermute | solution.py:46
  80.5 5.1 %collective-permute-start.14 = (f32[8,128]{1,0:T(8,128)S(1)}, f32[8,128]{1,0:T(8,128)S(1)}, u32[]{:S(2)}, u32[]{:S(2)}) collective-permute-start(f32[8,128]{1,0:T(8,128)S(1)} %add.6.refs_0_), channel_id=1, source_target_pairs={{0,4},{1,5},{4,0},{5,1},{2,6},{3,7},{6,2},{7,3},{8,12},{9,13},{12,... | collective-permute-start | bytes 12296 | tf_op jit(solution)/shard_map/ppermute | solution.py:31
  82.0 3.6 %collective-permute-start.15 = (f32[8,128]{1,0:T(8,128)S(1)}, f32[8,128]{1,0:T(8,128)S(1)}, u32[]{:S(2)}, u32[]{:S(2)}) collective-permute-start(f32[8,128]{1,0:T(8,128)S(1)} %collective-permute-done.13.refs_1_), channel_id=1, source_target_pairs={{0,2},{2,0},{1,3},{3,1},{4,6},{6,4},{5,7},{7,5},{8,10},{10,8},{9,1... | collective-permute-start | bytes 12296 | tf_op jit(solution)/shard_map/ppermute | solution.py:31
  100.1 1.3 collective-permute-start.16
  101.3 3.6 %collective-permute-start.17 = (f32[8,128]{1,0:T(8,128)S(1)}, f32[8,128]{1,0:T(8,128)S(1)}, u32[]{:S(2)}, u32[]{:S(2)}) collective-permute-start(f32[8,128]{1,0:T(8,128)S(1)} %add.7.refs_0_), channel_id=1, source_target_pairs={{0,1},{2,7},{1,4},{3,2},{4,5},{6,3},{5,0},{7,6},{8,9},{10,15},{9,1... | collective-permute-start | bytes 12296 | tf_op jit(solution)/shard_map/ppermute | solution.py:46
  102.5 5.1 %collective-permute-start.18 = (f32[8,128]{1,0:T(8,128)S(1)}, f32[8,128]{1,0:T(8,128)S(1)}, u32[]{:S(2)}, u32[]{:S(2)}) collective-permute-start(f32[8,128]{1,0:T(8,128)S(1)} %add.7.refs_0_), channel_id=1, source_target_pairs={{0,4},{1,5},{4,0},{5,1},{2,6},{3,7},{6,2},{7,3},{8,12},{9,13},{12,... | collective-permute-start | bytes 12296 | tf_op jit(solution)/shard_map/ppermute | solution.py:31
  104.9 2.7 %collective-permute-start.19 = (f32[8,128]{1,0:T(8,128)S(1)}, f32[8,128]{1,0:T(8,128)S(1)}, u32[]{:S(2)}, u32[]{:S(2)}) collective-permute-start(f32[8,128]{1,0:T(8,128)S(1)} %collective-permute-done.17.refs_1_), channel_id=1, source_target_pairs={{0,2},{2,0},{1,3},{3,1},{4,6},{6,4},{5,7},{7,5},{8,10},{10,8},{9,1... | collective-permute-start | bytes 12296 | tf_op jit(solution)/shard_map/ppermute | solution.py:31
  122.5 3.7 %collective-permute-start.20 = (f32[1024]{0:T(1024)S(1)}, f32[1024]{0:T(1024)S(1)}, u32[]{:S(2)}, u32[]{:S(2)}) collective-permute-start(f32[1024]{0:T(1024)S(1)} %log_bitcast_fusion), channel_id=1, source_target_pairs={{0,1},{1,0},{2,3},{3,2},{4,5},{5,4},{6,7},{7,6},{8,9},{9,8},{10,11... | collective-permute-start | bytes 12296 | tf_op jit(solution)/shard_map/ppermute | solution.py:31

commit v5 on v4

--- a/solution.py
+++ b/solution.py
@@ -256,11 +256,11 @@
         out_specs=(VMEM, VMEM),
         compiler_params=SWEEP,
     )(own_band)
-    swapped = [shift(s, "c", 2, 1) for s in (src, *src_a[:2])]
+    swapped = [shift(s, "c", 2, 1) for s in (src, src_a[0])]
     near = [wheel_y(v, 1) for v in split_band]
     away = wheel_y(own_band, -1)
-    late, _ = lax.optimization_barrier((src_a[2], near[0]))
-    swapped.append(shift(late, "c", 2, 1))
+    *late, _ = lax.optimization_barrier((src_a[1], src_a[2], near[1]))
+    swapped += [shift(s, "c", 2, 1) for s in late]
     far = [wheel_y(v, 1) for v in near]
 
     where = jnp.stack([lax.axis_index(a) for a in ("y", "c", "xh", "xl")]).astype(jnp.int32)

time: 127 us -> 127 us (level)
  transfers between devices with their start and end apart: 22 -> 22, of which waited for: 11 -> 12; matrix products, arithmetic and copies ran while one was open for 0% -> 0% of each run, Pallas kernels for 4% -> 4%
where the time goes in v5:
time: 127 us; the launch traced here: 126 us
  blocking collectives  51.6 us (41%)
  waiting for transfers between devices  37.7 us (30%)
  starting transfers between devices  25.8 us (20%)
  Pallas kernels  9.08 us (7%)
    all_to_all x3, blocking collectives, shards(): parts = lax.all_to_all(outs[-1], PLANE, 0, 0, tiled=True)  42.4 us
    ppermute x5, waiting for transfers between devices, wheel_y(): return lax.ppermute(value, ('y', 'c'), pairs)  12.1 us
    all_to_all x1, waiting for transfers between devices, shards(): lax.all_to_all(sent, ('z', 'xl'), 0, 0, tiled=True).reshape(BAND, COLS)  11.9 us
    ppermute x11, waiting for transfers between devices, shift(): lax.ppermute(value, axis, [(i, (i + by) % size) for i in range(size)])  11 us
    all_to_all x1, starting transfers between devices, shards(): lax.all_to_all(sent, ('z', 'xl'), 0, 0, tiled=True).reshape(BAND, COLS)  9.94 us
    all_to_all x1, blocking collectives, shards(): parts = [lax.all_to_all(sums, ('xh', 'c', 'xl'), 0, 0, tiled=True)]  9.23 us
    ppermute x5, starting transfers between devices, wheel_x(): return lax.ppermute(value, ('xh', 'c', 'xl'), pairs)  6.69 us
    ppermute x5, starting transfers between devices, wheel_y(): return lax.ppermute(value, ('y', 'c'), pairs)  5.55 us
  transfers between devices with their start and end apart: 22, of which 12 were waited for; matrix products, arithmetic and copies ran while one was open for 0% of the time, Pallas kernels for 4%

profile of v5, /device:TPU:6, one launch (start us, length us, event | category | flops | bytes accessed | tf_op | source)
XLA Modules:
  0.0 126.5 jit_solution(3668315542875075855)
XLA Ops:
  0.6 0.8 copy-done
  1.5 0.8 shard_map.68
  2.3 9.9 %all-to-all-start = ((bf16[16,16,1024]{2,1,0:T(8,128)(2,1)}), bf16[16,16,1024]{2,1,0:T(8,128)(2,1)S(1)}, u32[]{:S(2)}, u32[]{:S(2)}) async-start(bf16[16,16,1024]{2,1,0:T(8,128)(2,1)} %shard_map.68), calls=%async_computation | async-start | bytes 1048576 | tf_op jit(solution)/shard_map/all_to_all | solution.py:251
  12.4 3.1 %collective-permute-start = (bf16[128,1024]{1,0:T(8,128)(2,1)}, bf16[128,1024]{1,0:T(8,128)(2,1)S(1)}, u32[]{:S(2)}, u32[]{:S(2)}) collective-permute-start(bf16[128,1024]{1,0:T(8,128)(2,1)} %bitcast.18), channel_id=1, source_target_pairs={{0,1},{2,7},{1,4},{3,2},{4,5},{6,3},{5,0},{7,6},{8,9},{10,15},{9,1... | collective-permute-start | bytes 786440 | tf_op jit(solution)/shard_map/ppermute | solution.py:46
  15.7 11.9 %all-to-all-done = bf16[16,16,1024]{2,1,0:T(8,128)(2,1)S(1)} async-done(((bf16[16,16,1024]{2,1,0:T(8,128)(2,1)}), bf16[16,16,1024]{2,1,0:T(8,128)(2,1)S(1)}, u32[]{:S(2)}, u32[]{:S(2)}) %all-to-all-start) | async-done | bytes 524320 | tf_op jit(solution)/shard_map/all_to_all | solution.py:251
  27.6 0.7 shard_map.69
  28.3 1.6 %collective-permute-start.5 = (bf16[128,1024]{1,0:T(8,128)(2,1)S(1)}, bf16[128,1024]{1,0:T(8,128)(2,1)S(1)}, u32[]{:S(2)}, u32[]{:S(2)}) collective-permute-start(bf16[128,1024]{1,0:T(8,128)(2,1)S(1)} %get-tuple-element.17), channel_id=1, source_target_pairs={{0,8},{2,26},{8,16},{10,2},{16,24},{18,10},{24,0},{26,18},{1,9},{3... | collective-permute-start | bytes 786440 | tf_op jit(solution)/shard_map/ppermute | solution.py:38
  29.9 1.7 %collective-permute-start.9 = (bf16[256,1024]{1,0:T(8,128)(2,1)S(1)}, bf16[256,1024]{1,0:T(8,128)(2,1)S(1)}, u32[]{:S(2)}, u32[]{:S(2)}) collective-permute-start(bf16[256,1024]{1,0:T(8,128)(2,1)S(1)} %bitcast.13), channel_id=1, source_target_pairs={{0,24},{2,10},{8,0},{10,18},{16,8},{18,26},{24,16},{26,2},{1,25},{... | collective-permute-start | bytes 1572872 | tf_op jit(solution)/shard_map/ppermute | solution.py:38
  31.9 1.6 %collective-permute-start.8 = (bf16[128,1024]{1,0:T(8,128)(2,1)}, bf16[128,1024]{1,0:T(8,128)(2,1)S(1)}, u32[]{:S(2)}, u32[]{:S(2)}) collective-permute-start(bf16[128,1024]{1,0:T(8,128)(2,1)} %get-tuple-element.22), channel_id=1, source_target_pairs={{0,8},{2,26},{8,16},{10,2},{16,24},{18,10},{24,0},{26,18},{1,9},{3... | collective-permute-start | bytes 786440 | tf_op jit(solution)/shard_map/ppermute | solution.py:38
  33.5 4.1 %collective-permute-done.5.near_1_ref = bf16[128,1024]{1,0:T(8,128)(2,1)S(1)} collective-permute-done((bf16[128,1024]{1,0:T(8,128)(2,1)S(1)}, bf16[128,1024]{1,0:T(8,128)(2,1)S(1)}, u32[]{:S(2)}, u32[]{:S(2)}) %collective-permute-start.5) | collective-permute-done | bytes 262176 | tf_op jit(solution)/shard_map/ppermute | solution.py:38
  38.5 4.7 %collective-permute-done.8.near_0_ref = bf16[128,1024]{1,0:T(8,128)(2,1)S(1)} collective-permute-done((bf16[128,1024]{1,0:T(8,128)(2,1)}, bf16[128,1024]{1,0:T(8,128)(2,1)S(1)}, u32[]{:S(2)}, u32[]{:S(2)}) %collective-permute-start.8) | collective-permute-done | bytes 262176 | tf_op jit(solution)/shard_map/ppermute | solution.py:38
  43.6 2.4 %shard_map.70 = (f32[1024,1024]{1,0:T(8,128)S(1)}, bf16[1024,1024]{1,0:T(8,128)(2,1)S(1)}, f32[2,2,8,128]{3,2,1,0:T(8,128)S(1)}, f32[8,128]{1,0:T(8,128)S(1)}, f32[4,128]{1,0:T(4,128)S(1)}) custom-call(s32[4]{0:T(128)S(1)} %pad_add_fusion.where_ref, s32[2,4]{1,0:T(2,128)} %mask_hbm.1, f32[16,128]{1,0:T(8,128)} %bitcast.22, bf16[128,1024]{1,0:T(8,128)(2,1)} %bitcast.21, ...), custom_call_target="tpu_custom_call" | custom-call | flops 536870912 | bytes 8000000 | tf_op jit(solution)/shard_map/pallas_call | solution.py:267
  46.1 1.3 %shard_map.71.scores_ref = f32[1024,1024]{1,0:T(8,128)S(1)} custom-call(bf16[1024,1024]{1,0:T(8,128)(2,1)S(1)} %get-tuple-element.20.ordered_ref, f32[1024,1024]{1,0:T(8,128)S(1)} %get-tuple-element.21.scores_ref, bf16[128,1024]{1,0:T(8,128)(2,1)S(1)} %collective-permute-done.8.near_0_ref, bf16[128,1024]{1,0:T(8,128)(2,1)S(1)} %collective-permute-done.5.near_1_ref, ...), custom_call_target="tpu_custom_call" | custom-call | flops 1073741824 | bytes 8000000 | tf_op jit(solution)/shard_map/pallas_call | solution.py:288
  47.4 3.3 %collective-permute-done.10.far_0_ref = bf16[128,1024]{1,0:T(8,128)(2,1)S(1)} collective-permute-done((bf16[128,1024]{1,0:T(8,128)(2,1)S(1)}, bf16[128,1024]{1,0:T(8,128)(2,1)S(1)}, u32[]{:S(2)}, u32[]{:S(2)}) %collective-permute-start.10) | collective-permute-done | bytes 262176 | tf_op jit(solution)/shard_map/ppermute | solution.py:38
  50.8 1.3 %shard_map.72 = (f32[1024,1024]{1,0:T(8,128)S(1)}, f32[8,16,128]{2,1,0:T(8,128)S(1)}) custom-call(bf16[1024,1024]{1,0:T(8,128)(2,1)S(1)} %get-tuple-element.20.ordered_ref, f32[1024,1024]{1,0:T(8,128)S(1)} %shard_map.71.scores_ref, f32[2,2,8,128]{3,2,1,0:T(8,128)S(1)} %get-tuple-element.23.live_ref, f32[4,128]{1,0:T(4,128)S(1)} %bitcast.16, ...), custom_call_target="tpu_custom_call" | custom-call | flops 536870912 | bytes 8000000 | tf_op jit(solution)/shard_map/pallas_call | solution.py:298
  52.1 9.2 %all_to_all.25.parts_ref = f32[8,16,128]{2,1,0:T(8,128)S(1)} all-to-all(f32[8,16,128]{2,1,0:T(8,128)S(1)} %get-tuple-element.25), channel_id=1, replica_groups=mesh['z'=8,'y'=4,'xh'=2,'c'=2,'xl'=2] {'xh','c','xl'}, dimensions={0} | all-to-all | bytes 131072 | tf_op jit(solution)/shard_map/all_to_all | solution.py:311
  61.7 14.8 %all_to_all.26.parts_ref = f32[32,8,128]{2,1,0:T(8,128)S(1)} all-to-all(f32[32,8,128]{2,1,0:T(8,128)S(1)} %get-tuple-element.29), channel_id=1, replica_groups=mesh['z'=8,'y'=4,'xh'=2,'c'=2,'xl'=2] {'z','y'}, dimensions={0} | all-to-all | bytes 262144 | tf_op jit(solution)/shard_map/all_to_all | solution.py:329
  76.9 1.2 collective-permute-done.12
  78.1 2.1 %collective-permute-start.13 = (f32[8,128]{1,0:T(8,128)S(1)}, f32[8,128]{1,0:T(8,128)S(1)}, u32[]{:S(2)}, u32[]{:S(2)}) collective-permute-start(f32[8,128]{1,0:T(8,128)S(1)} %add.6.refs_0_), channel_id=1, source_target_pairs={{0,1},{2,7},{1,4},{3,2},{4,5},{6,3},{5,0},{7,6},{8,9},{10,15},{9,1... | collective-permute-start | bytes 12296 | tf_op jit(solution)/shard_map/ppermute | solution.py:46
  80.7 1.0 collective-permute-done.13.refs_1_
  81.9 3.3 %collective-permute-done.14.refs_2_ = f32[8,128]{1,0:T(8,128)S(1)} collective-permute-done((f32[8,128]{1,0:T(8,128)S(1)}, f32[8,128]{1,0:T(8,128)S(1)}, u32[]{:S(2)}, u32[]{:S(2)}) %collective-permute-start.14) | collective-permute-done | bytes 4128 | tf_op jit(solution)/shard_map/ppermute | solution.py:31
  85.7 13.7 %all_to_all.27.parts_ref = f32[32,8,128]{2,1,0:T(8,128)S(1)} all-to-all(f32[32,8,128]{2,1,0:T(8,128)S(1)} %shard_map.75), channel_id=1, replica_groups=mesh['z'=8,'y'=4,'xh'=2,'c'=2,'xl'=2] {'z','y'}, dimensions={0} | all-to-all | bytes 262144 | tf_op jit(solution)/shard_map/all_to_all | solution.py:329
  99.9 1.2 collective-permute-done.16
  101.0 1.2 collective-permute-start.17
  102.2 1.0 collective-permute-start.18
  103.2 1.4 %collective-permute-done.17.refs_1_ = f32[8,128]{1,0:T(8,128)S(1)} collective-permute-done((f32[8,128]{1,0:T(8,128)S(1)}, f32[8,128]{1,0:T(8,128)S(1)}, u32[]{:S(2)}, u32[]{:S(2)}) %collective-permute-start.17) | collective-permute-done | bytes 4128 | tf_op jit(solution)/shard_map/ppermute | solution.py:46
  104.9 2.5 %collective-permute-done.18.refs_2_ = f32[8,128]{1,0:T(8,128)S(1)} collective-permute-done((f32[8,128]{1,0:T(8,128)S(1)}, f32[8,128]{1,0:T(8,128)S(1)}, u32[]{:S(2)}, u32[]{:S(2)}) %collective-permute-start.18) | collective-permute-done | bytes 4128 | tf_op jit(solution)/shard_map/ppermute | solution.py:31
  107.3 0.9 shard_map.77
  108.3 13.9 %all_to_all.28 = f32[32,8,128]{2,1,0:T(8,128)S(1)} all-to-all(f32[32,8,128]{2,1,0:T(8,128)S(1)} %get-tuple-element.31), channel_id=1, replica_groups=mesh['z'=8,'y'=4,'xh'=2,'c'=2,'xl'=2] {'z','y'}, dimensions={0} | all-to-all | bytes 262144 | tf_op jit(solution)/shard_map/all_to_all | solution.py:329
  122.2 0.8 collective-permute-start.20
  123.0 2.9 %collective-permute-done.20 = f32[1024]{0:T(1024)S(1)} collective-permute-done((f32[1024]{0:T(1024)S(1)}, f32[1024]{0:T(1024)S(1)}, u32[]{:S(2)}, u32[]{:S(2)}) %collective-permute-start.20) | collective-permute-done | bytes 4128 | tf_op jit(solution)/shard_map/ppermute | solution.py:31
  125.9 0.6 maximum_select_fusion
  (36 shorter events, 4.8 us)
Async XLA Ops:
  0.6 0.8 copy-start
  2.3 25.3 %all-to-all-start = ((bf16[16,16,1024]{2,1,0:T(8,128)(2,1)}), bf16[16,16,1024]{2,1,0:T(8,128)(2,1)S(1)}, u32[]{:S(2)}, u32[]{:S(2)}) async-start(bf16[16,16,1024]{2,1,0:T(8,128)(2,1)} %shard_map.68), calls=%async_computation | async-start | bytes 1048576 | tf_op jit(solution)/shard_map/all_to_all | solution.py:251
  12.3 17.6 %collective-permute-start.1 = (bf16[128,1024]{1,0:T(8,128)(2,1)}, bf16[128,1024]{1,0:T(8,128)(2,1)S(1)}, u32[]{:S(2)}, u32[]{:S(2)}) collective-permute-start(bf16[128,1024]{1,0:T(8,128)(2,1)} %bitcast.17), channel_id=1, source_target_pairs={{0,5},{2,3},{1,0},{3,6},{4,1},{6,7},{5,4},{7,2},{8,13},{10,11},{9,... | collective-permute-start | bytes 786440 | tf_op jit(solution)/shard_map/ppermute | solution.py:46
  12.4 19.1 %collective-permute-start = (bf16[128,1024]{1,0:T(8,128)(2,1)}, bf16[128,1024]{1,0:T(8,128)(2,1)S(1)}, u32[]{:S(2)}, u32[]{:S(2)}) collective-permute-start(bf16[128,1024]{1,0:T(8,128)(2,1)} %bitcast.18), channel_id=1, source_target_pairs={{0,1},{2,7},{1,4},{3,2},{4,5},{6,3},{5,0},{7,6},{8,9},{10,15},{9,1... | collective-permute-start | bytes 786440 | tf_op jit(solution)/shard_map/ppermute | solution.py:46
  15.5 16.4 %collective-permute-start.2 = (bf16[128,1024]{1,0:T(8,128)(2,1)}, bf16[128,1024]{1,0:T(8,128)(2,1)S(1)}, u32[]{:S(2)}, u32[]{:S(2)}) collective-permute-start(bf16[128,1024]{1,0:T(8,128)(2,1)} %bitcast.19), channel_id=1, source_target_pairs={{0,4},{2,6},{1,5},{3,7},{4,0},{6,2},{5,1},{7,3},{8,12},{10,14},{9,... | collective-permute-start | bytes 786440 | tf_op jit(solution)/shard_map/ppermute | solution.py:46
  28.3 9.3 %collective-permute-start.5 = (bf16[128,1024]{1,0:T(8,128)(2,1)S(1)}, bf16[128,1024]{1,0:T(8,128)(2,1)S(1)}, u32[]{:S(2)}, u32[]{:S(2)}) collective-permute-start(bf16[128,1024]{1,0:T(8,128)(2,1)S(1)} %get-tuple-element.17), channel_id=1, source_target_pairs={{0,8},{2,26},{8,16},{10,2},{16,24},{18,10},{24,0},{26,18},{1,9},{3... | collective-permute-start | bytes 786440 | tf_op jit(solution)/shard_map/ppermute | solution.py:38
  29.9 7.7 %collective-permute-start.3 = (bf16[128,1024]{1,0:T(8,128)(2,1)}, bf16[128,1024]{1,0:T(8,128)(2,1)S(1)}, u32[]{:S(2)}, u32[]{:S(2)}) collective-permute-start(bf16[128,1024]{1,0:T(8,128)(2,1)} %bitcast.20), channel_id=1, source_target_pairs={{0,2},{2,0},{1,3},{3,1},{4,6},{6,4},{5,7},{7,5},{8,10},{10,8},{9,1... | collective-permute-start | bytes 786440 | tf_op jit(solution)/shard_map/ppermute | solution.py:31
  29.9 16.2 %collective-permute-start.9 = (bf16[256,1024]{1,0:T(8,128)(2,1)S(1)}, bf16[256,1024]{1,0:T(8,128)(2,1)S(1)}, u32[]{:S(2)}, u32[]{:S(2)}) collective-permute-start(bf16[256,1024]{1,0:T(8,128)(2,1)S(1)} %bitcast.13), channel_id=1, source_target_pairs={{0,24},{2,10},{8,0},{10,18},{16,8},{18,26},{24,16},{26,2},{1,25},{... | collective-permute-start | bytes 1572872 | tf_op jit(solution)/shard_map/ppermute | solution.py:38
  31.6 6.5 %collective-permute-start.4 = (bf16[128,1024]{1,0:T(8,128)(2,1)S(1)}, bf16[128,1024]{1,0:T(8,128)(2,1)S(1)}, u32[]{:S(2)}, u32[]{:S(2)}) collective-permute-start(bf16[128,1024]{1,0:T(8,128)(2,1)S(1)} %collective-permute-done.refs_0_), channel_id=1, source_target_pairs={{0,2},{2,0},{1,3},{3,1},{4,6},{6,4},{5,7},{7,5},{8,10},{10,8},{9,1... | collective-permute-start | bytes 786440 | tf_op jit(solution)/shard_map/ppermute | solution.py:31
  31.9 11.3 %collective-permute-start.8 = (bf16[128,1024]{1,0:T(8,128)(2,1)}, bf16[128,1024]{1,0:T(8,128)(2,1)S(1)}, u32[]{:S(2)}, u32[]{:S(2)}) collective-permute-start(bf16[128,1024]{1,0:T(8,128)(2,1)} %get-tuple-element.22), channel_id=1, source_target_pairs={{0,8},{2,26},{8,16},{10,2},{16,24},{18,10},{24,0},{26,18},{1,9},{3... | collective-permute-start | bytes 786440 | tf_op jit(solution)/shard_map/ppermute | solution.py:38
  37.6 6.1 %collective-permute-start.6 = (bf16[128,1024]{1,0:T(8,128)(2,1)S(1)}, bf16[128,1024]{1,0:T(8,128)(2,1)S(1)}, u32[]{:S(2)}, u32[]{:S(2)}) collective-permute-start(bf16[128,1024]{1,0:T(8,128)(2,1)S(1)} %collective-permute-done.1.refs_1_), channel_id=1, source_target_pairs={{0,2},{2,0},{1,3},{3,1},{4,6},{6,4},{5,7},{7,5},{8,10},{10,8},{9,1... | collective-permute-start | bytes 786440 | tf_op jit(solution)/shard_map/ppermute | solution.py:31
  37.6 6.1 %collective-permute-start.7 = (bf16[128,1024]{1,0:T(8,128)(2,1)S(1)}, bf16[128,1024]{1,0:T(8,128)(2,1)S(1)}, u32[]{:S(2)}, u32[]{:S(2)}) collective-permute-start(bf16[128,1024]{1,0:T(8,128)(2,1)S(1)} %collective-permute-done.2.refs_2_), channel_id=1, source_target_pairs={{0,2},{2,0},{1,3},{3,1},{4,6},{6,4},{5,7},{7,5},{8,10},{10,8},{9,1... | collective-permute-start | bytes 786440 | tf_op jit(solution)/shard_map/ppermute | solution.py:31
  38.1 9.3 %collective-permute-start.11 = (bf16[128,1024]{1,0:T(8,128)(2,1)S(1)}, bf16[128,1024]{1,0:T(8,128)(2,1)S(1)}, u32[]{:S(2)}, u32[]{:S(2)}) collective-permute-start(bf16[128,1024]{1,0:T(8,128)(2,1)S(1)} %collective-permute-done.5.near_1_ref), channel_id=1, source_target_pairs={{0,8},{2,26},{8,16},{10,2},{16,24},{18,10},{24,0},{26,18},{1,9},{3... | collective-permute-start | bytes 786440 | tf_op jit(solution)/shard_map/ppermute | solution.py:38
  43.2 7.6 %collective-permute-start.10 = (bf16[128,1024]{1,0:T(8,128)(2,1)S(1)}, bf16[128,1024]{1,0:T(8,128)(2,1)S(1)}, u32[]{:S(2)}, u32[]{:S(2)}) collective-permute-start(bf16[128,1024]{1,0:T(8,128)(2,1)S(1)} %collective-permute-done.8.near_0_ref), channel_id=1, source_target_pairs={{0,8},{2,26},{8,16},{10,2},{16,24},{18,10},{24,0},{26,18},{1,9},{3... | collective-permute-start | bytes 786440 | tf_op jit(solution)/shard_map/ppermute | solution.py:38
  46.1 4.7 %copy-start.1 = (f32[512]{0:T(512)S(1)}, f32[512]{0:T(512)}, u32[]{:S(2)}) copy-start(f32[512]{0:T(512)} %param.8) | copy-start | bytes 6148
  76.8 1.3 collective-permute-start.12
  78.1 3.6 %collective-permute-start.13 = (f32[8,128]{1,0:T(8,128)S(1)}, f32[8,128]{1,0:T(8,128)S(1)}, u32[]{:S(2)}, u32[]{:S(2)}) collective-permute-start(f32[8,128]{1,0:T(8,128)S(1)} %add.6.refs_0_), channel_id=1, source_target_pairs={{0,1},{2,7},{1,4},{3,2},{4,5},{6,3},{5,0},{7,6},{8,9},{10,15},{9,1... | collective-permute-start | bytes 12296 | tf_op jit(solution)/shard_map/ppermute | solution.py:46
  80.2 5.1 %collective-permute-start.14 = (f32[8,128]{1,0:T(8,128)S(1)}, f32[8,128]{1,0:T(8,128)S(1)}, u32[]{:S(2)}, u32[]{:S(2)}) collective-permute-start(f32[8,128]{1,0:T(8,128)S(1)} %add.6.refs_0_), channel_id=1, source_target_pairs={{0,4},{1,5},{4,0},{5,1},{2,6},{3,7},{6,2},{7,3},{8,12},{9,13},{12,... | collective-permute-start | bytes 12296 | tf_op jit(solution)/shard_map/ppermute | solution.py:31
  81.7 3.6 %collective-permute-start.15 = (f32[8,128]{1,0:T(8,128)S(1)}, f32[8,128]{1,0:T(8,128)S(1)}, u32[]{:S(2)}, u32[]{:S(2)}) collective-permute-start(f32[8,128]{1,0:T(8,128)S(1)} %collective-permute-done.13.refs_1_), channel_id=1, source_target_pairs={{0,2},{2,0},{1,3},{3,1},{4,6},{6,4},{5,7},{7,5},{8,10},{10,8},{9,1... | collective-permute-start | bytes 12296 | tf_op jit(solution)/shard_map/ppermute | solution.py:31
  99.8 1.3 collective-permute-start.16
  101.0 3.6 %collective-permute-start.17 = (f32[8,128]{1,0:T(8,128)S(1)}, f32[8,128]{1,0:T(8,128)S(1)}, u32[]{:S(2)}, u32[]{:S(2)}) collective-permute-start(f32[8,128]{1,0:T(8,128)S(1)} %add.7.refs_0_), channel_id=1, source_target_pairs={{0,1},{2,7},{1,4},{3,2},{4,5},{6,3},{5,0},{7,6},{8,9},{10,15},{9,1... | collective-permute-start | bytes 12296 | tf_op jit(solution)/shard_map/ppermute | solution.py:46
  102.2 5.1 %collective-permute-start.18 = (f32[8,128]{1,0:T(8,128)S(1)}, f32[8,128]{1,0:T(8,128)S(1)}, u32[]{:S(2)}, u32[]{:S(2)}) collective-permute-start(f32[8,128]{1,0:T(8,128)S(1)} %add.7.refs_0_), channel_id=1, source_target_pairs={{0,4},{1,5},{4,0},{5,1},{2,6},{3,7},{6,2},{7,3},{8,12},{9,13},{12,... | collective-permute-start | bytes 12296 | tf_op jit(solution)/shard_map/ppermute | solution.py:31
  104.7 2.7 %collective-permute-start.19 = (f32[8,128]{1,0:T(8,128)S(1)}, f32[8,128]{1,0:T(8,128)S(1)}, u32[]{:S(2)}, u32[]{:S(2)}) collective-permute-start(f32[8,128]{1,0:T(8,128)S(1)} %collective-permute-done.17.refs_1_), channel_id=1, source_target_pairs={{0,2},{2,0},{1,3},{3,1},{4,6},{6,4},{5,7},{7,5},{8,10},{10,8},{9,1... | collective-permute-start | bytes 12296 | tf_op jit(solution)/shard_map/ppermute | solution.py:31
  122.2 3.7 %collective-permute-start.20 = (f32[1024]{0:T(1024)S(1)}, f32[1024]{0:T(1024)S(1)}, u32[]{:S(2)}, u32[]{:S(2)}) collective-permute-start(f32[1024]{0:T(1024)S(1)} %log_bitcast_fusion), channel_id=1, source_target_pairs={{0,1},{1,0},{2,3},{3,2},{4,5},{5,4},{6,7},{7,6},{8,9},{9,8},{10,11... | collective-permute-start | bytes 12296 | tf_op jit(solution)/shard_map/ppermute | solution.py:31

commit v6 on v4

--- a/solution.py
+++ b/solution.py
@@ -173,15 +173,17 @@
                 folded = folded + part[:, k * LANES : (k + 1) * LANES]
         folded_ref[rows, :] = folded
     own = mass_ref[...]
-    sums = jnp.concatenate([lane_sums(folded_ref[...]), own, own], axis=0)
-    sums_ref[...] = jnp.broadcast_to(sums[None], sums_ref.shape)
-
-
-def first_columns_body(kernel_ref, parts_ref, mass_ref, out_ref):
+    sums_ref[...] = jnp.concatenate([lane_sums(folded_ref[...]), own, own], axis=0)
+
+
+def first_columns_body(kernel_ref, side_ref, *refs):
+    part_refs, (mass_ref, out_ref) = refs[:4], refs[4:]
     half = CHUNKS // 2
-    mass = jnp.concatenate([parts_ref[k, CHUNKS : CHUNKS + half, :] for k in range(2)], axis=0)
+    own, other = (part_refs[k][CHUNKS : CHUNKS + half, :] * 0.5 for k in range(2))
+    first = side_ref[...] == 0.0
+    mass = jnp.concatenate([jnp.where(first, own, other), jnp.where(first, other, own)], axis=0)
     mass_ref[...] = mass
-    column_sums(kernel_ref, mass / jnp.sum(parts_ref[:, :CHUNKS, :], axis=0), out_ref)
+    column_sums(kernel_ref, mass / sum(part[:CHUNKS, :] for part in part_refs), out_ref)
 
 
 def columns_body(kernel_ref, mass_ref, *refs):
@@ -297,7 +299,7 @@
     own = src_mass.reshape(-1, LANES)
     kernel, sums = pl.pallas_call(
         build_body,
-        out_shape=(KERNEL, pltpu.VMEM((2 * N_X, 2 * CHUNKS, LANES), F32)),
+        out_shape=(KERNEL, jax.ShapeDtypeStruct((2 * CHUNKS, LANES), F32)),
         in_specs=[VMEM] * 6,
         out_specs=(VMEM, VMEM),
         scratch_shapes=[pltpu.VMEM((ROWS, LANES), F32), pltpu.VMEM((BAND, COLS), jnp.bfloat16)],
@@ -307,12 +309,9 @@
 
     kernel = in_vmem(kernel)
     for sweep in range(ITERS):
+        parts = ring_parts(sums)
         if sweep == 0:
-            parts = [lax.all_to_all(sums, ("xh", "c", "xl"), 0, 0, tiled=True)]
-        else:
-            parts = ring_parts(sums)
-        if sweep == 0:
-            body, operands, extra = first_columns_body, (), (SMALL,)
+            body, operands, extra = first_columns_body, (side,), (SMALL,)
         elif sweep < ITERS - 1:
             body, operands, extra = columns_body, (mass,), ()
         else:

time: 127 us -> 126 us (level)
  blocking collectives: 51.9 us -> 42.8 us
  starting transfers between devices: 25.5 us -> 30.4 us
  waiting for transfers between devices: 38 us -> 40.8 us
    all_to_all x1 -> x0, blocking collectives: 9.23 us -> none  [shards(): parts = [lax.all_to_all(sums, ('xh', 'c', 'xl'), 0, 0, tiled=True)]]
    ppermute x11 -> x14, starting transfers between devices: 3.64 us -> 7.43 us  [shift(): lax.ppermute(value, axis, [(i, (i + by) % size) for i in range(size)])]
    ppermute x11 -> x14, waiting for transfers between devices: 11 us -> 14.6 us  [shift(): lax.ppermute(value, axis, [(i, (i + by) % size) for i in range(size)])]
    ppermute x5 -> x6, starting transfers between devices: 6.69 us -> 7.76 us  [wheel_x(): return lax.ppermute(value, ('xh', 'c', 'xl'), pairs)]
  transfers between devices with their start and end apart: 22 -> 26, of which waited for: 11 -> 13; matrix products, arithmetic and copies ran while one was open for 0% -> 0% of each run, Pallas kernels for 4% -> 4%
where the time goes in v6:
time: 126 us; the launch traced here: 125 us
  blocking collectives  42.8 us (34%)
  waiting for transfers between devices  40.8 us (32%)
  starting transfers between devices  30.4 us (24%)
  Pallas kernels  9.11 us (7%)
    all_to_all x3, blocking collectives, shards(): parts = lax.all_to_all(outs[-1], PLANE, 0, 0, tiled=True)  42.8 us
    ppermute x14, waiting for transfers between devices, shift(): lax.ppermute(value, axis, [(i, (i + by) % size) for i in range(size)])  14.6 us
    ppermute x5, waiting for transfers between devices, wheel_y(): return lax.ppermute(value, ('y', 'c'), pairs)  12.6 us
    all_to_all x1, waiting for transfers between devices, shards(): lax.all_to_all(sent, ('z', 'xl'), 0, 0, tiled=True).reshape(BAND, COLS)  11.9 us
    all_to_all x1, starting transfers between devices, shards(): lax.all_to_all(sent, ('z', 'xl'), 0, 0, tiled=True).reshape(BAND, COLS)  9.94 us
    ppermute x6, starting transfers between devices, wheel_x(): return lax.ppermute(value, ('xh', 'c', 'xl'), pairs)  7.76 us
    ppermute x14, starting transfers between devices, shift(): lax.ppermute(value, axis, [(i, (i + by) % size) for i in range(size)])  7.43 us
    ppermute x5, starting transfers between devices, wheel_y(): return lax.ppermute(value, ('y', 'c'), pairs)  5.25 us
  transfers between devices with their start and end apart: 26, of which 13 were waited for; matrix products, arithmetic and copies ran while one was open for 0% of the time, Pallas kernels for 4%

profile of v6, /device:TPU:6, one launch (start us, length us, event | category | flops | bytes accessed | tf_op | source)
XLA Modules:
  0.0 125.4 jit_solution(1378143136122933914)
XLA Ops:
  1.5 0.8 shard_map.68
  2.3 9.9 %all-to-all-start = ((bf16[16,16,1024]{2,1,0:T(8,128)(2,1)}), bf16[16,16,1024]{2,1,0:T(8,128)(2,1)S(1)}, u32[]{:S(2)}, u32[]{:S(2)}) async-start(bf16[16,16,1024]{2,1,0:T(8,128)(2,1)} %shard_map.68), calls=%async_computation | async-start | bytes 1048576 | tf_op jit(solution)/shard_map/all_to_all | solution.py:253
  12.3 1.4 %collective-permute-start.2 = (bf16[128,1024]{1,0:T(8,128)(2,1)}, bf16[128,1024]{1,0:T(8,128)(2,1)S(1)}, u32[]{:S(2)}, u32[]{:S(2)}) collective-permute-start(bf16[128,1024]{1,0:T(8,128)(2,1)} %bitcast.17), channel_id=1, source_target_pairs={{0,4},{2,6},{1,5},{3,7},{4,0},{6,2},{5,1},{7,3},{8,12},{10,14},{9,... | collective-permute-start | bytes 786440 | tf_op jit(solution)/shard_map/ppermute | solution.py:46
  13.7 1.5 %collective-permute-start = (bf16[128,1024]{1,0:T(8,128)(2,1)}, bf16[128,1024]{1,0:T(8,128)(2,1)S(1)}, u32[]{:S(2)}, u32[]{:S(2)}) collective-permute-start(bf16[128,1024]{1,0:T(8,128)(2,1)} %bitcast.18), channel_id=1, source_target_pairs={{0,1},{2,7},{1,4},{3,2},{4,5},{6,3},{5,0},{7,6},{8,9},{10,15},{9,1... | collective-permute-start | bytes 786440 | tf_op jit(solution)/shard_map/ppermute | solution.py:46
  15.7 11.9 %all-to-all-done = bf16[16,16,1024]{2,1,0:T(8,128)(2,1)S(1)} async-done(((bf16[16,16,1024]{2,1,0:T(8,128)(2,1)}), bf16[16,16,1024]{2,1,0:T(8,128)(2,1)S(1)}, u32[]{:S(2)}, u32[]{:S(2)}) %all-to-all-start) | async-done | bytes 524320 | tf_op jit(solution)/shard_map/all_to_all | solution.py:253
  28.3 1.6 %collective-permute-start.6 = (bf16[128,1024]{1,0:T(8,128)(2,1)S(1)}, bf16[128,1024]{1,0:T(8,128)(2,1)S(1)}, u32[]{:S(2)}, u32[]{:S(2)}) collective-permute-start(bf16[128,1024]{1,0:T(8,128)(2,1)S(1)} %get-tuple-element.16), channel_id=1, source_target_pairs={{0,8},{2,26},{8,16},{10,2},{16,24},{18,10},{24,0},{26,18},{1,9},{3... | collective-permute-start | bytes 786440 | tf_op jit(solution)/shard_map/ppermute | solution.py:38
  29.9 1.7 %collective-permute-start.9 = (bf16[256,1024]{1,0:T(8,128)(2,1)S(1)}, bf16[256,1024]{1,0:T(8,128)(2,1)S(1)}, u32[]{:S(2)}, u32[]{:S(2)}) collective-permute-start(bf16[256,1024]{1,0:T(8,128)(2,1)S(1)} %bitcast.13), channel_id=1, source_target_pairs={{0,24},{2,10},{8,0},{10,18},{16,8},{18,26},{24,16},{26,2},{1,25},{... | collective-permute-start | bytes 1572872 | tf_op jit(solution)/shard_map/ppermute | solution.py:38
  31.7 1.3 %collective-permute-start.8 = (bf16[128,1024]{1,0:T(8,128)(2,1)}, bf16[128,1024]{1,0:T(8,128)(2,1)S(1)}, u32[]{:S(2)}, u32[]{:S(2)}) collective-permute-start(bf16[128,1024]{1,0:T(8,128)(2,1)} %get-tuple-element.20), channel_id=1, source_target_pairs={{0,8},{2,26},{8,16},{10,2},{16,24},{18,10},{24,0},{26,18},{1,9},{3... | collective-permute-start | bytes 786440 | tf_op jit(solution)/shard_map/ppermute | solution.py:38
  33.0 4.6 %collective-permute-done.6.near_0_ref = bf16[128,1024]{1,0:T(8,128)(2,1)S(1)} collective-permute-done((bf16[128,1024]{1,0:T(8,128)(2,1)S(1)}, bf16[128,1024]{1,0:T(8,128)(2,1)S(1)}, u32[]{:S(2)}, u32[]{:S(2)}) %collective-permute-start.6) | collective-permute-done | bytes 262176 | tf_op jit(solution)/shard_map/ppermute | solution.py:38
  38.5 4.7 %collective-permute-done.8.near_1_ref = bf16[128,1024]{1,0:T(8,128)(2,1)S(1)} collective-permute-done((bf16[128,1024]{1,0:T(8,128)(2,1)}, bf16[128,1024]{1,0:T(8,128)(2,1)S(1)}, u32[]{:S(2)}, u32[]{:S(2)}) %collective-permute-start.8) | collective-permute-done | bytes 262176 | tf_op jit(solution)/shard_map/ppermute | solution.py:38
  43.6 2.4 %shard_map.70 = (f32[1024,1024]{1,0:T(8,128)S(1)}, bf16[1024,1024]{1,0:T(8,128)(2,1)S(1)}, f32[2,2,8,128]{3,2,1,0:T(8,128)S(1)}, f32[8,128]{1,0:T(8,128)S(1)}, f32[4,128]{1,0:T(4,128)S(1)}) custom-call(s32[4]{0:T(128)S(1)} %pad_add_fusion.where_ref, s32[2,4]{1,0:T(2,128)} %mask_hbm.1, f32[16,128]{1,0:T(8,128)} %bitcast.22, bf16[128,1024]{1,0:T(8,128)(2,1)} %bitcast.21, ...), custom_call_target="tpu_custom_call" | custom-call | flops 536870912 | bytes 8000000 | tf_op jit(solution)/shard_map/pallas_call | solution.py:269
  46.1 1.3 %shard_map.71.scores_ref = f32[1024,1024]{1,0:T(8,128)S(1)} custom-call(bf16[1024,1024]{1,0:T(8,128)(2,1)S(1)} %get-tuple-element.18.ordered_ref, f32[1024,1024]{1,0:T(8,128)S(1)} %get-tuple-element.19.scores_ref, bf16[128,1024]{1,0:T(8,128)(2,1)S(1)} %collective-permute-done.6.near_0_ref, bf16[128,1024]{1,0:T(8,128)(2,1)S(1)} %collective-permute-done.8.near_1_ref, ...), custom_call_target="tpu_custom_call" | custom-call | flops 1073741824 | bytes 8000000 | tf_op jit(solution)/shard_map/pallas_call | solution.py:290
  47.5 3.3 %collective-permute-done.11.far_1_ref = bf16[128,1024]{1,0:T(8,128)(2,1)S(1)} collective-permute-done((bf16[128,1024]{1,0:T(8,128)(2,1)S(1)}, bf16[128,1024]{1,0:T(8,128)(2,1)S(1)}, u32[]{:S(2)}, u32[]{:S(2)}) %collective-permute-start.11) | collective-permute-done | bytes 262176 | tf_op jit(solution)/shard_map/ppermute | solution.py:38
  50.8 1.3 %shard_map.72 = (f32[1024,1024]{1,0:T(8,128)S(1)}, f32[16,128]{1,0:T(8,128)S(1)}) custom-call(bf16[1024,1024]{1,0:T(8,128)(2,1)S(1)} %get-tuple-element.18.ordered_ref, f32[1024,1024]{1,0:T(8,128)S(1)} %shard_map.71.scores_ref, f32[2,2,8,128]{3,2,1,0:T(8,128)S(1)} %get-tuple-element.21.live_ref, f32[4,128]{1,0:T(4,128)S(1)} %bitcast.16, ...), custom_call_target="tpu_custom_call" | custom-call | flops 536870912 | bytes 8000000 | tf_op jit(solution)/shard_map/pallas_call | solution.py:300
  52.4 1.2 collective-permute-done.12
  53.5 1.9 %collective-permute-start.13 = (f32[16,128]{1,0:T(8,128)S(1)}, f32[16,128]{1,0:T(8,128)S(1)}, u32[]{:S(2)}, u32[]{:S(2)}) collective-permute-start(f32[16,128]{1,0:T(8,128)S(1)} %add.9.refs_0_), channel_id=1, source_target_pairs={{0,1},{2,7},{1,4},{3,2},{4,5},{6,3},{5,0},{7,6},{8,9},{10,15},{9,1... | collective-permute-start | bytes 24584 | tf_op jit(solution)/shard_map/ppermute | solution.py:46
  55.4 2.1 %collective-permute-start.14 = (f32[16,128]{1,0:T(8,128)S(1)}, f32[16,128]{1,0:T(8,128)S(1)}, u32[]{:S(2)}, u32[]{:S(2)}) collective-permute-start(f32[16,128]{1,0:T(8,128)S(1)} %add.9.refs_0_), channel_id=1, source_target_pairs={{0,4},{1,5},{4,0},{5,1},{2,6},{3,7},{6,2},{7,3},{8,12},{9,13},{12,... | collective-permute-start | bytes 24584 | tf_op jit(solution)/shard_map/ppermute | solution.py:31
  57.5 3.0 %collective-permute-done.14.refs_2_ = f32[16,128]{1,0:T(8,128)S(1)} collective-permute-done((f32[16,128]{1,0:T(8,128)S(1)}, f32[16,128]{1,0:T(8,128)S(1)}, u32[]{:S(2)}, u32[]{:S(2)}) %collective-permute-start.14) | collective-permute-done | bytes 8224 | tf_op jit(solution)/shard_map/ppermute | solution.py:31
  60.9 15.1 %all_to_all.20.parts_ref = f32[32,8,128]{2,1,0:T(8,128)S(1)} all-to-all(f32[32,8,128]{2,1,0:T(8,128)S(1)} %get-tuple-element.27), channel_id=1, replica_groups=mesh['z'=8,'y'=4,'xh'=2,'c'=2,'xl'=2] {'z','y'}, dimensions={0} | all-to-all | bytes 262144 | tf_op jit(solution)/shard_map/all_to_all | solution.py:328
  76.6 1.2 collective-permute-done.16
  77.7 1.1 collective-permute-start.17
  78.8 1.6 %collective-permute-start.18 = (f32[8,128]{1,0:T(8,128)S(1)}, f32[8,128]{1,0:T(8,128)S(1)}, u32[]{:S(2)}, u32[]{:S(2)}) collective-permute-start(f32[8,128]{1,0:T(8,128)S(1)} %add.10.refs_0_), channel_id=1, source_target_pairs={{0,4},{1,5},{4,0},{5,1},{2,6},{3,7},{6,2},{7,3},{8,12},{9,13},{12,... | collective-permute-start | bytes 12296 | tf_op jit(solution)/shard_map/ppermute | solution.py:31
  80.4 0.9 collective-permute-done.17.refs_1_
  81.6 2.4 %collective-permute-done.18.refs_2_ = f32[8,128]{1,0:T(8,128)S(1)} collective-permute-done((f32[8,128]{1,0:T(8,128)S(1)}, f32[8,128]{1,0:T(8,128)S(1)}, u32[]{:S(2)}, u32[]{:S(2)}) %collective-permute-start.18) | collective-permute-done | bytes 4128 | tf_op jit(solution)/shard_map/ppermute | solution.py:31
  84.3 13.9 %all_to_all.21.parts_ref = f32[32,8,128]{2,1,0:T(8,128)S(1)} all-to-all(f32[32,8,128]{2,1,0:T(8,128)S(1)} %shard_map.75), channel_id=1, replica_groups=mesh['z'=8,'y'=4,'xh'=2,'c'=2,'xl'=2] {'z','y'}, dimensions={0} | all-to-all | bytes 262144 | tf_op jit(solution)/shard_map/all_to_all | solution.py:328
  98.7 1.2 collective-permute-done.20
  99.9 1.4 %collective-permute-start.21 = (f32[8,128]{1,0:T(8,128)S(1)}, f32[8,128]{1,0:T(8,128)S(1)}, u32[]{:S(2)}, u32[]{:S(2)}) collective-permute-start(f32[8,128]{1,0:T(8,128)S(1)} %add.11.refs_0_), channel_id=1, source_target_pairs={{0,1},{2,7},{1,4},{3,2},{4,5},{6,3},{5,0},{7,6},{8,9},{10,15},{9,1... | collective-permute-start | bytes 12296 | tf_op jit(solution)/shard_map/ppermute | solution.py:46
  101.2 1.5 %collective-permute-start.22 = (f32[8,128]{1,0:T(8,128)S(1)}, f32[8,128]{1,0:T(8,128)S(1)}, u32[]{:S(2)}, u32[]{:S(2)}) collective-permute-start(f32[8,128]{1,0:T(8,128)S(1)} %add.11.refs_0_), channel_id=1, source_target_pairs={{0,4},{1,5},{4,0},{5,1},{2,6},{3,7},{6,2},{7,3},{8,12},{9,13},{12,... | collective-permute-start | bytes 12296 | tf_op jit(solution)/shard_map/ppermute | solution.py:31
  103.7 2.7 %collective-permute-done.22.refs_2_ = f32[8,128]{1,0:T(8,128)S(1)} collective-permute-done((f32[8,128]{1,0:T(8,128)S(1)}, f32[8,128]{1,0:T(8,128)S(1)}, u32[]{:S(2)}, u32[]{:S(2)}) %collective-permute-start.22) | collective-permute-done | bytes 4128 | tf_op jit(solution)/shard_map/ppermute | solution.py:31
  106.4 0.9 shard_map.77
  107.3 13.8 %all_to_all.22 = f32[32,8,128]{2,1,0:T(8,128)S(1)} all-to-all(f32[32,8,128]{2,1,0:T(8,128)S(1)} %get-tuple-element.29), channel_id=1, replica_groups=mesh['z'=8,'y'=4,'xh'=2,'c'=2,'xl'=2] {'z','y'}, dimensions={0} | all-to-all | bytes 262144 | tf_op jit(solution)/shard_map/all_to_all | solution.py:328
  121.8 3.1 %collective-permute-done.24 = f32[1024]{0:T(1024)S(1)} collective-permute-done((f32[1024]{0:T(1024)S(1)}, f32[1024]{0:T(1024)S(1)}, u32[]{:S(2)}, u32[]{:S(2)}) %collective-permute-start.24) | collective-permute-done | bytes 4128 | tf_op jit(solution)/shard_map/ppermute | solution.py:31
  (44 shorter events, 8.1 us)
Async XLA Ops:
  0.6 0.8 copy-start
  2.3 25.3 %all-to-all-start = ((bf16[16,16,1024]{2,1,0:T(8,128)(2,1)}), bf16[16,16,1024]{2,1,0:T(8,128)(2,1)S(1)}, u32[]{:S(2)}, u32[]{:S(2)}) async-start(bf16[16,16,1024]{2,1,0:T(8,128)(2,1)} %shard_map.68), calls=%async_computation | async-start | bytes 1048576 | tf_op jit(solution)/shard_map/all_to_all | solution.py:253
  12.3 17.7 %collective-permute-start.2 = (bf16[128,1024]{1,0:T(8,128)(2,1)}, bf16[128,1024]{1,0:T(8,128)(2,1)S(1)}, u32[]{:S(2)}, u32[]{:S(2)}) collective-permute-start(bf16[128,1024]{1,0:T(8,128)(2,1)} %bitcast.17), channel_id=1, source_target_pairs={{0,4},{2,6},{1,5},{3,7},{4,0},{6,2},{5,1},{7,3},{8,12},{10,14},{9,... | collective-permute-start | bytes 786440 | tf_op jit(solution)/shard_map/ppermute | solution.py:46
  13.7 17.9 %collective-permute-start = (bf16[128,1024]{1,0:T(8,128)(2,1)}, bf16[128,1024]{1,0:T(8,128)(2,1)S(1)}, u32[]{:S(2)}, u32[]{:S(2)}) collective-permute-start(bf16[128,1024]{1,0:T(8,128)(2,1)} %bitcast.18), channel_id=1, source_target_pairs={{0,1},{2,7},{1,4},{3,2},{4,5},{6,3},{5,0},{7,6},{8,9},{10,15},{9,1... | collective-permute-start | bytes 786440 | tf_op jit(solution)/shard_map/ppermute | solution.py:46
  15.1 16.6 %collective-permute-start.1 = (bf16[128,1024]{1,0:T(8,128)(2,1)}, bf16[128,1024]{1,0:T(8,128)(2,1)S(1)}, u32[]{:S(2)}, u32[]{:S(2)}) collective-permute-start(bf16[128,1024]{1,0:T(8,128)(2,1)} %bitcast.19), channel_id=1, source_target_pairs={{0,5},{2,3},{1,0},{3,6},{4,1},{6,7},{5,4},{7,2},{8,13},{10,11},{9,... | collective-permute-start | bytes 786440 | tf_op jit(solution)/shard_map/ppermute | solution.py:46
  28.3 9.3 %collective-permute-start.6 = (bf16[128,1024]{1,0:T(8,128)(2,1)S(1)}, bf16[128,1024]{1,0:T(8,128)(2,1)S(1)}, u32[]{:S(2)}, u32[]{:S(2)}) collective-permute-start(bf16[128,1024]{1,0:T(8,128)(2,1)S(1)} %get-tuple-element.16), channel_id=1, source_target_pairs={{0,8},{2,26},{8,16},{10,2},{16,24},{18,10},{24,0},{26,18},{1,9},{3... | collective-permute-start | bytes 786440 | tf_op jit(solution)/shard_map/ppermute | solution.py:38
  29.9 7.7 %collective-permute-start.3 = (bf16[128,1024]{1,0:T(8,128)(2,1)}, bf16[128,1024]{1,0:T(8,128)(2,1)S(1)}, u32[]{:S(2)}, u32[]{:S(2)}) collective-permute-start(bf16[128,1024]{1,0:T(8,128)(2,1)} %bitcast.20), channel_id=1, source_target_pairs={{0,2},{2,0},{1,3},{3,1},{4,6},{6,4},{5,7},{7,5},{8,10},{10,8},{9,1... | collective-permute-start | bytes 786440 | tf_op jit(solution)/shard_map/ppermute | solution.py:31
  29.9 16.2 %collective-permute-start.9 = (bf16[256,1024]{1,0:T(8,128)(2,1)S(1)}, bf16[256,1024]{1,0:T(8,128)(2,1)S(1)}, u32[]{:S(2)}, u32[]{:S(2)}) collective-permute-start(bf16[256,1024]{1,0:T(8,128)(2,1)S(1)} %bitcast.13), channel_id=1, source_target_pairs={{0,24},{2,10},{8,0},{10,18},{16,8},{18,26},{24,16},{26,2},{1,25},{... | collective-permute-start | bytes 1572872 | tf_op jit(solution)/shard_map/ppermute | solution.py:38
  31.6 6.5 %collective-permute-start.4 = (bf16[128,1024]{1,0:T(8,128)(2,1)S(1)}, bf16[128,1024]{1,0:T(8,128)(2,1)S(1)}, u32[]{:S(2)}, u32[]{:S(2)}) collective-permute-start(bf16[128,1024]{1,0:T(8,128)(2,1)S(1)} %collective-permute-done.refs_0_), channel_id=1, source_target_pairs={{0,2},{2,0},{1,3},{3,1},{4,6},{6,4},{5,7},{7,5},{8,10},{10,8},{9,1... | collective-permute-start | bytes 786440 | tf_op jit(solution)/shard_map/ppermute | solution.py:31
  31.7 11.5 %collective-permute-start.8 = (bf16[128,1024]{1,0:T(8,128)(2,1)}, bf16[128,1024]{1,0:T(8,128)(2,1)S(1)}, u32[]{:S(2)}, u32[]{:S(2)}) collective-permute-start(bf16[128,1024]{1,0:T(8,128)(2,1)} %get-tuple-element.20), channel_id=1, source_target_pairs={{0,8},{2,26},{8,16},{10,2},{16,24},{18,10},{24,0},{26,18},{1,9},{3... | collective-permute-start | bytes 786440 | tf_op jit(solution)/shard_map/ppermute | solution.py:38
  37.6 6.1 %collective-permute-start.5 = (bf16[128,1024]{1,0:T(8,128)(2,1)S(1)}, bf16[128,1024]{1,0:T(8,128)(2,1)S(1)}, u32[]{:S(2)}, u32[]{:S(2)}) collective-permute-start(bf16[128,1024]{1,0:T(8,128)(2,1)S(1)} %collective-permute-done.1.refs_1_), channel_id=1, source_target_pairs={{0,2},{2,0},{1,3},{3,1},{4,6},{6,4},{5,7},{7,5},{8,10},{10,8},{9,1... | collective-permute-start | bytes 786440 | tf_op jit(solution)/shard_map/ppermute | solution.py:31
  37.6 6.1 %collective-permute-start.7 = (bf16[128,1024]{1,0:T(8,128)(2,1)S(1)}, bf16[128,1024]{1,0:T(8,128)(2,1)S(1)}, u32[]{:S(2)}, u32[]{:S(2)}) collective-permute-start(bf16[128,1024]{1,0:T(8,128)(2,1)S(1)} %collective-permute-done.2.refs_2_), channel_id=1, source_target_pairs={{0,2},{2,0},{1,3},{3,1},{4,6},{6,4},{5,7},{7,5},{8,10},{10,8},{9,1... | collective-permute-start | bytes 786440 | tf_op jit(solution)/shard_map/ppermute | solution.py:31
  38.1 9.4 %collective-permute-start.10 = (bf16[128,1024]{1,0:T(8,128)(2,1)S(1)}, bf16[128,1024]{1,0:T(8,128)(2,1)S(1)}, u32[]{:S(2)}, u32[]{:S(2)}) collective-permute-start(bf16[128,1024]{1,0:T(8,128)(2,1)S(1)} %collective-permute-done.6.near_0_ref), channel_id=1, source_target_pairs={{0,8},{2,26},{8,16},{10,2},{16,24},{18,10},{24,0},{26,18},{1,9},{3... | collective-permute-start | bytes 786440 | tf_op jit(solution)/shard_map/ppermute | solution.py:38
  43.2 7.6 %collective-permute-start.11 = (bf16[128,1024]{1,0:T(8,128)(2,1)S(1)}, bf16[128,1024]{1,0:T(8,128)(2,1)S(1)}, u32[]{:S(2)}, u32[]{:S(2)}) collective-permute-start(bf16[128,1024]{1,0:T(8,128)(2,1)S(1)} %collective-permute-done.8.near_1_ref), channel_id=1, source_target_pairs={{0,8},{2,26},{8,16},{10,2},{16,24},{18,10},{24,0},{26,18},{1,9},{3... | collective-permute-start | bytes 786440 | tf_op jit(solution)/shard_map/ppermute | solution.py:38
  46.1 4.7 %copy-start.1 = (f32[512]{0:T(512)S(1)}, f32[512]{0:T(512)}, u32[]{:S(2)}) copy-start(f32[512]{0:T(512)} %param.8) | copy-start | bytes 6148
  52.1 1.4 %collective-permute-start.12 = (f32[16,128]{1,0:T(8,128)S(1)}, f32[16,128]{1,0:T(8,128)S(1)}, u32[]{:S(2)}, u32[]{:S(2)}) collective-permute-start(f32[16,128]{1,0:T(8,128)S(1)} %get-tuple-element.24), channel_id=1, source_target_pairs={{0,2},{2,0},{1,3},{3,1},{4,6},{6,4},{5,7},{7,5},{8,10},{10,8},{9,1... | collective-permute-start | bytes 24584 | tf_op jit(solution)/shard_map/ppermute | solution.py:31
  53.5 4.0 %collective-permute-start.13 = (f32[16,128]{1,0:T(8,128)S(1)}, f32[16,128]{1,0:T(8,128)S(1)}, u32[]{:S(2)}, u32[]{:S(2)}) collective-permute-start(f32[16,128]{1,0:T(8,128)S(1)} %add.9.refs_0_), channel_id=1, source_target_pairs={{0,1},{2,7},{1,4},{3,2},{4,5},{6,3},{5,0},{7,6},{8,9},{10,15},{9,1... | collective-permute-start | bytes 24584 | tf_op jit(solution)/shard_map/ppermute | solution.py:46
  55.4 5.2 %collective-permute-start.14 = (f32[16,128]{1,0:T(8,128)S(1)}, f32[16,128]{1,0:T(8,128)S(1)}, u32[]{:S(2)}, u32[]{:S(2)}) collective-permute-start(f32[16,128]{1,0:T(8,128)S(1)} %add.9.refs_0_), channel_id=1, source_target_pairs={{0,4},{1,5},{4,0},{5,1},{2,6},{3,7},{6,2},{7,3},{8,12},{9,13},{12,... | collective-permute-start | bytes 24584 | tf_op jit(solution)/shard_map/ppermute | solution.py:31
  57.5 3.0 %collective-permute-start.15 = (f32[16,128]{1,0:T(8,128)S(1)}, f32[16,128]{1,0:T(8,128)S(1)}, u32[]{:S(2)}, u32[]{:S(2)}) collective-permute-start(f32[16,128]{1,0:T(8,128)S(1)} %collective-permute-done.13.refs_1_), channel_id=1, source_target_pairs={{0,2},{2,0},{1,3},{3,1},{4,6},{6,4},{5,7},{7,5},{8,10},{10,8},{9,1... | collective-permute-start | bytes 24584 | tf_op jit(solution)/shard_map/ppermute | solution.py:31
  76.5 1.3 collective-permute-start.16
  77.7 3.6 %collective-permute-start.17 = (f32[8,128]{1,0:T(8,128)S(1)}, f32[8,128]{1,0:T(8,128)S(1)}, u32[]{:S(2)}, u32[]{:S(2)}) collective-permute-start(f32[8,128]{1,0:T(8,128)S(1)} %add.10.refs_0_), channel_id=1, source_target_pairs={{0,1},{2,7},{1,4},{3,2},{4,5},{6,3},{5,0},{7,6},{8,9},{10,15},{9,1... | collective-permute-start | bytes 12296 | tf_op jit(solution)/shard_map/ppermute | solution.py:46
  78.8 5.1 %collective-permute-start.18 = (f32[8,128]{1,0:T(8,128)S(1)}, f32[8,128]{1,0:T(8,128)S(1)}, u32[]{:S(2)}, u32[]{:S(2)}) collective-permute-start(f32[8,128]{1,0:T(8,128)S(1)} %add.10.refs_0_), channel_id=1, source_target_pairs={{0,4},{1,5},{4,0},{5,1},{2,6},{3,7},{6,2},{7,3},{8,12},{9,13},{12,... | collective-permute-start | bytes 12296 | tf_op jit(solution)/shard_map/ppermute | solution.py:31
  81.3 2.6 %collective-permute-start.19 = (f32[8,128]{1,0:T(8,128)S(1)}, f32[8,128]{1,0:T(8,128)S(1)}, u32[]{:S(2)}, u32[]{:S(2)}) collective-permute-start(f32[8,128]{1,0:T(8,128)S(1)} %collective-permute-done.17.refs_1_), channel_id=1, source_target_pairs={{0,2},{2,0},{1,3},{3,1},{4,6},{6,4},{5,7},{7,5},{8,10},{10,8},{9,1... | collective-permute-start | bytes 12296 | tf_op jit(solution)/shard_map/ppermute | solution.py:31
  98.6 1.3 collective-permute-start.20
  99.9 3.6 %collective-permute-start.21 = (f32[8,128]{1,0:T(8,128)S(1)}, f32[8,128]{1,0:T(8,128)S(1)}, u32[]{:S(2)}, u32[]{:S(2)}) collective-permute-start(f32[8,128]{1,0:T(8,128)S(1)} %add.11.refs_0_), channel_id=1, source_target_pairs={{0,1},{2,7},{1,4},{3,2},{4,5},{6,3},{5,0},{7,6},{8,9},{10,15},{9,1... | collective-permute-start | bytes 12296 | tf_op jit(solution)/shard_map/ppermute | solution.py:46
  101.2 5.1 %collective-permute-start.22 = (f32[8,128]{1,0:T(8,128)S(1)}, f32[8,128]{1,0:T(8,128)S(1)}, u32[]{:S(2)}, u32[]{:S(2)}) collective-permute-start(f32[8,128]{1,0:T(8,128)S(1)} %add.11.refs_0_), channel_id=1, source_target_pairs={{0,4},{1,5},{4,0},{5,1},{2,6},{3,7},{6,2},{7,3},{8,12},{9,13},{12,... | collective-permute-start | bytes 12296 | tf_op jit(solution)/shard_map/ppermute | solution.py:31
  103.5 2.9 %collective-permute-start.23 = (f32[8,128]{1,0:T(8,128)S(1)}, f32[8,128]{1,0:T(8,128)S(1)}, u32[]{:S(2)}, u32[]{:S(2)}) collective-permute-start(f32[8,128]{1,0:T(8,128)S(1)} %collective-permute-done.21.refs_1_), channel_id=1, source_target_pairs={{0,2},{2,0},{1,3},{3,1},{4,6},{6,4},{5,7},{7,5},{8,10},{10,8},{9,1... | collective-permute-start | bytes 12296 | tf_op jit(solution)/shard_map/ppermute | solution.py:31
  121.1 3.7 %collective-permute-start.24 = (f32[1024]{0:T(1024)S(1)}, f32[1024]{0:T(1024)S(1)}, u32[]{:S(2)}, u32[]{:S(2)}) collective-permute-start(f32[1024]{0:T(1024)S(1)} %log_bitcast_fusion), channel_id=1, source_target_pairs={{0,1},{1,0},{2,3},{3,2},{4,5},{5,4},{6,7},{7,6},{8,9},{9,8},{10,11... | collective-permute-start | bytes 12296 | tf_op jit(solution)/shard_map/ppermute | solution.py:31
